TPU v7x, 32 devices: a whole 2x2x4 slice. The times are simulated.
32 devices in a mesh: row: 4 (over y, x), col: 8 (over z, core).
Axes of the slice: x: 2, y: 2, z: 4, core: 2. Of those that a mesh axis runs over, the one named last changes fastest.
Arguments:
- front_trailing: float32 [16384, 16384], P('row', 'col'), may hold values from -6 to 6
- panel_columns: float32 [16384, 1024], P('row', 'col'), may hold values from -0.1875 to 0.1875
- panel_rows: float32 [1024, 16384], P('row', 'col'), may hold values from -6 to 6
- pivots: int32 [1024], replicated, may hold values from 0 to 1023, each once
- diag_inverse: float32 [1024, 1024], replicated, may hold values from -0.1875 to 0.1875
- test_matrix: float32 [16384, 512], P('col'), may hold values from -0.046875 to 0.046875
Outputs:
- schur: float32 [16384, 16384], P('row', 'col')
- off_samples: float32 [16384, 512], P(('row', 'col'))
- leaf_blocks: float32 [16384, 128], P(('row', 'col'))
- group_gram: float32 [4, 512, 512], P('row')
Inputs may be any that keep to these rules, and one draw needn't show every extreme that they name: pivots names each of 0 to 1023 once.
All inputs are finite; a program needn't handle non-finite values.
Results may differ from a plain program's by a relative error of at most 0.000084.
Values sent between devices are 32-bit elements; how exact they have to be, the bound alone decides.
No kernel may reach another device: no remote copies, remote signals or barrier semaphores. Data moves between devices by JAX's collectives and lax.ppermute only.
A program may use at most 192 MiB of HBM per device.

v0:
```python
import jax
import jax.numpy as jnp
from jax import lax
from jax.sharding import PartitionSpec as P

LEAF = 128


def swapped(block, axis, apart):
    count = lax.axis_size(axis)
    route = []
    for low in range(count):
        high = low | 1 << apart
        if high != low and high < count:
            route += [(low, high), (high, low)]
    return lax.ppermute(block, axis, route)


def from_root(block, axis, source):
    block = jnp.where(lax.axis_index(axis) == source, block, jnp.zeros_like(block))
    return lax.psum(block, axis)


def product(left, right):
    return jnp.dot(left, right, precision=lax.Precision.HIGHEST, preferred_element_type=jnp.float32)


def inner_gram(samples_local):
    return lax.dot_general(
        samples_local,
        samples_local,
        (((0,), (0,)), ((), ())),
        precision=lax.Precision.HIGHEST,
        preferred_element_type=jnp.float32,
    )


def body(front_trailing, panel_columns, panel_rows, pivots, diag_inverse, test_matrix):
    row_count = lax.axis_size("row")
    col_count = lax.axis_size("col")
    row_index = lax.axis_index("row")
    col_index = lax.axis_index("col")
    height, width = front_trailing.shape
    upper_full = lax.all_gather(panel_rows, "row", axis=0, tiled=True)
    upper = jnp.take(upper_full, pivots, axis=0)
    lower = product(lax.all_gather(panel_columns, "col", axis=1, tiled=True), diag_inverse)
    update = product(lower, upper)
    schur = front_trailing - update
    global_rows = row_index * height + jnp.arange(height, dtype=jnp.int32)
    global_cols = col_index * width + jnp.arange(width, dtype=jnp.int32)
    same_leaf = global_rows[:, None] // LEAF == global_cols[None, :] // LEAF
    masked = jnp.where(same_leaf, jnp.zeros_like(schur), schur)
    per_device = height // col_count
    own_samples = lax.psum_scatter(
        product(masked, test_matrix), "col", scatter_dimension=0, tiled=True
    )
    gram = lax.psum(inner_gram(own_samples), "col")
    partner = swapped(gram, "row", 0)
    group_gram = ((gram + partner) / (2 * height))[None]
    ratio = col_count // row_count
    blocks_count = width // LEAF
    region_start = col_index % ratio * width
    region = lax.dynamic_slice_in_dim(schur, region_start, width, 0)
    candidates = jnp.diagonal(
        region.reshape(blocks_count, LEAF, blocks_count, LEAF), axis1=0, axis2=2
    )
    candidates = jnp.moveaxis(candidates, -1, 0)
    received = [from_root(candidates, "col", row_index * ratio + source) for source in range(ratio)]
    stacked = jnp.stack(received).reshape(ratio * blocks_count, LEAF, LEAF)
    first_row = col_index * per_device
    picked = lax.dynamic_slice_in_dim(stacked, first_row // LEAF, per_device // LEAF, 0)
    leaf_blocks = picked.reshape(per_device, LEAF)
    return (schur, own_samples, leaf_blocks, group_gram)


def solution(mesh):
    placed = (P("row", "col"), P("row", "col"), P("row", "col"), P(), P(), P("col", None))
    return jax.shard_map(
        body,
        mesh=mesh,
        in_specs=placed,
        out_specs=(
            P("row", "col"),
            P(("row", "col"), None),
            P(("row", "col"), None),
            P("row", None, None),
        ),
        check_vma=False,
    )
```

profile of v0, /device:TPU:0, one launch (start us, length us, event | category | flops | bytes accessed | tf_op | source)
XLA Modules:
  0.0 698.5 jit_solution(15575006938902999287)
XLA Ops:
  7.2 0.7 all-gather.5.cloned.1.call-update
  7.9 0.7 all-gather.3.cloned.1.call-update
  8.7 0.7 compare_and_fusion
  9.4 0.7 fusion.15
  10.1 90.1 %all-gather.5.cloned.1.call-done = f32[1024,2048]{1,0:T(8,128)} async-done(((f32[256,2048]{1,0:T(8,128)}), f32[1024,2048]{1,0:T(8,128)}) %all-gather.5.cloned.1.call-update) | async-done | bytes 8388624 | tf_op jit(solution)/shard_map/all_gather | solution.py:44
  100.2 12.2 %gather_fusion = f32[1024,2048]{1,0:T(8,128)} fusion(f32[1024,2048]{1,0:T(8,128)} %all-gather.5.cloned.1.call-done, s32[1024]{0:T(1024)S(1)} %fusion.15), kind=kCustom, calls=%fused_computation | custom fusion | bytes 16781312 | tf_op jit(solution)/shard_map/jit(_take)/gather | solution.py:45
  112.4 141.2 %all-gather.3.cloned.1.call-done = f32[4096,1024]{1,0:T(8,128)} async-done(((f32[4096,128]{1,0:T(8,128)}), f32[4096,1024]{1,0:T(8,128)}) %all-gather.3.cloned.1.call-update) | async-done | bytes 16777232 | tf_op jit(solution)/shard_map/all_gather | solution.py:46
  253.6 60.0 %fusion.18 = f32[4096,1024]{1,0:T(8,128)} fusion(f32[4096,1024]{1,0:T(8,128)} %all-gather.3.cloned.1.call-done, f32[1024,1024]{1,0:T(8,128)} %param.10), kind=kOutput, calls=%fused_computation.43 | convolution fusion | flops 51539607552 | bytes 37748736 | tf_op jit(solution)/shard_map/dot_general | solution.py:25
  313.6 118.8 %convolution_subtract_fusion = f32[4096,2048]{1,0:T(8,128)} fusion(f32[4096,2048]{1,0:T(8,128)} %param.6, f32[4096,1024]{1,0:T(8,128)} %fusion.18, f32[1024,2048]{1,0:T(8,128)S(1)} %copy-done, pred[1024]{0:T(1024)(128)(4,1)S(1)} %compare_and_fusion), kind=kOutput, calls=%fused_computation.5 | convolution fusion | flops 103089700864 | bytes 92275712 | tf_op jit(solution)/shard_map/dot_general | solution.py:25
  432.4 64.0 %fusion = f32[4096,512]{1,0:T(8,128)} fusion(f32[2048,512]{1,0:T(8,128)} %param.11, f32[4096,2048]{1,0:T(8,128)} %convolution_subtract_fusion, s32[2048]{0:T(1024)S(1)} %add_select_fusion.1, s32[4096]{0:T(1024)S(1)} %add_select_fusion), kind=kOutput, calls=%fused_computation.2 | convolution fusion | flops 51556384768 | bytes 46161920 | tf_op jit(solution)/shard_map/dot_general | solution.py:25
  496.5 0.0 all-reduce.3.cloned.1.call-start
  496.6 7.1 %dynamic-slice_bitcast_fusion = f32[256,8,16,128]{3,1,2,0:T(8,128)S(1)} fusion(f32[4096,2048]{1,0:T(8,128)} %convolution_subtract_fusion, s32[]{:T(128)S(6)} %select_n.81), kind=kLoop, calls=%fused_computation.7 | loop fusion | bytes 33554436
  503.7 3.6 copy.12
  507.3 7.9 %copy.14 = f32[16,128,16,128]{3,1,2,0:T(8,128)} copy(f32[16,128,16,128]{3,2,1,0:T(8,128)S(1)} %bitcast.25) | data formatting | bytes 33554432 | tf_op jit(solution)/shard_map/reshape | solution.py:65
  515.2 6.6 gather_fusion.1
  521.7 1.6 select_bitcast_fusion.1
  523.3 61.1 %reduce-scatter.2.cloned.1.call-done = f32[512,512]{1,0:T(8,128)} async-done(((f32[4096,512]{1,0:T(8,128)}), f32[512,512]{1,0:T(8,128)}) %reduce-scatter.2.cloned.1.call-update) | async-done | bytes 1048592 | tf_op jit(solution)/shard_map/reduce_scatter | solution.py:54
  584.4 4.4 fusion.19
  588.8 76.0 %all-reduce.3.cloned.1.call-done = (f32[1,16,128,128]{3,2,1,0:T(8,128)}, f32[1,16,128,128]{3,2,1,0:T(8,128)}, f32[512,512]{1,0:T(8,128)}) async-done(((f32[1,16,128,128]{3,2,1,0:T(8,128)}, f32[1,16,128,128]{3,2,1,0:T(8,128)}, f32[512,512]{1,0:T(8,128)}), (f32[1,16,128,128]{3,2,1,0:T(8,128)}, f32[1,16,128,128]{3,2,1,0:T(8,128)}, f32[512,512]{1,0:T(8,128)})) %all-reduce.3.cloned.1.call-update) | async-done | bytes 3145744 | tf_op jit(solution)/shard_map/psum | solution.py:21
  664.8 1.5 collective-permute-start
  666.3 1.7 pad_maximum_fusion
  668.0 0.7 constant_dynamic-slice_fusion
  668.7 20.8 %collective-permute-done = f32[512,512]{1,0:T(8,128)S(1)} collective-permute-done((f32[512,512]{1,0:T(8,128)}, f32[512,512]{1,0:T(8,128)S(1)}, u32[]{:S(2)}, u32[]{:S(2)}) %collective-permute-start) | collective-permute-done | bytes 1048608 | tf_op jit(solution)/shard_map/ppermute | solution.py:16
  689.5 2.4 multiply_bitcast_fusion
  (10 shorter events, 0.2 us)
Async XLA Ops:
  7.2 93.0 %all-gather.5.cloned.1.call-start = ((), (), s32[]{:S(2)}) async-start(), calls=%async_computation.2 | async-start | bytes 10485760 | tf_op jit(solution)/shard_map/all_gather | solution.py:44
  7.9 245.7 %all-gather.3.cloned.1.call-start = ((), (), s32[]{:S(2)}) async-start(), calls=%async_computation.1 | async-start | bytes 18874368 | tf_op jit(solution)/shard_map/all_gather | solution.py:46
  8.6 575.8 %reduce-scatter.2.cloned.1.call-start = ((), (), s32[]{:S(2)}) async-start(), calls=%async_computation.3 | async-start | bytes 9437184 | tf_op jit(solution)/shard_map/reduce_scatter | solution.py:54
  253.6 60.0 %copy-start = (f32[1024,2048]{1,0:T(8,128)S(1)}, f32[1024,2048]{1,0:T(8,128)}, u32[]{:S(2)}) copy-start(f32[1024,2048]{1,0:T(8,128)} %gather_fusion) | copy-start | bytes 25165828
  496.5 168.3 %all-reduce.3.cloned.1.call-start = ((), (), s32[]{:S(2)}) async-start(), calls=%async_computation.4 | async-start | bytes 6291456 | tf_op jit(solution)/shard_map/psum | solution.py:21
  664.8 24.7 %collective-permute-start = (f32[512,512]{1,0:T(8,128)}, f32[512,512]{1,0:T(8,128)S(1)}, u32[]{:S(2)}, u32[]{:S(2)}) collective-permute-start(f32[512,512]{1,0:T(8,128)} %get-tuple-element.6), channel_id=1, source_target_pairs={{0,8},{8,0},{16,24},{24,16},{1,9},{9,1},{17,25},{25,17},{2,10},{10... | collective-permute-start | bytes 3145736 | tf_op jit(solution)/shard_map/ppermute | solution.py:16
Sparse Core Ops, SparseCore 0:
  9.8 90.2 all-gather.4
  101.8 151.8 all-gather.2
  496.6 87.8 reduce-scatter.1
  588.9 75.8 all-reduce.2
where the time goes:
time: 699 us; the launch traced here: 698 us
  waiting for transfers between devices  391 us (56%)
  matrix products  247 us (35%)
  local copies, waits for them, and re-layouts  38.1 us (5%)
  between operations  13.9 us (2%)
  other arithmetic  7.08 us (1%)
    dot_general x3, matrix products, product(): jnp.dot(left, right, precision=lax.Precision.HIGHEST, preferred_element_t...  243 us
    all_gather x1, waiting for transfers between devices, body(): lax.all_gather(panel_columns, 'col', axis=1, tiled=True)  141 us
    all_gather x1, waiting for transfers between devices, body(): upper_full = lax.all_gather(panel_rows, 'row', axis=0, tiled=True)  90.1 us
    psum x1, waiting for transfers between devices, from_root(): return lax.psum(block, axis)  76 us
    reduce_scatter x1, waiting for transfers between devices, body(): lax.psum_scatter(product(masked, test_matrix), 'col', scatter_dimension=0...  61.1 us
    ppermute x1, waiting for transfers between devices, swapped(): return lax.ppermute(block, axis, route)  20.8 us
  transfers between devices with their start and end apart: 5, of which 5 were waited for; matrix products, arithmetic and copies ran while one was open for 6% of the time, Pallas kernels for 0%

commit v1 on v0

v1 whole, which is shorter than its diff:
```python
import functools

import jax
import jax.numpy as jnp
from jax import lax
from jax.experimental import pallas as pl
from jax.experimental.pallas import tpu as pltpu
from jax.sharding import Mesh, PartitionSpec as P

LEAF = 128
CHUNKS = 4
VMEM = 56 * 1024 * 1024
F32 = jnp.float32
BF16 = jnp.bfloat16
ALL = ("hi", "lo", "z", "core")


def split(value):
    high = value.astype(BF16)
    return high, (value - high.astype(F32)).astype(BF16)


def split_outside(value):
    high = lax.reduce_precision(value, exponent_bits=8, mantissa_bits=7)
    return high.astype(BF16), (value - high).astype(BF16)


def triple(left_high, left_low, right_high, right_low):
    dot = functools.partial(jnp.dot, preferred_element_type=F32)
    return dot(left_high, right_high) + (dot(left_high, right_low) + dot(left_low, right_high))


def high_dot(left, right, dims=(((1,), (0,)), ((), ()))):
    return lax.dot_general(left, right, dims, precision=lax.Precision.HIGH, preferred_element_type=F32)


def swap(value, axis):
    return lax.ppermute(value, axis, [(0, 1), (1, 0)])


def shift(value, axis, step):
    count = lax.axis_size(axis)
    return lax.ppermute(value, axis, [(at, (at + step) % count) for at in range(count)])


def hop(value, step, count=None):
    chips = lax.axis_size("z")
    count = chips - 1 if count is None else count
    if step > 0:
        route = [(at, at + 1) for at in range(count)]
    else:
        route = [(at, at - 1) for at in range(chips - count, chips)]
    return lax.ppermute(value, "z", route)


def samples_kernel(place, front, test, out, test_high, test_low):
    step = pl.program_id(0)

    @pl.when(step == 0)
    def _():
        high, low = split(test[...])
        test_high[...] = high
        test_low[...] = low

    rows, width = front.shape
    first_row = place[1] + (2 * step + place[0]) * (rows // LEAF)
    row_leaf = first_row + lax.broadcasted_iota(jnp.int32, (rows, 1), 0) // LEAF
    col_leaf = place[2] + lax.broadcasted_iota(jnp.int32, (1, width), 1) // LEAF
    value = jnp.where(row_leaf == col_leaf, 0.0, front[...])
    high, low = split(value)
    out[...] = triple(high, low, test_high[...], test_low[...])


def samples_half(front, test, place, rows):
    height, width = front.shape
    samples = test.shape[1]
    tiles = height // (2 * rows)
    flops = 6 * tiles * rows * width * samples
    return pl.pallas_call(
        samples_kernel,
        out_shape=jax.ShapeDtypeStruct((tiles * rows, samples), F32),
        grid_spec=pltpu.PrefetchScalarGridSpec(
            num_scalar_prefetch=1,
            grid=(tiles,),
            in_specs=[
                pl.BlockSpec((rows, width), lambda s, place: (2 * s + place[0], 0)),
                pl.BlockSpec((width, samples), lambda s, place: (0, 0), pipeline_mode=pl.Buffered(1)),
            ],
            out_specs=pl.BlockSpec((rows, samples), lambda s, place: (s, 0)),
            scratch_shapes=[pltpu.VMEM((width, samples), BF16)] * 2,
        ),
        compiler_params=pltpu.CompilerParams(vmem_limit_bytes=VMEM),
        cost_estimate=pl.CostEstimate(flops=flops, bytes_accessed=height * width * 2, transcendentals=0),
        name="samples",
    )(place, front, test)


def weights_kernel(parts, *refs):
    left_high, left_low = refs[0], refs[1]
    rows = jnp.concatenate([ref[...] for ref in refs[2 : 2 + parts]], axis=0)
    high, low = split(rows)
    out_high, out_low = refs[2 + parts :]
    high, low = split(triple(left_high[...], left_low[...], high, low))
    out_high[...] = high
    out_low[...] = low


def weights(left_high, left_low, blocks):
    panel = left_high.shape[0]
    width = blocks[0].shape[1]
    tile = min(width, 512)
    whole = pl.BlockSpec((panel, panel), lambda n: (0, 0), pipeline_mode=pl.Buffered(1))
    return pl.pallas_call(
        functools.partial(weights_kernel, len(blocks)),
        out_shape=[jax.ShapeDtypeStruct((panel, width), BF16)] * 2,
        grid=(width // tile,),
        in_specs=[whole, whole] + [pl.BlockSpec((b.shape[0], tile), lambda n: (0, n)) for b in blocks],
        out_specs=[pl.BlockSpec((panel, tile), lambda n: (0, n))] * 2,
        compiler_params=pltpu.CompilerParams(vmem_limit_bytes=VMEM),
        cost_estimate=pl.CostEstimate(flops=6 * panel * panel * width, bytes_accessed=panel * width * 8, transcendentals=0),
        name="weights",
    )(left_high, left_low, *blocks)


def update_kernel(first, place, own, beside, mine, other, high, low, front, *refs):
    out, leaves = refs[-2:]
    columns = jnp.concatenate([own[...], beside[...], mine[...], other[...]], axis=1)
    left_high, left_low = split(columns)
    out[...] = front[...] - triple(left_high, left_low, high[...], low[...])
    rows, width = out.shape
    leaf = place[1] - place[2] + first + pl.program_id(0) * (rows // LEAF)
    for at in range(rows // LEAF):
        column = jnp.clip(leaf + at, 0, width // LEAF - 1) * LEAF
        piece = pl.ds(at * LEAF, LEAF)
        leaves[piece, :] = out[piece, pl.ds(pl.multiple_of(column, LEAF), LEAF)]


def update(place, own, beside, mine, other, high, low, front, schur, start):
    height, width = front.shape
    panel = high.shape[0]
    rows = mine.shape[0]
    tile = 256 if rows % 256 == 0 else LEAF
    base = start // tile
    slot = own.shape[1]
    far = mine.shape[1]
    whole = pl.BlockSpec((panel, width), lambda i, place: (0, 0), pipeline_mode=pl.Buffered(1))
    operands = [place, own, beside, mine, other, high, low, front]
    specs = [
        pl.BlockSpec((tile, slot), lambda i, place: (base + i, 0)),
        pl.BlockSpec((tile, slot), lambda i, place: (base + i, 0)),
        pl.BlockSpec((tile, far), lambda i, place: (i, 0)),
        pl.BlockSpec((tile, far), lambda i, place: (i, 0)),
        whole,
        whole,
        pl.BlockSpec((tile, width), lambda i, place: (base + i, 0)),
    ]
    aliases = {}
    if schur is not None:
        aliases = {len(operands): 0}
        operands.append(schur)
        specs.append(pl.BlockSpec(memory_space=pl.ANY))
    return pl.pallas_call(
        functools.partial(update_kernel, start // LEAF),
        out_shape=[jax.ShapeDtypeStruct((height, width), F32), jax.ShapeDtypeStruct((rows, LEAF), F32)],
        grid_spec=pltpu.PrefetchScalarGridSpec(
            num_scalar_prefetch=1,
            grid=(rows // tile,),
            in_specs=specs,
            out_specs=[
                pl.BlockSpec((tile, width), lambda i, place: (base + i, 0)),
                pl.BlockSpec((tile, LEAF), lambda i, place: (i, 0)),
            ],
        ),
        input_output_aliases=aliases,
        compiler_params=pltpu.CompilerParams(vmem_limit_bytes=VMEM),
        cost_estimate=pl.CostEstimate(
            flops=6 * rows * panel * width, bytes_accessed=rows * width * 8 + panel * width * 4, transcendentals=0
        ),
        name="update",
    )(*operands)


def body(front_trailing, panel_columns, panel_rows, pivots, diag_inverse, test_matrix):
    hi_count, z_count = lax.axis_size("hi"), lax.axis_size("z")
    row_count, col_count = 2 * hi_count, 2 * z_count
    hi, lo, z, core = [lax.axis_index(name) for name in ALL]
    row, col = hi * 2 + lo, z * 2 + core
    height, width = front_trailing.shape
    depth, slot = panel_rows.shape[0], panel_columns.shape[1]
    panel = depth * row_count
    samples = test_matrix.shape[1]
    per = height // col_count
    ratio = col_count // row_count
    targets = col_count // ratio
    chunk = height // CHUNKS
    starts = list(range(0, height, chunk))

    over_lo = swap(panel_rows, "lo")
    over_hi = [shift(panel_rows, "hi", step) for step in range(1, hi_count)]
    blocks, owners = [panel_rows, over_lo], [row, row ^ 1]
    for step, block in enumerate(over_hi, 1):
        far_hi = (hi - step) % hi_count
        first = shift(over_lo[: depth // 2], "hi", step)
        second = swap(block[depth // 2 :], "lo")
        blocks += [block, first, second]
        owners += [far_hi * 2 + lo, far_hi * 2 + (1 - lo)]

    beside = swap(panel_columns, "core")
    gathered = []
    for start in starts:
        right = left = panel_columns[start : start + chunk]
        rights, lefts = [], []
        for _ in range(z_count - 1):
            right, left = hop(right, 1), hop(left, -1)
            rights.append(right)
            lefts.append(left)
        mine = jnp.concatenate(
            [jnp.where(z >= at, rights[at - 1], lefts[z_count - at - 1]) for at in range(1, z_count)], axis=1
        )
        gathered.append((mine, swap(mine, "core")))

    chips = [(z - at) % z_count for at in range(z_count)]
    order = [2 * chips[0] + core, 2 * chips[0] + 1 - core]
    order += [2 * chip + core for chip in chips[1:]] + [2 * chip + 1 - core for chip in chips[1:]]
    left = jnp.take(diag_inverse.reshape(col_count, slot, panel), jnp.stack(order), axis=0).reshape(panel, panel)
    position = (jnp.stack(owners)[:, None] * depth + jnp.arange(depth, dtype=jnp.int32)[None, :]).reshape(panel)
    chosen = (pivots[:, None] == position[None, :]).astype(BF16)
    left_high, left_low = [
        jnp.dot(part, chosen, preferred_element_type=F32).astype(BF16) for part in split_outside(left)
    ]

    inner = lax.psum(high_dot(panel_rows, test_matrix), ("z", "core"))
    inner = lax.all_gather(inner, ("hi", "lo"), axis=0, tiled=False)
    inner = jnp.take(inner, jnp.stack(owners), axis=0).reshape(panel, samples)
    inner_high, inner_low = split_outside(inner)
    near = 2 * slot
    middle = triple(left_high[:near], left_low[:near], inner_high, inner_low)

    row_leaf, col_leaf = row * (height // LEAF), col * (width // LEAF)
    sent = samples_half(front_trailing, test_matrix, jnp.stack([1 - core, row_leaf, col_leaf]), per)
    kept = samples_half(front_trailing, test_matrix, jnp.stack([core, row_leaf, col_leaf]), per)
    sent = swap(sent, "core")
    near_columns = jnp.concatenate([panel_columns, beside], axis=1).reshape(z_count, 2, per, near)
    near_columns = lax.dynamic_index_in_dim(near_columns, core, 1, keepdims=False).reshape(z_count * per, near)
    partial = (kept + sent - high_dot(near_columns, middle)).reshape(z_count, per, samples)
    right = left = None
    for step in range(1, z_count):
        right_part = lax.dynamic_index_in_dim(partial, jnp.minimum(z + z_count - step, z_count - 1), 0, keepdims=False)
        left_part = lax.dynamic_index_in_dim(partial, jnp.maximum(z - z_count + step, 0), 0, keepdims=False)
        right = hop(right_part if right is None else right_part + right, 1, step)
        left = hop(left_part if left is None else left_part + left, -1, step)
    sums = lax.dynamic_index_in_dim(partial, z, 0, keepdims=False) + right + left

    half = col % ratio
    leaf_count = per // LEAF
    routes = [
        [(r * col_count + ratio * r + h, r * col_count + h * targets + m) for r in range(row_count) for h in range(ratio)]
        for m in range(targets)
    ]

    def to_owners(pieces):
        return sum(lax.ppermute(piece, ALL, route) for piece, route in zip(pieces, routes))

    def front_leaf(at):
        return lax.dynamic_slice(front_trailing, (half * width + at * LEAF, at * LEAF), (LEAF, LEAF))

    early = []
    for m in range(targets):
        leaf = jnp.concatenate([front_leaf(m * leaf_count + at) for at in range(leaf_count)], axis=0)
        early.append(jnp.concatenate([test_matrix[m * per : (m + 1) * per], leaf], axis=1))
    early = to_owners(early)
    own_test, own_front = early[:, :samples], early[:, samples:]

    high, low = weights(left_high, left_low, blocks)
    place = jnp.stack([core, row_leaf, col_leaf])
    schur, leaves = None, []
    for start, (mine, other) in zip(starts, gathered):
        schur, leaf = update(place, panel_columns, beside, mine, other, high, low, front_trailing, schur, start)
        leaves.append(leaf)

    def leaf_rows(start):
        return leaves[start // chunk][start % chunk : start % chunk + per]

    late = []
    for m in range(targets):
        piece = leaf_rows(m * per)
        for h in range(1, ratio):
            piece = jnp.where(half == h, leaf_rows(h * width + m * per), piece)
        late.append(piece)
    leaf_blocks = to_owners(late)
    change = (own_front - leaf_blocks).reshape(leaf_count, LEAF, LEAF)
    change = high_dot(change, own_test.reshape(leaf_count, LEAF, samples), (((2,), (1,)), ((0,), (0,))))
    off_samples = sums + change.reshape(per, samples)
    gram = high_dot(off_samples, off_samples, (((0,), (0,)), ((), ())))
    group_gram = (lax.psum(gram, ("lo", "z", "core")) / (2 * height))[None]
    return (schur, off_samples, leaf_blocks, group_gram)


def solution(mesh):
    rows, cols = mesh.shape["row"], mesh.shape["col"]
    fine = Mesh(mesh.devices.reshape(rows // 2, 2, cols // 2, 2), ALL)
    row, col = ("hi", "lo"), ("z", "core")
    placed = (P(row, col), P(row, col), P(row, col), P(), P(), P(col, None))
    return jax.shard_map(
        body,
        mesh=fine,
        in_specs=placed,
        out_specs=(P(row, col), P(ALL, None), P(ALL, None), P(row, None, None)),
        check_vma=False,
    )
```

time: 699 us -> 576 us (0.82); the launches traced: 698 us -> 566 us
  matrix products: 247 us -> 23.9 us
  waiting for transfers between devices: 391 us -> 213 us
  Pallas kernels: 0 us -> 141 us
  starting transfers between devices: 1.62 us -> 119 us
  other arithmetic: 7.08 us -> 32.5 us
  local copies, waits for them, and re-layouts: 38.1 us -> 22.1 us
    all_gather x2 -> x1, waiting for transfers between devices: 231 us -> 0.01 us  [body(): inner = lax.all_gather(inner, ('hi', 'lo'), axis=0, tiled=False)]
    dot_general x4 -> x9, matrix products: 247 us -> 23.9 us  [the longest x4 11.5 us: high_dot(): lax.dot_general(left, right, dims, precision=lax.Precision.HIGH, preferre...]
    pallas_call x0 -> x7, Pallas kernels: none -> 141 us  [the longest x4 82.3 us: update(): pl.pallas_call(functools.partial(update_kernel, start // LEAF), out_shape...]
    ppermute x1 -> x48, starting transfers between devices: 1.47 us -> 118 us  [the longest x30 86.8 us: hop(): return lax.ppermute(value, 'z', route)]
    ppermute x1 -> x48, waiting for transfers between devices: 20.8 us -> 116 us  [the longest x30 57.3 us: hop(): return lax.ppermute(value, 'z', route)]
    reduce_scatter x1 -> x0, waiting for transfers between devices: 61.1 us -> none  [body(): lax.psum_scatter(product(masked, test_matrix), 'col', scatter_dimension=0...]
    psum x1 -> x2, waiting for transfers between devices: 76 us -> 96.8 us  [the longest x1 96.8 us: body(): group_gram = (lax.psum(gram, ('lo', 'z', 'core')) / (2 * height))[None]]
    gather x2, local copies, waits for them, and re-layouts: 18.8 us -> 7.3 us  [the longest x1 5.03 us: body(): jnp.take(diag_inverse.reshape(col_count, slot, panel), jnp.stack(order),...]
  transfers between devices with their start and end apart: 5 -> 51, of which waited for: 5 -> 17; matrix products, arithmetic and copies ran while one was open for 6% -> 12% of each run, Pallas kernels for 0% -> 25%
where the time goes in v1:
time: 576 us; the launch traced here: 566 us
  waiting for transfers between devices  213 us (37%)
  Pallas kernels  141 us (24%)
  starting transfers between devices  119 us (21%)
  other arithmetic  32.5 us (6%)
  matrix products  23.9 us (4%)
  local copies, waits for them, and re-layouts  22.1 us (4%)
  between operations  15.2 us (3%)
    psum x1, waiting for transfers between devices, body(): group_gram = (lax.psum(gram, ('lo', 'z', 'core')) / (2 * height))[None]  96.8 us
    ppermute x30, starting transfers between devices, hop(): return lax.ppermute(value, 'z', route)  86.8 us
    pallas_call x4, Pallas kernels, update(): pl.pallas_call(functools.partial(update_kernel, start // LEAF), out_shape...  82.3 us
    ppermute x30, waiting for transfers between devices, hop(): return lax.ppermute(value, 'z', route)  57.3 us
    ppermute x8, waiting for transfers between devices, to_owners(): lax.ppermute(piece, ALL, route)  46.1 us
    pallas_call x2, Pallas kernels, samples_half(): pl.pallas_call(samples_kernel, out_shape=jax.ShapeDtypeStruct((tiles * ro...  39.5 us
    ppermute x8, starting transfers between devices, to_owners(): lax.ppermute(piece, ALL, route)  26.3 us
    pallas_call x1, Pallas kernels, weights(): pl.pallas_call(functools.partial(weights_kernel, len(blocks)), out_shape=...  18.7 us
  transfers between devices with their start and end apart: 51, of which 17 were waited for; matrix products, arithmetic and copies ran while one was open for 12% of the time, Pallas kernels for 25%

profile of v1, /device:TPU:0, one launch (start us, length us, event | category | flops | bytes accessed | tf_op | source)
XLA Modules:
  0.0 565.8 jit_solution(5550715223903126295)
XLA Ops:
  11.3 6.4 %collective-permute-start.26 = (f32[1024,128]{1,0:T(8,128)S(1)}, f32[1024,128]{1,0:T(8,128)}, u32[]{:S(2)}, u32[]{:S(2)}) collective-permute-start(f32[1024,128]{1,0:T(8,128)S(1)} %get-tuple-element.56), channel_id=1, source_target_pairs={{0,2},{2,4},{4,6},{1,3},{3,5},{5,7},{8,10},{10,12},{12,14},{9,11},... | collective-permute-start | bytes 1572872 | tf_op jit(solution)/shard_map/ppermute | solution.py:53
  19.0 5.4 collective-permute-start.19
  32.1 19.7 %samples.2 = f32[2048,512]{1,0:T(8,128)} custom-call(s32[3]{0:T(128)} %add_add_fusion.2.place, f32[4096,2048]{1,0:T(8,128)} %front.11, f32[2048,512]{1,0:T(8,128)} %test.3), custom_call_target="tpu_custom_call" | custom-call | flops 12884901888 | bytes 16777216 | tf_op jit(solution)/shard_map/samples/pallas_call | solution.py:79
  51.8 19.8 %samples.3 = f32[2048,512]{1,0:T(8,128)} custom-call(s32[3]{0:T(128)} %add_add_fusion.3.place, f32[4096,2048]{1,0:T(8,128)} %front.11, f32[2048,512]{1,0:T(8,128)} %test.3), custom_call_target="tpu_custom_call" | custom-call | flops 12884901888 | bytes 16777216 | tf_op jit(solution)/shard_map/samples/pallas_call | solution.py:79
  71.6 5.0 gather_fusion
  99.6 6.0 %collective-permute-start.30 = (f32[1024,128]{1,0:T(8,128)}, f32[1024,128]{1,0:T(8,128)}, u32[]{:S(2)}, u32[]{:S(2)}) collective-permute-start(f32[1024,128]{1,0:T(8,128)} %collective-permute-done.26), channel_id=1, source_target_pairs={{0,2},{2,4},{4,6},{1,3},{3,5},{5,7},{8,10},{10,12},{12,14},{9,11},... | collective-permute-start | bytes 1572872 | tf_op jit(solution)/shard_map/ppermute | solution.py:53
  113.2 5.3 collective-permute-start.23
  163.8 8.2 %collective-permute-done.31 = f32[1024,128]{1,0:T(8,128)S(1)} collective-permute-done((f32[1024,128]{1,0:T(8,128)}, f32[1024,128]{1,0:T(8,128)S(1)}, u32[]{:S(2)}, u32[]{:S(2)}) %collective-permute-start.31) | collective-permute-done | bytes 524320 | tf_op jit(solution)/shard_map/ppermute | solution.py:53
  178.9 7.4 %collective-permute-done.24 = f32[1024,128]{1,0:T(8,128)S(1)} collective-permute-done((f32[1024,128]{1,0:T(8,128)}, f32[1024,128]{1,0:T(8,128)S(1)}, u32[]{:S(2)}, u32[]{:S(2)}) %collective-permute-start.24) | collective-permute-done | bytes 524320 | tf_op jit(solution)/shard_map/ppermute | solution.py:53
  188.6 5.3 collective-permute-done.22
  196.4 6.2 %collective-permute-done.15 = f32[1024,128]{1,0:T(8,128)S(1)} collective-permute-done((f32[1024,128]{1,0:T(8,128)S(1)}, f32[1024,128]{1,0:T(8,128)S(1)}, u32[]{:S(2)}, u32[]{:S(2)}) %collective-permute-start.15) | collective-permute-done | bytes 524320 | tf_op jit(solution)/shard_map/ppermute | solution.py:53
  208.7 7.3 %collective-permute-done.4 = f32[1024,128]{1,0:T(8,128)S(1)} collective-permute-done((f32[1024,128]{1,0:T(8,128)S(1)}, f32[1024,128]{1,0:T(8,128)S(1)}, u32[]{:S(2)}, u32[]{:S(2)}) %collective-permute-start.4) | collective-permute-done | bytes 524320 | tf_op jit(solution)/shard_map/ppermute | solution.py:53
  217.2 11.3 %collective-permute-start.40 = (f32[512,640]{1,0:T(8,128)}, f32[512,640]{1,0:T(8,128)}, u32[]{:S(2)}, u32[]{:S(2)}) collective-permute-start(f32[512,640]{1,0:T(8,128)} %maximum_maximum_fusion), channel_id=1, source_target_pairs={{0,0},{1,4},{10,8},{11,12},{20,16},{21,20},{30,24},{31,28}} | collective-permute-start | bytes 3932168 | tf_op jit(solution)/shard_map/ppermute | solution.py:262
  236.4 12.8 %collective-permute-done.10.refs_5_ = f32[128,2048]{1,0:T(8,128)S(1)} collective-permute-done((f32[128,2048]{1,0:T(8,128)S(1)}, f32[128,2048]{1,0:T(8,128)S(1)}, u32[]{:S(2)}, u32[]{:S(2)}) %collective-permute-start.10) | collective-permute-done | bytes 1048608 | tf_op jit(solution)/shard_map/ppermute | solution.py:43
  252.6 18.7 %weights.1 = (bf16[1024,2048]{1,0:T(8,128)(2,1)}, bf16[1024,2048]{1,0:T(8,128)(2,1)}) custom-call(bf16[1024,1024]{1,0:T(8,128)(2,1)} %fusion.10.refs_0_, bf16[1024,1024]{1,0:T(8,128)(2,1)} %fusion.13.refs_1_, f32[256,2048]{1,0:T(8,128)} %refs_2_.1, f32[256,2048]{1,0:T(8,128)} %copy-done.12, f32[256,2048]{1,0:T(8,128)} %copy-done.13, f32[128,2048]{1,0:T(8,128)} %copy-done.24, ...), custom_call_target="tpu_custom_call" | custom-call | flops 12884901888 | bytes 16777216 | tf_op jit(solution)/shard_map/weights/pallas_call | solution.py:113
  272.5 20.4 %update.4 = (f32[4096,2048]{1,0:T(8,128)}, f32[1024,128]{1,0:T(8,128)}) custom-call(s32[3]{0:T(128)} %add_add_fusion.2.place, f32[4096,128]{1,0:T(8,128)} %own.7, f32[4096,128]{1,0:T(8,128)} %copy-done.1, f32[1024,384]{1,0:T(8,128)} %copy-done.5, f32[1024,384]{1,0:T(8,128)} %copy-done.9, bf16[1024,2048]{1,0:T(8,128)(2,1)} %get-tuple-element.14.high, ...), custom_call_target="tpu_custom_call" | custom-call | flops 12884901888 | bytes 25165824 | tf_op jit(solution)/shard_map/update/pallas_call | solution.py:162
  309.0 20.5 %update.5 = (f32[4096,2048]{1,0:T(8,128)}, f32[1024,128]{1,0:T(8,128)}) custom-call(s32[3]{0:T(128)} %add_add_fusion.2.place, f32[4096,128]{1,0:T(8,128)} %own.7, f32[4096,128]{1,0:T(8,128)} %copy-done.1, f32[1024,384]{1,0:T(8,128)} %pad_maximum_fusion.3.mine, f32[1024,384]{1,0:T(8,128)} %collective-permute-done.25.other, ...), custom_call_target="tpu_custom_call", output_to_operand_aliasing={{0}: (8, {})} | custom-call | flops 12884901888 | bytes 25165824 | tf_op jit(solution)/shard_map/update/pallas_call | solution.py:162
  335.3 5.4 collective-permute-start.35
  340.6 20.9 %update.6 = (f32[4096,2048]{1,0:T(8,128)}, f32[1024,128]{1,0:T(8,128)}) custom-call(s32[3]{0:T(128)} %add_add_fusion.2.place, f32[4096,128]{1,0:T(8,128)} %own.7, f32[4096,128]{1,0:T(8,128)} %copy-done.1, f32[1024,384]{1,0:T(8,128)} %pad_maximum_fusion.2.mine, f32[1024,384]{1,0:T(8,128)} %collective-permute-done.18.other, ...), custom_call_target="tpu_custom_call", output_to_operand_aliasing={{0}: (8, {})} | custom-call | flops 12884901888 | bytes 25165824 | tf_op jit(solution)/shard_map/update/pallas_call | solution.py:162
  372.6 20.6 %update.7 = (f32[4096,2048]{1,0:T(8,128)}, f32[1024,128]{1,0:T(8,128)}) custom-call(s32[3]{0:T(128)} %add_add_fusion.2.place, f32[4096,128]{1,0:T(8,128)} %own.7, f32[4096,128]{1,0:T(8,128)} %copy-done.1, f32[1024,384]{1,0:T(8,128)} %pad_maximum_fusion.1.mine, f32[1024,384]{1,0:T(8,128)} %copy-done.10, ...), custom_call_target="tpu_custom_call", output_to_operand_aliasing={{0}: (8, {})} | custom-call | flops 12884901888 | bytes 25165824 | tf_op jit(solution)/shard_map/update/pallas_call | solution.py:162
  402.3 19.9 %collective-permute-done.43 = f32[512,640]{1,0:T(8,128)} collective-permute-done((f32[512,640]{1,0:T(8,128)}, f32[512,640]{1,0:T(8,128)}, u32[]{:S(2)}, u32[]{:S(2)}) %collective-permute-start.43) | collective-permute-done | bytes 1310752 | tf_op jit(solution)/shard_map/ppermute | solution.py:262
  429.6 20.6 %collective-permute-done.46 = f32[512,128]{1,0:T(8,128)S(1)} collective-permute-done((f32[512,128]{1,0:T(8,128)S(1)}, f32[512,128]{1,0:T(8,128)S(1)}, u32[]{:S(2)}, u32[]{:S(2)}) %collective-permute-start.46) | collective-permute-done | bytes 262176 | tf_op jit(solution)/shard_map/ppermute | solution.py:262
  450.2 5.6 collective-permute-done.47
  459.8 96.8 %all-reduce.5.cloned.1.call-done = f32[512,512]{1,0:T(8,128)} async-done(((f32[512,512]{1,0:T(8,128)}), f32[512,512]{1,0:T(8,128)}) %all-reduce.5.cloned.1.call-update) | async-done | bytes 1048592 | tf_op jit(solution)/shard_map/psum | solution.py:295
  (209 shorter events, 175.5 us)
Async XLA Ops:
  7.2 112.7 %all-reduce.3.cloned.1.call-start = ((), (), s32[]{:S(2)}) async-start(), calls=%async_computation | async-start | bytes 1048576 | tf_op jit(solution)/shard_map/psum | solution.py:232
  10.0 79.8 %collective-permute-start.27 = (f32[1024,128]{1,0:T(8,128)S(1)}, f32[1024,128]{1,0:T(8,128)}, u32[]{:S(2)}, u32[]{:S(2)}) collective-permute-start(f32[1024,128]{1,0:T(8,128)S(1)} %get-tuple-element.56), channel_id=1, source_target_pairs={{2,0},{4,2},{6,4},{3,1},{5,3},{7,5},{10,8},{12,10},{14,12},{11,9},... | collective-permute-start | bytes 1572872 | tf_op jit(solution)/shard_map/ppermute | solution.py:53
  11.3 83.1 %collective-permute-start.26 = (f32[1024,128]{1,0:T(8,128)S(1)}, f32[1024,128]{1,0:T(8,128)}, u32[]{:S(2)}, u32[]{:S(2)}) collective-permute-start(f32[1024,128]{1,0:T(8,128)S(1)} %get-tuple-element.56), channel_id=1, source_target_pairs={{0,2},{2,4},{4,6},{1,3},{3,5},{5,7},{8,10},{10,12},{12,14},{9,11},... | collective-permute-start | bytes 1572872 | tf_op jit(solution)/shard_map/ppermute | solution.py:53
  17.7 80.6 %collective-permute-start.20 = (f32[1024,128]{1,0:T(8,128)}, f32[1024,128]{1,0:T(8,128)}, u32[]{:S(2)}, u32[]{:S(2)}) collective-permute-start(f32[1024,128]{1,0:T(8,128)} %get-tuple-element.57), channel_id=1, source_target_pairs={{2,0},{4,2},{6,4},{3,1},{5,3},{7,5},{10,8},{12,10},{14,12},{11,9},... | collective-permute-start | bytes 1572872 | tf_op jit(solution)/shard_map/ppermute | solution.py:53
  19.0 80.6 %collective-permute-start.19 = (f32[1024,128]{1,0:T(8,128)}, f32[1024,128]{1,0:T(8,128)}, u32[]{:S(2)}, u32[]{:S(2)}) collective-permute-start(f32[1024,128]{1,0:T(8,128)} %get-tuple-element.57), channel_id=1, source_target_pairs={{0,2},{2,4},{4,6},{1,3},{3,5},{5,7},{8,10},{10,12},{12,14},{9,11},... | collective-permute-start | bytes 1572872 | tf_op jit(solution)/shard_map/ppermute | solution.py:53
  29.0 263.9 %all-gather.2.cloned.1.call-start = ((), (), s32[]{:S(2)}) async-start(), calls=%async_computation.1 | async-start | bytes 2621440 | tf_op jit(solution)/shard_map/all_gather | solution.py:233
  29.1 78.9 %collective-permute-start.13 = (f32[1024,128]{1,0:T(8,128)S(1)}, f32[1024,128]{1,0:T(8,128)S(1)}, u32[]{:S(2)}, u32[]{:S(2)}) collective-permute-start(f32[1024,128]{1,0:T(8,128)S(1)} %get-tuple-element.58), channel_id=1, source_target_pairs={{2,0},{4,2},{6,4},{3,1},{5,3},{7,5},{10,8},{12,10},{14,12},{11,9},... | collective-permute-start | bytes 1572872 | tf_op jit(solution)/shard_map/ppermute | solution.py:53
  119.9 436.7 %all-reduce.5.cloned.1.call-start = ((), (), s32[]{:S(2)}) async-start(), calls=%async_computation.2 | async-start | bytes 2097152 | tf_op jit(solution)/shard_map/psum | solution.py:295
  129.8 103.9 %collective-permute-start = (f32[4096,128]{1,0:T(8,128)S(1)}, f32[4096,128]{1,0:T(8,128)S(1)}, u32[]{:S(2)}, u32[]{:S(2)}) collective-permute-start(f32[4096,128]{1,0:T(8,128)S(1)} %copy-done), channel_id=1, source_target_pairs={{0,1},{1,0},{2,3},{3,2},{4,5},{5,4},{6,7},{7,6},{8,9},{9,8},{10,11... | collective-permute-start | bytes 6291464 | tf_op jit(solution)/shard_map/ppermute | solution.py:38
  145.5 83.0 %collective-permute-start.8 = (f32[256,2048]{1,0:T(8,128)S(1)}, f32[256,2048]{1,0:T(8,128)S(1)}, u32[]{:S(2)}, u32[]{:S(2)}) collective-permute-start(f32[256,2048]{1,0:T(8,128)S(1)} %copy-done.8), channel_id=1, source_target_pairs={{0,8},{8,0},{1,9},{9,1},{2,10},{10,2},{3,11},{11,3},{4,12},{12,4},... | collective-permute-start | bytes 6291464 | tf_op jit(solution)/shard_map/ppermute | solution.py:38
  155.6 73.2 %collective-permute-start.9 = (f32[256,2048]{1,0:T(8,128)S(1)}, f32[256,2048]{1,0:T(8,128)S(1)}, u32[]{:S(2)}, u32[]{:S(2)}) collective-permute-start(f32[256,2048]{1,0:T(8,128)S(1)} %copy-done.8), channel_id=1, source_target_pairs={{0,16},{16,0},{1,17},{17,1},{2,18},{18,2},{3,19},{19,3},{4,20},{20... | collective-permute-start | bytes 6291464 | tf_op jit(solution)/shard_map/ppermute | solution.py:43
  215.9 84.4 %collective-permute-start.33 = (f32[2048,512]{1,0:T(8,128)}, f32[2048,512]{1,0:T(8,128)}, u32[]{:S(2)}, u32[]{:S(2)}) collective-permute-start(f32[2048,512]{1,0:T(8,128)} %samples.3), channel_id=1, source_target_pairs={{0,1},{1,0},{2,3},{3,2},{4,5},{5,4},{6,7},{7,6},{8,9},{9,8},{10,11... | collective-permute-start | bytes 12582920 | tf_op jit(solution)/shard_map/ppermute | solution.py:38
  217.2 177.1 %collective-permute-start.40 = (f32[512,640]{1,0:T(8,128)}, f32[512,640]{1,0:T(8,128)}, u32[]{:S(2)}, u32[]{:S(2)}) collective-permute-start(f32[512,640]{1,0:T(8,128)} %maximum_maximum_fusion), channel_id=1, source_target_pairs={{0,0},{1,4},{10,8},{11,12},{20,16},{21,20},{30,24},{31,28}} | collective-permute-start | bytes 3932168 | tf_op jit(solution)/shard_map/ppermute | solution.py:262
  233.7 37.6 %collective-permute-start.32 = (f32[1024,384]{1,0:T(8,128)S(1)}, f32[1024,384]{1,0:T(8,128)S(1)}, u32[]{:S(2)}, u32[]{:S(2)}) collective-permute-start(f32[1024,384]{1,0:T(8,128)S(1)} %pad_maximum_fusion.4.mine), channel_id=1, source_target_pairs={{0,1},{1,0},{2,3},{3,2},{4,5},{5,4},{6,7},{7,6},{8,9},{9,8},{10,11... | collective-permute-start | bytes 4718600 | tf_op jit(solution)/shard_map/ppermute | solution.py:38
  249.3 149.0 %collective-permute-start.41 = (f32[512,640]{1,0:T(8,128)}, f32[512,640]{1,0:T(8,128)}, u32[]{:S(2)}, u32[]{:S(2)}) collective-permute-start(f32[512,640]{1,0:T(8,128)} %maximum_maximum_fusion.1), channel_id=1, source_target_pairs={{0,1},{1,5},{10,9},{11,13},{20,17},{21,21},{30,25},{31,29}} | collective-permute-start | bytes 3932168 | tf_op jit(solution)/shard_map/ppermute | solution.py:262
  252.6 54.1 %collective-permute-start.25 = (f32[1024,384]{1,0:T(8,128)}, f32[1024,384]{1,0:T(8,128)}, u32[]{:S(2)}, u32[]{:S(2)}) collective-permute-start(f32[1024,384]{1,0:T(8,128)} %pad_maximum_fusion.3.mine), channel_id=1, source_target_pairs={{0,1},{1,0},{2,3},{3,2},{4,5},{5,4},{6,7},{7,6},{8,9},{9,8},{10,11... | collective-permute-start | bytes 4718600 | tf_op jit(solution)/shard_map/ppermute | solution.py:38
  271.3 64.0 %collective-permute-start.18 = (f32[1024,384]{1,0:T(8,128)}, f32[1024,384]{1,0:T(8,128)}, u32[]{:S(2)}, u32[]{:S(2)}) collective-permute-start(f32[1024,384]{1,0:T(8,128)} %pad_maximum_fusion.2.mine), channel_id=1, source_target_pairs={{0,1},{1,0},{2,3},{3,2},{4,5},{5,4},{6,7},{7,6},{8,9},{9,8},{10,11... | collective-permute-start | bytes 4718600 | tf_op jit(solution)/shard_map/ppermute | solution.py:38
  300.4 71.0 %collective-permute-start.7 = (f32[1024,384]{1,0:T(8,128)S(1)}, f32[1024,384]{1,0:T(8,128)S(1)}, u32[]{:S(2)}, u32[]{:S(2)}) collective-permute-start(f32[1024,384]{1,0:T(8,128)S(1)} %copy-done.6), channel_id=1, source_target_pairs={{0,1},{1,0},{2,3},{3,2},{4,5},{5,4},{6,7},{7,6},{8,9},{9,8},{10,11... | collective-permute-start | bytes 4718600 | tf_op jit(solution)/shard_map/ppermute | solution.py:38
  331.2 32.1 %collective-permute-start.37 = (f32[512,512]{1,0:T(8,128)}, f32[512,512]{1,0:T(8,128)}, u32[]{:S(2)}, u32[]{:S(2)}) collective-permute-start(f32[512,512]{1,0:T(8,128)} %get-tuple-element.49), channel_id=1, source_target_pairs={{6,4},{7,5},{14,12},{15,13},{22,20},{23,21},{30,28},{31,29}} | collective-permute-start | bytes 3145736 | tf_op jit(solution)/shard_map/ppermute | solution.py:53
  363.3 36.4 %collective-permute-start.42 = (f32[512,640]{1,0:T(8,128)}, f32[512,640]{1,0:T(8,128)}, u32[]{:S(2)}, u32[]{:S(2)}) collective-permute-start(f32[512,640]{1,0:T(8,128)} %maximum_maximum_fusion.2), channel_id=1, source_target_pairs={{0,2},{1,6},{10,10},{11,14},{20,18},{21,22},{30,26},{31,30}} | collective-permute-start | bytes 3932168 | tf_op jit(solution)/shard_map/ppermute | solution.py:262
  365.7 56.5 %collective-permute-start.43 = (f32[512,640]{1,0:T(8,128)}, f32[512,640]{1,0:T(8,128)}, u32[]{:S(2)}, u32[]{:S(2)}) collective-permute-start(f32[512,640]{1,0:T(8,128)} %maximum_maximum_fusion.3), channel_id=1, source_target_pairs={{0,3},{1,7},{10,11},{11,15},{20,19},{21,23},{30,27},{31,31}} | collective-permute-start | bytes 3932168 | tf_op jit(solution)/shard_map/ppermute | solution.py:262
  394.5 62.7 %collective-permute-start.36 = (f32[512,512]{1,0:T(8,128)S(1)}, f32[512,512]{1,0:T(8,128)S(1)}, u32[]{:S(2)}, u32[]{:S(2)}) collective-permute-start(f32[512,512]{1,0:T(8,128)S(1)} %copy-done.11), channel_id=1, source_target_pairs={{0,2},{2,4},{4,6},{1,3},{3,5},{5,7},{8,10},{10,12},{12,14},{9,11},... | collective-permute-start | bytes 3145736 | tf_op jit(solution)/shard_map/ppermute | solution.py:53
  398.3 58.9 %collective-permute-start.39 = (f32[512,512]{1,0:T(8,128)S(1)}, f32[512,512]{1,0:T(8,128)S(1)}, u32[]{:S(2)}, u32[]{:S(2)}) collective-permute-start(f32[512,512]{1,0:T(8,128)S(1)} %bitcast_add_fusion.2), channel_id=1, source_target_pairs={{2,0},{4,2},{6,4},{3,1},{5,3},{7,5},{10,8},{12,10},{14,12},{11,9},... | collective-permute-start | bytes 3145736 | tf_op jit(solution)/shard_map/ppermute | solution.py:53
  423.5 32.3 %collective-permute-start.47 = (f32[512,128]{1,0:T(8,128)S(1)}, f32[512,128]{1,0:T(8,128)S(1)}, u32[]{:S(2)}, u32[]{:S(2)}) collective-permute-start(f32[512,128]{1,0:T(8,128)S(1)} %get-tuple-element.63), channel_id=1, source_target_pairs={{0,3},{1,7},{10,11},{11,15},{20,19},{21,23},{30,27},{31,31}} | collective-permute-start | bytes 786440 | tf_op jit(solution)/shard_map/ppermute | solution.py:262
  (54 other events, 866.3 us)
Sparse Core Ops, SparseCore 0:
  29.1 58.0 all-reduce.2
  120.0 41.8 all-gather.1
  459.9 96.6 all-reduce.4

commit v2 on v1

v2 whole, which is shorter than its diff:
```python
import functools

import jax
import jax.numpy as jnp
from jax import lax
from jax.experimental import pallas as pl
from jax.experimental.pallas import tpu as pltpu
from jax.sharding import Mesh, PartitionSpec as P

LEAF = 128
SHARES = (8, 5, 3)
VMEM = 56 * 1024 * 1024
F32 = jnp.float32
BF16 = jnp.bfloat16
ALL = ("hi", "lo", "z", "core")


def split(value):
    high = value.astype(BF16)
    return high, (value - high.astype(F32)).astype(BF16)


def split_outside(value):
    high = lax.reduce_precision(value, exponent_bits=8, mantissa_bits=7)
    return high.astype(BF16), (value - high).astype(BF16)


def triple(left_high, left_low, right_high, right_low):
    dot = functools.partial(jnp.dot, preferred_element_type=F32)
    return dot(left_high, right_high) + (dot(left_high, right_low) + dot(left_low, right_high))


def high_dot(left, right, dims=(((1,), (0,)), ((), ()))):
    return lax.dot_general(left, right, dims, precision=lax.Precision.HIGH, preferred_element_type=F32)


def swap(value, axis):
    return lax.ppermute(value, axis, [(0, 1), (1, 0)])


def shift(value, axis, step):
    count = lax.axis_size(axis)
    return lax.ppermute(value, axis, [(at, (at + step) % count) for at in range(count)])


def hop(value, step, count=None):
    chips = lax.axis_size("z")
    count = chips - 1 if count is None else count
    if step > 0:
        route = [(at, at + 1) for at in range(count)]
    else:
        route = [(at, at - 1) for at in range(chips - count, chips)]
    return lax.ppermute(value, "z", route)


def weights_kernel(parts, *refs):
    left_high, left_low = refs[0], refs[1]
    rows = jnp.concatenate([ref[...] for ref in refs[2 : 2 + parts]], axis=0)
    high, low = split(rows)
    out_high, out_low = refs[2 + parts :]
    out_high[...], out_low[...] = split(triple(left_high[...], left_low[...], high, low))


def weights(left_high, left_low, blocks):
    panel = left_high.shape[0]
    width = blocks[0].shape[1]
    tile = min(width, 512)
    whole = pl.BlockSpec((panel, panel), lambda n: (0, 0), pipeline_mode=pl.Buffered(1))
    return pl.pallas_call(
        functools.partial(weights_kernel, len(blocks)),
        out_shape=[jax.ShapeDtypeStruct((panel, width), BF16)] * 2,
        grid=(width // tile,),
        in_specs=[whole, whole] + [pl.BlockSpec((b.shape[0], tile), lambda n: (0, n)) for b in blocks],
        out_specs=[pl.BlockSpec((panel, tile), lambda n: (0, n))] * 2,
        compiler_params=pltpu.CompilerParams(vmem_limit_bytes=VMEM),
        cost_estimate=pl.CostEstimate(flops=6 * panel * panel * width, bytes_accessed=panel * width * 8, transcendentals=0),
        name="weights",
    )(left_high, left_low, *blocks)


def update_kernel(first, place, gathered, beside, high, low, test_high, test_low, front, *refs):
    out, leaves, kept, sent = refs[-4:]
    chips, _, rows, _ = gathered.shape
    width, samples = out.shape[-1], kept.shape[-1]
    per_leaf = place[3]
    columns = [gathered[at].reshape(2 * rows, -1) for at in range(chips)]
    columns += [beside[at].reshape(2 * rows, -1) for at in range(chips)]
    left_high, left_low = split(jnp.concatenate(columns, axis=1))
    dot = functools.partial(jnp.dot, preferred_element_type=F32)

    number = lax.broadcasted_iota(jnp.int32, (2 * rows, 1), 0)
    second = number >= rows
    owner = place[1] + 2 * pl.program_id(0) * per_leaf
    row_leaf = owner + jnp.where(second, per_leaf + (number - rows + first) // LEAF, (number + first) // LEAF)

    step = min(width, 512)
    sums = jnp.zeros((2 * rows, samples), F32)
    for at in range(0, width, step):
        part = slice(at, at + step)
        value = dot(left_high, high[:, part])
        value = value + dot(left_high, low[:, part])
        value = value + dot(left_low, high[:, part])
        value = front[:, :, part].reshape(2 * rows, step) - value
        out[:, :, part] = value.reshape(2, rows, step)
        col_leaf = place[2] + at // LEAF + lax.broadcasted_iota(jnp.int32, (1, step), 1) // LEAF
        value_high, value_low = split(jnp.where(row_leaf == col_leaf, 0.0, value))
        sums = sums + dot(value_high, test_high[part])
        sums = sums + dot(value_high, test_low[part])
        sums = sums + dot(value_low, test_high[part])
    kept[0] = jnp.where(place[0] == 0, sums[:rows], sums[rows:])
    sent[0] = jnp.where(place[0] == 0, sums[rows:], sums[:rows])

    for which in range(2):
        at = 0
        while at < rows:
            size = min(rows - at, LEAF - (first + at) % LEAF)
            leaf = owner + which * per_leaf + (first + at) // LEAF - place[2]
            column = pl.multiple_of(jnp.clip(leaf, 0, width // LEAF - 1) * LEAF, LEAF)
            leaves[which, at : at + size] = out[which, at : at + size, pl.ds(column, LEAF)]
            at += size


def update(place, gathered, beside, weight, test, front, schur, first):
    chips, owners, rows, slot = gathered.shape
    _, per, width = front.shape
    panel, samples = weight[0].shape[0], test[0].shape[1]

    def whole(array):
        return pl.BlockSpec(array.shape, lambda i, place: (0, 0), pipeline_mode=pl.Buffered(1))

    def window(size):
        return pl.BlockSpec(
            (pl.Element(2), pl.Element(rows), pl.Element(size)), lambda i, place: (2 * i, first, 0)
        )

    block = pl.BlockSpec((chips, 2, rows, slot), lambda i, place: (0, i, 0, 0))
    operands = [place, gathered, beside, *weight, *test, front]
    specs = [block, block, *map(whole, weight), *map(whole, test), window(width)]
    aliases = {}
    if schur is not None:
        aliases = {len(operands): 0}
        operands.append(schur)
        specs.append(pl.BlockSpec(memory_space=pl.ANY))
    sums = jax.ShapeDtypeStruct((owners // 2, rows, samples), F32)
    flops = 6 * owners * rows * width * (panel + samples)
    return pl.pallas_call(
        functools.partial(update_kernel, first),
        out_shape=[
            jax.ShapeDtypeStruct(front.shape, F32),
            jax.ShapeDtypeStruct((owners, rows, LEAF), F32),
            sums,
            sums,
        ],
        grid_spec=pltpu.PrefetchScalarGridSpec(
            num_scalar_prefetch=1,
            grid=(owners // 2,),
            in_specs=specs,
            out_specs=[
                window(width),
                pl.BlockSpec((2, rows, LEAF), lambda i, place: (i, 0, 0)),
                pl.BlockSpec((1, rows, samples), lambda i, place: (i, 0, 0)),
                pl.BlockSpec((1, rows, samples), lambda i, place: (i, 0, 0)),
            ],
        ),
        input_output_aliases=aliases,
        compiler_params=pltpu.CompilerParams(vmem_limit_bytes=VMEM),
        cost_estimate=pl.CostEstimate(
            flops=flops, bytes_accessed=owners * rows * width * 8 + panel * width * 4, transcendentals=0
        ),
        name="update",
    )(*operands)


def scatter_sum(kept, sent):
    chips, z = lax.axis_size("z"), lax.axis_index("z")
    partial = kept + swap(sent, "core")
    right = left = None
    for step in range(1, chips):
        right_part = lax.dynamic_index_in_dim(partial, jnp.minimum(z + chips - step, chips - 1), 0, keepdims=False)
        left_part = lax.dynamic_index_in_dim(partial, jnp.maximum(z - chips + step, 0), 0, keepdims=False)
        right = hop(right_part if right is None else right_part + right, 1, step)
        left = hop(left_part if left is None else left_part + left, -1, step)
    return lax.dynamic_index_in_dim(partial, z, 0, keepdims=False) + right + left


def halve(value, axis):
    half = value.shape[0] // 2
    at = lax.axis_index(axis)
    mine = lax.dynamic_slice_in_dim(value, at * half, half, 0)
    return mine + swap(lax.dynamic_slice_in_dim(value, (1 - at) * half, half, 0), axis)


def double(value, axis):
    other = swap(value, axis)
    first = lax.axis_index(axis) == 0
    return jnp.concatenate([jnp.where(first, value, other), jnp.where(first, other, value)], axis=0)


def group_sum(gram):
    chips, z = lax.axis_size("z"), lax.axis_index("z")
    value = halve(halve(gram, "core"), "lo")
    parts = value.reshape(chips, value.shape[0] // chips, value.shape[1])
    total = lax.dynamic_index_in_dim(parts, z, 0, keepdims=False)
    for step in range(1, chips):
        part = lax.dynamic_index_in_dim(parts, (z + step) % chips, 0, keepdims=False)
        total = total + shift(part, "z", step)
    parts = jnp.stack([total] + [shift(total, "z", step) for step in range(1, chips)])
    value = jnp.take(parts, (z - jnp.arange(chips)) % chips, axis=0).reshape(value.shape)
    return double(double(value, "lo"), "core")


def body(front_trailing, panel_columns, panel_rows, pivots, diag_inverse, test_matrix):
    hi_count, z_count = lax.axis_size("hi"), lax.axis_size("z")
    row_count, col_count = 2 * hi_count, 2 * z_count
    hi, lo, z, core = [lax.axis_index(name) for name in ALL]
    row, col = hi * 2 + lo, z * 2 + core
    height, width = front_trailing.shape
    depth, slot = panel_rows.shape[0], panel_columns.shape[1]
    panel = depth * row_count
    samples = test_matrix.shape[1]
    per = height // col_count
    ratio = col_count // row_count
    targets = col_count // ratio

    stops = [per * sum(SHARES[: at + 1]) // 16 for at in range(len(SHARES))]
    chunks = list(zip([0] + stops[:-1], stops))
    owned = panel_columns.reshape(col_count, per, slot)
    gathered = [lax.all_gather(owned[:, start:stop], "z", axis=0, tiled=False) for start, stop in chunks]

    over_lo = swap(panel_rows, "lo")
    over_hi = [shift(panel_rows, "hi", step) for step in range(1, hi_count)]
    blocks, owners = [panel_rows, over_lo], [row, row ^ 1]
    for step, block in enumerate(over_hi, 1):
        far_hi = (hi - step) % hi_count
        first = shift(over_lo[: depth // 2], "hi", step)
        second = swap(block[depth // 2 :], "lo")
        blocks += [block, first, second]
        owners += [far_hi * 2 + lo, far_hi * 2 + (1 - lo)]

    order = [2 * chip + core for chip in range(z_count)] + [2 * chip + 1 - core for chip in range(z_count)]
    left = jnp.take(diag_inverse.reshape(col_count, slot, panel), jnp.stack(order), axis=0).reshape(panel, panel)
    position = (jnp.stack(owners)[:, None] * depth + jnp.arange(depth, dtype=jnp.int32)[None, :]).reshape(panel)
    chosen = (pivots[:, None] == position[None, :]).astype(BF16)
    left_high, left_low = [
        jnp.dot(part, chosen, preferred_element_type=F32).astype(BF16) for part in split_outside(left)
    ]
    weight = weights(left_high, left_low, blocks)
    test = split_outside(test_matrix)

    place = jnp.stack([core, row * (height // LEAF), col * (width // LEAF), jnp.int32(per // LEAF)])
    front = front_trailing.reshape(col_count, per, width)
    schur, leaves, sums = None, [], []
    for (start, stop), mine in zip(chunks, gathered):
        schur, leaf, kept, sent = update(place, mine, swap(mine, "core"), weight, test, front, schur, start)
        leaves.append(leaf)
        sums.append(scatter_sum(kept, sent))

    off_samples = jnp.concatenate(sums, axis=0)
    gram = high_dot(off_samples, off_samples, (((0,), (0,)), ((), ())))
    group_gram = (group_sum(gram) / (2 * height))[None]

    half = col % ratio
    leaf_blocks = 0
    for m in range(targets):
        pieces = [lax.dynamic_index_in_dim(leaf, half * targets + m, 0, keepdims=False) for leaf in leaves]
        route = [
            (r * col_count + ratio * r + h, r * col_count + h * targets + m)
            for r in range(row_count)
            for h in range(ratio)
        ]
        leaf_blocks = leaf_blocks + lax.ppermute(jnp.concatenate(pieces, axis=0), ALL, route)
    return (schur.reshape(height, width), off_samples, leaf_blocks, group_gram)


def solution(mesh):
    rows, cols = mesh.shape["row"], mesh.shape["col"]
    fine = Mesh(mesh.devices.reshape(rows // 2, 2, cols // 2, 2), ALL)
    row, col = ("hi", "lo"), ("z", "core")
    placed = (P(row, col), P(row, col), P(row, col), P(), P(), P(col, None))
    return jax.shard_map(
        body,
        mesh=fine,
        in_specs=placed,
        out_specs=(P(row, col), P(ALL, None), P(ALL, None), P(row, None, None)),
        check_vma=False,
    )
```

time: 576 us -> 458 us (0.80); the launches traced: 566 us -> 457 us
  starting transfers between devices: 119 us -> 71.9 us
  waiting for transfers between devices: 213 us -> 171 us
  matrix products: 23.9 us -> 8.69 us
  Pallas kernels: 141 us -> 132 us
    all_gather x1 -> x3, waiting for transfers between devices: 0.01 us -> 121 us  [body(): lax.all_gather(owned[:, start:stop], 'z', axis=0, tiled=False)]
    psum x2 -> x0, waiting for transfers between devices: 96.8 us -> none  [the longest x1 96.8 us: body(): group_gram = (lax.psum(gram, ('lo', 'z', 'core')) / (2 * height))[None]]
    ppermute x30 -> x18, starting transfers between devices: 86.8 us -> 43.7 us  [hop(): return lax.ppermute(value, 'z', route)]
    ppermute x30 -> x18, waiting for transfers between devices: 57.3 us -> 19 us  [hop(): return lax.ppermute(value, 'z', route)]
    ppermute x8 -> x4, waiting for transfers between devices: 46.1 us -> 8.03 us  [body(): lax.ppermute(jnp.concatenate(pieces, axis=0), ALL, route)]
    ppermute x8 -> x4, starting transfers between devices: 26.3 us -> 7.3 us  [body(): lax.ppermute(jnp.concatenate(pieces, axis=0), ALL, route)]
    add x5 -> x19, other arithmetic: 9.18 us -> 27.5 us  [the longest x6 11.8 us: scatter_sum(): right = hop(right_part if right is None else right_part + right, 1, step)]
    ppermute x8 -> x12, waiting for transfers between devices: 0.02 us -> 13.5 us  [swap(): return lax.ppermute(value, axis, [(0, 1), (1, 0)])]
  transfers between devices with their start and end apart: 51 -> 45, of which waited for: 17 -> 18; matrix products, arithmetic and copies ran while one was open for 12% -> 12% of each run, Pallas kernels for 25% -> 29%
where the time goes in v2:
time: 458 us; the launch traced here: 457 us
  waiting for transfers between devices  171 us (37%)
  Pallas kernels  132 us (29%)
  starting transfers between devices  71.9 us (16%)
  other arithmetic  37.2 us (8%)
  local copies, waits for them, and re-layouts  21.5 us (5%)
  between operations  14.3 us (3%)
  matrix products  8.69 us (2%)
    all_gather x3, waiting for transfers between devices, body(): lax.all_gather(owned[:, start:stop], 'z', axis=0, tiled=False)  121 us
    pallas_call x3, Pallas kernels, update(): pl.pallas_call(functools.partial(update_kernel, first), out_shape=[jax.Sh...  113 us
    ppermute x18, starting transfers between devices, hop(): return lax.ppermute(value, 'z', route)  43.7 us
    ppermute x18, waiting for transfers between devices, hop(): return lax.ppermute(value, 'z', route)  19 us
    pallas_call x1, Pallas kernels, weights(): pl.pallas_call(functools.partial(weights_kernel, len(blocks)), out_shape=...  18.9 us
    ppermute x12, waiting for transfers between devices, swap(): return lax.ppermute(value, axis, [(0, 1), (1, 0)])  13.5 us
    add x6, other arithmetic, scatter_sum(): right = hop(right_part if right is None else right_part + right, 1, step)  11.8 us
    ppermute x8, starting transfers between devices, shift(): lax.ppermute(value, axis, [(at, (at + step) % count) for at in range(coun...  11.2 us
  transfers between devices with their start and end apart: 45, of which 18 were waited for; matrix products, arithmetic and copies ran while one was open for 12% of the time, Pallas kernels for 29%

profile of v2, /device:TPU:0, one launch (start us, length us, event | category | flops | bytes accessed | tf_op | source)
XLA Modules:
  0.0 456.7 jit_solution(13122715085732877985)
XLA Ops:
  10.6 3.0 collective-permute-start.1
  16.3 77.4 %all-gather.11.cloned.1.call-done = f32[32,256,128]{2,1,0:T(8,128)} async-done(((f32[8,256,128]{2,1,0:T(8,128)}), f32[32,256,128]{2,1,0:T(8,128)}) %all-gather.11.cloned.1.call-update) | async-done | bytes 4194320 | tf_op jit(solution)/shard_map/all_gather | solution.py:228
  93.7 5.0 %gather_fusion = f32[8,128,1024]{2,1,0:T(8,128)} fusion(f32[8,128,1024]{2,1,0:T(8,128)} %bitcast.149, s32[1024]{0:T(1024)S(1)} %pad_clamp_fusion.1), kind=kCustom, calls=%fused_computation | custom fusion | bytes 8388640 | tf_op jit(solution)/shard_map/jit(_take)/gather | solution.py:241
  99.5 3.0 fusion.4
  102.6 3.8 fusion.10.refs_0_
  112.1 3.8 fusion.13.refs_1_
  116.0 2.8 fusion.5
  118.7 12.1 %all-gather.7.cloned.1.call-done = f32[32,96,128]{2,1,0:T(8,128)} async-done(((f32[8,96,128]{2,1,0:T(8,128)}), f32[32,96,128]{2,1,0:T(8,128)}) %all-gather.7.cloned.1.call-update) | async-done | bytes 1572880 | tf_op jit(solution)/shard_map/all_gather | solution.py:228
  136.1 18.9 %weights.1 = (bf16[1024,2048]{1,0:T(8,128)(2,1)}, bf16[1024,2048]{1,0:T(8,128)(2,1)}) custom-call(bf16[1024,1024]{1,0:T(8,128)(2,1)} %fusion.10.refs_0_, bf16[1024,1024]{1,0:T(8,128)(2,1)} %fusion.13.refs_1_, f32[256,2048]{1,0:T(8,128)} %refs_2_.1, f32[256,2048]{1,0:T(8,128)} %collective-permute-done.1.refs_3_, f32[256,2048]{1,0:T(8,128)} %collective-permute-done.2.refs_4_, ...), custom_call_target="tpu_custom_call" | custom-call | flops 12884901888 | bytes 16777216 | tf_op jit(solution)/shard_map/weights/pallas_call | solution.py:69
  155.0 31.7 %all-gather.9.cloned.1.call-done = f32[32,160,128]{2,1,0:T(8,128)} async-done(((f32[8,160,128]{2,1,0:T(8,128)}), f32[32,160,128]{2,1,0:T(8,128)}) %all-gather.9.cloned.1.call-update) | async-done | bytes 2621456 | tf_op jit(solution)/shard_map/all_gather | solution.py:228
  186.7 52.0 %update.3 = (f32[8,512,2048]{2,1,0:T(8,128)}, f32[8,256,128]{2,1,0:T(8,128)}, f32[4,256,512]{2,1,0:T(8,128)}, f32[4,256,512]{2,1,0:T(8,128)}) custom-call(s32[4]{0:T(128)} %pad_add_fusion.place, f32[4,8,256,128]{3,2,1,0:T(8,128)} %bitcast.164, f32[4,8,256,128]{3,2,1,0:T(8,128)} %collective-permute-done.6.beside, bf16[1024,2048]{1,0:T(8,128)(2,1)} %get-tuple-element.18.high, ...), custom_call_target="tpu_custom_call" | custom-call | flops 38654705664 | bytes 41943040 | tf_op jit(solution)/shard_map/update/pallas_call | solution.py:146
  240.8 36.1 %update.4 = (f32[8,512,2048]{2,1,0:T(8,128)}, f32[8,160,128]{2,1,0:T(8,128)}, f32[4,160,512]{2,1,0:T(8,128)}, f32[4,160,512]{2,1,0:T(8,128)}) custom-call(s32[4]{0:T(128)} %pad_add_fusion.place, f32[4,8,160,128]{3,2,1,0:T(8,128)} %bitcast.166, f32[4,8,160,128]{3,2,1,0:T(8,128)} %copy-done.8, ...), custom_call_target="tpu_custom_call", output_to_operand_aliasing={{0}: (8, {})} | custom-call | flops 24159191040 | bytes 29360128 | tf_op jit(solution)/shard_map/update/pallas_call | solution.py:146
  276.9 24.9 %update.5 = (f32[8,512,2048]{2,1,0:T(8,128)}, f32[8,96,128]{2,1,0:T(8,128)}, f32[4,96,512]{2,1,0:T(8,128)}, f32[4,96,512]{2,1,0:T(8,128)}) custom-call(s32[4]{0:T(128)} %pad_add_fusion.place, f32[4,8,96,128]{3,2,1,0:T(8,128)} %bitcast.154, f32[4,8,96,128]{3,2,1,0:T(8,128)} %collective-permute-done.beside, ...), custom_call_target="tpu_custom_call", output_to_operand_aliasing={{0}: (8, {})} | custom-call | flops 14495514624 | bytes 20971520 | tf_op jit(solution)/shard_map/update/pallas_call | solution.py:146
  337.5 5.2 %collective-permute-start.9 = (f32[256,512]{1,0:T(8,128)}, f32[256,512]{1,0:T(8,128)}, u32[]{:S(2)}, u32[]{:S(2)}) collective-permute-start(f32[256,512]{1,0:T(8,128)} %bitcast_add_fusion.2), channel_id=1, source_target_pairs={{0,2},{2,4},{1,3},{3,5},{8,10},{10,12},{9,11},{11,13},{16,18},{18,... | collective-permute-start | bytes 1572872 | tf_op jit(solution)/shard_map/ppermute | solution.py:53
  349.5 6.7 %collective-permute-done.9 = f32[256,512]{1,0:T(8,128)} collective-permute-done((f32[256,512]{1,0:T(8,128)}, f32[256,512]{1,0:T(8,128)}, u32[]{:S(2)}, u32[]{:S(2)}) %collective-permute-start.9) | collective-permute-done | bytes 524320 | tf_op jit(solution)/shard_map/ppermute | solution.py:53
  360.0 4.9 %collective-permute-start.24 = (f32[96,512]{1,0:T(8,128)}, f32[96,512]{1,0:T(8,128)}, u32[]{:S(2)}, u32[]{:S(2)}) collective-permute-start(f32[96,512]{1,0:T(8,128)} %get-tuple-element.50), channel_id=1, source_target_pairs={{0,2},{2,4},{4,6},{1,3},{3,5},{5,7},{8,10},{10,12},{12,14},{9,11},... | collective-permute-start | bytes 589832 | tf_op jit(solution)/shard_map/ppermute | solution.py:53
  368.0 5.3 %collective-permute-start.17 = (f32[160,512]{1,0:T(8,128)}, f32[160,512]{1,0:T(8,128)}, u32[]{:S(2)}, u32[]{:S(2)}) collective-permute-start(f32[160,512]{1,0:T(8,128)} %get-tuple-element.40), channel_id=1, source_target_pairs={{0,2},{2,4},{4,6},{1,3},{3,5},{5,7},{8,10},{10,12},{12,14},{9,11},... | collective-permute-start | bytes 983048 | tf_op jit(solution)/shard_map/ppermute | solution.py:53
  376.3 5.4 %collective-permute-start.10 = (f32[256,512]{1,0:T(8,128)}, f32[256,512]{1,0:T(8,128)}, u32[]{:S(2)}, u32[]{:S(2)}) collective-permute-start(f32[256,512]{1,0:T(8,128)} %get-tuple-element.36), channel_id=1, source_target_pairs={{0,2},{2,4},{4,6},{1,3},{3,5},{5,7},{8,10},{10,12},{12,14},{9,11},... | collective-permute-start | bytes 1572872 | tf_op jit(solution)/shard_map/ppermute | solution.py:53
  387.5 3.5 collective-permute-done.10
  391.1 6.8 %collective-permute-done.13 = f32[256,512]{1,0:T(8,128)} collective-permute-done((f32[256,512]{1,0:T(8,128)}, f32[256,512]{1,0:T(8,128)}, u32[]{:S(2)}, u32[]{:S(2)}) %collective-permute-start.13) | collective-permute-done | bytes 524320 | tf_op jit(solution)/shard_map/ppermute | solution.py:53
  404.4 6.6 %collective-permute-done.33 = f32[128,512]{1,0:T(8,128)S(1)} collective-permute-done((f32[128,512]{1,0:T(8,128)S(1)}, f32[128,512]{1,0:T(8,128)S(1)}, u32[]{:S(2)}, u32[]{:S(2)}) %collective-permute-start.33) | collective-permute-done | bytes 262176 | tf_op jit(solution)/shard_map/ppermute | solution.py:38
  412.4 2.8 collective-permute-start.36
  437.3 2.8 collective-permute-start.31
  442.6 5.6 %collective-permute-done.31 = f32[512,128]{1,0:T(8,128)S(1)} collective-permute-done((f32[512,128]{1,0:T(8,128)}, f32[512,128]{1,0:T(8,128)S(1)}, u32[]{:S(2)}, u32[]{:S(2)}) %collective-permute-start.31) | collective-permute-done | bytes 262176 | tf_op jit(solution)/shard_map/ppermute | solution.py:271
  (161 shorter events, 112.0 us)
Async XLA Ops:
  7.2 86.5 %all-gather.11.cloned.1.call-start = ((), (), s32[]{:S(2)}) async-start(), calls=%async_computation.2 | async-start | bytes 5242880 | tf_op jit(solution)/shard_map/all_gather | solution.py:228
  9.7 121.2 %all-gather.7.cloned.1.call-start = ((), (), s32[]{:S(2)}) async-start(), calls=%async_computation | async-start | bytes 1966080 | tf_op jit(solution)/shard_map/all_gather | solution.py:228
  10.5 176.2 %all-gather.9.cloned.1.call-start = ((), (), s32[]{:S(2)}) async-start(), calls=%async_computation.1 | async-start | bytes 3276800 | tf_op jit(solution)/shard_map/all_gather | solution.py:228
  10.6 95.8 %collective-permute-start.1 = (f32[256,2048]{1,0:T(8,128)}, f32[256,2048]{1,0:T(8,128)}, u32[]{:S(2)}, u32[]{:S(2)}) collective-permute-start(f32[256,2048]{1,0:T(8,128)} %refs_2_.1), channel_id=1, source_target_pairs={{0,8},{8,0},{1,9},{9,1},{2,10},{10,2},{3,11},{11,3},{4,12},{12,4},... | collective-permute-start | bytes 6291464 | tf_op jit(solution)/shard_map/ppermute | solution.py:38
  13.6 95.7 %collective-permute-start.2 = (f32[256,2048]{1,0:T(8,128)}, f32[256,2048]{1,0:T(8,128)}, u32[]{:S(2)}, u32[]{:S(2)}) collective-permute-start(f32[256,2048]{1,0:T(8,128)} %refs_2_.1), channel_id=1, source_target_pairs={{0,16},{16,0},{1,17},{17,1},{2,18},{18,2},{3,19},{19,3},{4,20},{20... | collective-permute-start | bytes 6291464 | tf_op jit(solution)/shard_map/ppermute | solution.py:43
  93.6 93.1 %collective-permute-start.6 = (f32[4,8,256,128]{3,2,1,0:T(8,128)}, f32[4,8,256,128]{3,2,1,0:T(8,128)}, u32[]{:S(2)}, u32[]{:S(2)}) collective-permute-start(f32[4,8,256,128]{3,2,1,0:T(8,128)} %bitcast.163), channel_id=1, source_target_pairs={{0,1},{1,0},{2,3},{3,2},{4,5},{5,4},{6,7},{7,6},{8,9},{9,8},{10,11... | collective-permute-start | bytes 12582920 | tf_op jit(solution)/shard_map/ppermute | solution.py:38
  107.7 25.6 %collective-permute-start.3 = (f32[128,2048]{1,0:T(8,128)S(1)}, f32[128,2048]{1,0:T(8,128)S(1)}, u32[]{:S(2)}, u32[]{:S(2)}) collective-permute-start(f32[128,2048]{1,0:T(8,128)S(1)} %slice.25), channel_id=1, source_target_pairs={{0,16},{16,0},{1,17},{17,1},{2,18},{18,2},{3,19},{19,3},{4,20},{20... | collective-permute-start | bytes 3145736 | tf_op jit(solution)/shard_map/ppermute | solution.py:43
  110.6 25.5 %collective-permute-start.4 = (f32[128,2048]{1,0:T(8,128)S(1)}, f32[128,2048]{1,0:T(8,128)}, u32[]{:S(2)}, u32[]{:S(2)}) collective-permute-start(f32[128,2048]{1,0:T(8,128)S(1)} %slice.26), channel_id=1, source_target_pairs={{0,8},{8,0},{1,9},{9,1},{2,10},{10,2},{3,11},{11,3},{4,12},{12,4},... | collective-permute-start | bytes 3145736 | tf_op jit(solution)/shard_map/ppermute | solution.py:38
  130.9 146.0 %collective-permute-start = (f32[4,8,96,128]{3,2,1,0:T(8,128)}, f32[4,8,96,128]{3,2,1,0:T(8,128)}, u32[]{:S(2)}, u32[]{:S(2)}) collective-permute-start(f32[4,8,96,128]{3,2,1,0:T(8,128)} %bitcast.153), channel_id=1, source_target_pairs={{0,1},{1,0},{2,3},{3,2},{4,5},{5,4},{6,7},{7,6},{8,9},{9,8},{10,11... | collective-permute-start | bytes 4718600 | tf_op jit(solution)/shard_map/ppermute | solution.py:38
  186.7 52.6 %collective-permute-start.5 = (f32[4,8,160,128]{3,2,1,0:T(8,128)}, f32[4,8,160,128]{3,2,1,0:T(8,128)S(1)}, u32[]{:S(2)}, u32[]{:S(2)}) collective-permute-start(f32[4,8,160,128]{3,2,1,0:T(8,128)} %bitcast.165), channel_id=1, source_target_pairs={{0,1},{1,0},{2,3},{3,2},{4,5},{5,4},{6,7},{7,6},{8,9},{9,8},{10,11... | collective-permute-start | bytes 7864328 | tf_op jit(solution)/shard_map/ppermute | solution.py:38
  238.8 76.5 %collective-permute-start.7 = (f32[4,256,512]{2,1,0:T(8,128)}, f32[4,256,512]{2,1,0:T(8,128)S(1)}, u32[]{:S(2)}, u32[]{:S(2)}) collective-permute-start(f32[4,256,512]{2,1,0:T(8,128)} %get-tuple-element.24), channel_id=1, source_target_pairs={{0,1},{1,0},{2,3},{3,2},{4,5},{5,4},{6,7},{7,6},{8,9},{9,8},{10,11... | collective-permute-start | bytes 6291464 | tf_op jit(solution)/shard_map/ppermute | solution.py:38
  276.9 32.3 %collective-permute-start.14 = (f32[4,160,512]{2,1,0:T(8,128)}, f32[4,160,512]{2,1,0:T(8,128)S(1)}, u32[]{:S(2)}, u32[]{:S(2)}) collective-permute-start(f32[4,160,512]{2,1,0:T(8,128)} %get-tuple-element.26), channel_id=1, source_target_pairs={{0,1},{1,0},{2,3},{3,2},{4,5},{5,4},{6,7},{7,6},{8,9},{9,8},{10,11... | collective-permute-start | bytes 3932168 | tf_op jit(solution)/shard_map/ppermute | solution.py:38
  306.9 16.3 %collective-permute-start.22 = (f32[96,512]{1,0:T(8,128)}, f32[96,512]{1,0:T(8,128)}, u32[]{:S(2)}, u32[]{:S(2)}) collective-permute-start(f32[96,512]{1,0:T(8,128)} %get-tuple-element.52), channel_id=1, source_target_pairs={{0,2},{1,3},{8,10},{9,11},{16,18},{17,19},{24,26},{25,27}} | collective-permute-start | bytes 589832 | tf_op jit(solution)/shard_map/ppermute | solution.py:53
  321.9 15.7 %collective-permute-start.25 = (f32[96,512]{1,0:T(8,128)}, f32[96,512]{1,0:T(8,128)}, u32[]{:S(2)}, u32[]{:S(2)}) collective-permute-start(f32[96,512]{1,0:T(8,128)} %get-tuple-element.53), channel_id=1, source_target_pairs={{6,4},{7,5},{14,12},{15,13},{22,20},{23,21},{30,28},{31,29}} | collective-permute-start | bytes 589832 | tf_op jit(solution)/shard_map/ppermute | solution.py:53
  324.9 17.8 %collective-permute-start.23 = (f32[96,512]{1,0:T(8,128)}, f32[96,512]{1,0:T(8,128)}, u32[]{:S(2)}, u32[]{:S(2)}) collective-permute-start(f32[96,512]{1,0:T(8,128)} %bitcast_add_fusion.12), channel_id=1, source_target_pairs={{0,2},{2,4},{1,3},{3,5},{8,10},{10,12},{9,11},{11,13},{16,18},{18,... | collective-permute-start | bytes 589832 | tf_op jit(solution)/shard_map/ppermute | solution.py:53
  326.9 19.2 %collective-permute-start.18 = (f32[160,512]{1,0:T(8,128)}, f32[160,512]{1,0:T(8,128)}, u32[]{:S(2)}, u32[]{:S(2)}) collective-permute-start(f32[160,512]{1,0:T(8,128)} %get-tuple-element.43), channel_id=1, source_target_pairs={{6,4},{7,5},{14,12},{15,13},{22,20},{23,21},{30,28},{31,29}} | collective-permute-start | bytes 983048 | tf_op jit(solution)/shard_map/ppermute | solution.py:53
  330.0 16.1 %collective-permute-start.16 = (f32[160,512]{1,0:T(8,128)}, f32[160,512]{1,0:T(8,128)}, u32[]{:S(2)}, u32[]{:S(2)}) collective-permute-start(f32[160,512]{1,0:T(8,128)} %bitcast_add_fusion.7), channel_id=1, source_target_pairs={{0,2},{2,4},{1,3},{3,5},{8,10},{10,12},{9,11},{11,13},{16,18},{18,... | collective-permute-start | bytes 983048 | tf_op jit(solution)/shard_map/ppermute | solution.py:53
  337.5 18.6 %collective-permute-start.9 = (f32[256,512]{1,0:T(8,128)}, f32[256,512]{1,0:T(8,128)}, u32[]{:S(2)}, u32[]{:S(2)}) collective-permute-start(f32[256,512]{1,0:T(8,128)} %bitcast_add_fusion.2), channel_id=1, source_target_pairs={{0,2},{2,4},{1,3},{3,5},{8,10},{10,12},{9,11},{11,13},{16,18},{18,... | collective-permute-start | bytes 1572872 | tf_op jit(solution)/shard_map/ppermute | solution.py:53
  344.8 20.2 %collective-permute-start.26 = (f32[96,512]{1,0:T(8,128)}, f32[96,512]{1,0:T(8,128)}, u32[]{:S(2)}, u32[]{:S(2)}) collective-permute-start(f32[96,512]{1,0:T(8,128)} %get-tuple-element.51), channel_id=1, source_target_pairs={{4,2},{6,4},{5,3},{7,5},{12,10},{14,12},{13,11},{15,13},{20,18},{2... | collective-permute-start | bytes 589832 | tf_op jit(solution)/shard_map/ppermute | solution.py:53
  348.1 25.1 %collective-permute-start.19 = (f32[160,512]{1,0:T(8,128)}, f32[160,512]{1,0:T(8,128)}, u32[]{:S(2)}, u32[]{:S(2)}) collective-permute-start(f32[160,512]{1,0:T(8,128)} %get-tuple-element.41), channel_id=1, source_target_pairs={{4,2},{6,4},{5,3},{7,5},{12,10},{14,12},{13,11},{15,13},{20,18},{2... | collective-permute-start | bytes 983048 | tf_op jit(solution)/shard_map/ppermute | solution.py:53
  358.6 17.7 %collective-permute-start.12 = (f32[256,512]{1,0:T(8,128)}, f32[256,512]{1,0:T(8,128)}, u32[]{:S(2)}, u32[]{:S(2)}) collective-permute-start(f32[256,512]{1,0:T(8,128)} %get-tuple-element.37), channel_id=1, source_target_pairs={{4,2},{6,4},{5,3},{7,5},{12,10},{14,12},{13,11},{15,13},{20,18},{2... | collective-permute-start | bytes 1572872 | tf_op jit(solution)/shard_map/ppermute | solution.py:53
  360.0 23.6 %collective-permute-start.24 = (f32[96,512]{1,0:T(8,128)}, f32[96,512]{1,0:T(8,128)}, u32[]{:S(2)}, u32[]{:S(2)}) collective-permute-start(f32[96,512]{1,0:T(8,128)} %get-tuple-element.50), channel_id=1, source_target_pairs={{0,2},{2,4},{4,6},{1,3},{3,5},{5,7},{8,10},{10,12},{12,14},{9,11},... | collective-permute-start | bytes 589832 | tf_op jit(solution)/shard_map/ppermute | solution.py:53
  366.7 18.5 %collective-permute-start.27 = (f32[96,512]{1,0:T(8,128)}, f32[96,512]{1,0:T(8,128)}, u32[]{:S(2)}, u32[]{:S(2)}) collective-permute-start(f32[96,512]{1,0:T(8,128)} %bitcast_add_fusion.11), channel_id=1, source_target_pairs={{2,0},{4,2},{6,4},{3,1},{5,3},{7,5},{10,8},{12,10},{14,12},{11,9},... | collective-permute-start | bytes 589832 | tf_op jit(solution)/shard_map/ppermute | solution.py:53
  368.0 18.4 %collective-permute-start.17 = (f32[160,512]{1,0:T(8,128)}, f32[160,512]{1,0:T(8,128)}, u32[]{:S(2)}, u32[]{:S(2)}) collective-permute-start(f32[160,512]{1,0:T(8,128)} %get-tuple-element.40), channel_id=1, source_target_pairs={{0,2},{2,4},{4,6},{1,3},{3,5},{5,7},{8,10},{10,12},{12,14},{9,11},... | collective-permute-start | bytes 983048 | tf_op jit(solution)/shard_map/ppermute | solution.py:53
  (32 other events, 228.1 us)
Sparse Core Ops, SparseCore 0:
  10.2 83.4 all-gather.10
  95.2 35.6 all-gather.6
  133.0 53.6 all-gather.8

commit v3 on v1

v3 whole, which is shorter than its diff:
```python
import functools

import jax
import jax.numpy as jnp
from jax import lax
from jax.experimental import pallas as pl
from jax.experimental.pallas import tpu as pltpu
from jax.sharding import Mesh, PartitionSpec as P

LEAF = 128
CHUNKS = 4
VMEM = 56 * 1024 * 1024
F32 = jnp.float32
BF16 = jnp.bfloat16
ALL = ("hi", "lo", "z", "core")


def split(value):
    high = value.astype(BF16)
    return high, (value - high.astype(F32)).astype(BF16)


def split_outside(value):
    high = lax.reduce_precision(value, exponent_bits=8, mantissa_bits=7)
    return high.astype(BF16), (value - high).astype(BF16)


def triple(left_high, left_low, right_high, right_low):
    dot = functools.partial(jnp.dot, preferred_element_type=F32)
    return dot(left_high, right_high) + (dot(left_high, right_low) + dot(left_low, right_high))


def high_dot(left, right, dims=(((1,), (0,)), ((), ()))):
    return lax.dot_general(left, right, dims, precision=lax.Precision.HIGH, preferred_element_type=F32)


def swap(value, axis):
    return lax.ppermute(value, axis, [(0, 1), (1, 0)])


def shift(value, axis, step):
    count = lax.axis_size(axis)
    return lax.ppermute(value, axis, [(at, (at + step) % count) for at in range(count)])


def after(value, *others):
    return lax.optimization_barrier((value, others))[0]


def hop(value, step, count=None):
    chips = lax.axis_size("z")
    count = chips - 1 if count is None else count
    if step > 0:
        route = [(at, at + 1) for at in range(count)]
    else:
        route = [(at, at - 1) for at in range(chips - count, chips)]
    return lax.ppermute(value, "z", route)


def samples_kernel(base, place, front, test_high, test_low, *refs):
    out = refs[-1]
    rows, width = front.shape
    first_row = place[1] + (2 * (pl.program_id(0) + base) + place[0]) * (rows // LEAF)
    row_leaf = first_row + lax.broadcasted_iota(jnp.int32, (rows, 1), 0) // LEAF
    step = min(width, 512)
    sums = jnp.zeros(out.shape, F32)
    for at in range(0, width, step):
        part = slice(at, at + step)
        col_leaf = place[2] + at // LEAF + lax.broadcasted_iota(jnp.int32, (1, step), 1) // LEAF
        high, low = split(jnp.where(row_leaf == col_leaf, 0.0, front[:, part]))
        sums = sums + jnp.dot(high, test_high[part], preferred_element_type=F32)
        sums = sums + jnp.dot(high, test_low[part], preferred_element_type=F32)
        sums = sums + jnp.dot(low, test_high[part], preferred_element_type=F32)
    out[...] = sums


def samples_part(front, test, place, rows, base, tiles, total, previous):
    height, width = front.shape
    samples = test[0].shape[1]
    whole = pl.BlockSpec((width, samples), lambda s, place: (0, 0), pipeline_mode=pl.Buffered(1))
    operands = [place, front, *test]
    specs = [pl.BlockSpec((rows, width), lambda s, place: (2 * (s + base) + place[0], 0)), whole, whole]
    aliases = {}
    if previous is not None:
        aliases = {len(operands): 0}
        operands.append(previous)
        specs.append(pl.BlockSpec(memory_space=pl.ANY))
    return pl.pallas_call(
        functools.partial(samples_kernel, base),
        out_shape=jax.ShapeDtypeStruct((total * rows, samples), F32),
        grid_spec=pltpu.PrefetchScalarGridSpec(
            num_scalar_prefetch=1,
            grid=(tiles,),
            in_specs=specs,
            out_specs=pl.BlockSpec((rows, samples), lambda s, place: (s + base, 0)),
        ),
        input_output_aliases=aliases,
        compiler_params=pltpu.CompilerParams(vmem_limit_bytes=VMEM),
        cost_estimate=pl.CostEstimate(
            flops=6 * tiles * rows * width * samples, bytes_accessed=tiles * rows * width * 4, transcendentals=0
        ),
        name="samples",
    )(*operands)


def weights_kernel(parts, *refs):
    left_high, left_low = refs[0], refs[1]
    rows = jnp.concatenate([ref[...] for ref in refs[2 : 2 + parts]], axis=0)
    high, low = split(rows)
    out_high, out_low = refs[2 + parts :]
    out_high[...], out_low[...] = split(triple(left_high[...], left_low[...], high, low))


def weights(left_high, left_low, blocks):
    panel = left_high.shape[0]
    width = blocks[0].shape[1]
    tile = min(width, 512)
    whole = pl.BlockSpec((panel, panel), lambda n: (0, 0), pipeline_mode=pl.Buffered(1))
    return pl.pallas_call(
        functools.partial(weights_kernel, len(blocks)),
        out_shape=[jax.ShapeDtypeStruct((panel, width), BF16)] * 2,
        grid=(width // tile,),
        in_specs=[whole, whole] + [pl.BlockSpec((b.shape[0], tile), lambda n: (0, n)) for b in blocks],
        out_specs=[pl.BlockSpec((panel, tile), lambda n: (0, n))] * 2,
        compiler_params=pltpu.CompilerParams(vmem_limit_bytes=VMEM),
        cost_estimate=pl.CostEstimate(flops=6 * panel * panel * width, bytes_accessed=panel * width * 8, transcendentals=0),
        name="weights",
    )(left_high, left_low, *blocks)


def update_kernel(first, place, own, beside, mine, other, high_all, low_all, front, *refs):
    out, leaves, high, low, sems = refs[-5:]
    rows, width = out.shape
    step = min(width, 512)
    begin = pl.program_id(0) == 0

    def fetches(at):
        part = slice(at, at + step)
        return [
            pltpu.make_async_copy(source.at[:, part], target.at[:, part], sems.at[which, at // step])
            for which, (source, target) in enumerate([(high_all, high), (low_all, low)])
        ]

    @pl.when(begin)
    def _():
        for at in range(0, width, step):
            for fetch in fetches(at):
                fetch.start()

    left_high, left_low = split(jnp.concatenate([own[...], beside[...], mine[...], other[...]], axis=1))
    for at in range(0, width, step):

        @pl.when(begin)
        def _():
            for fetch in fetches(at):
                fetch.wait()

        part = slice(at, at + step)
        value = jnp.dot(left_high, high[:, part], preferred_element_type=F32)
        value = value + jnp.dot(left_high, low[:, part], preferred_element_type=F32)
        value = value + jnp.dot(left_low, high[:, part], preferred_element_type=F32)
        out[:, part] = front[:, part] - value
    leaf = place[1] - place[2] + first + pl.program_id(0) * (rows // LEAF)
    for at in range(rows // LEAF):
        column = jnp.clip(leaf + at, 0, width // LEAF - 1) * LEAF
        piece = pl.ds(at * LEAF, LEAF)
        leaves[piece, :] = out[piece, pl.ds(pl.multiple_of(column, LEAF), LEAF)]


def update(place, own, beside, mine, other, weight, front, schur, start):
    height, width = front.shape
    panel = weight[0].shape[0]
    rows = mine.shape[0]
    tile = 512 if rows % 512 == 0 else LEAF
    base = start // tile
    slot = own.shape[1]
    far = mine.shape[1]
    anywhere = pl.BlockSpec(memory_space=pl.ANY)
    operands = [place, own, beside, mine, other, *weight, front]
    specs = [
        pl.BlockSpec((tile, slot), lambda i, place: (base + i, 0)),
        pl.BlockSpec((tile, slot), lambda i, place: (base + i, 0)),
        pl.BlockSpec((tile, far), lambda i, place: (i, 0)),
        pl.BlockSpec((tile, far), lambda i, place: (i, 0)),
        anywhere,
        anywhere,
        pl.BlockSpec((tile, width), lambda i, place: (base + i, 0)),
    ]
    aliases = {}
    if schur is not None:
        aliases = {len(operands): 0}
        operands.append(schur)
        specs.append(anywhere)
    return pl.pallas_call(
        functools.partial(update_kernel, start // LEAF),
        out_shape=[jax.ShapeDtypeStruct((height, width), F32), jax.ShapeDtypeStruct((rows, LEAF), F32)],
        grid_spec=pltpu.PrefetchScalarGridSpec(
            num_scalar_prefetch=1,
            grid=(rows // tile,),
            in_specs=specs,
            out_specs=[
                pl.BlockSpec((tile, width), lambda i, place: (base + i, 0)),
                pl.BlockSpec((tile, LEAF), lambda i, place: (i, 0)),
            ],
            scratch_shapes=[
                pltpu.VMEM((panel, width), BF16),
                pltpu.VMEM((panel, width), BF16),
                pltpu.SemaphoreType.DMA((2, width // min(width, 512))),
            ],
        ),
        input_output_aliases=aliases,
        compiler_params=pltpu.CompilerParams(vmem_limit_bytes=VMEM),
        cost_estimate=pl.CostEstimate(
            flops=6 * rows * panel * width, bytes_accessed=rows * width * 8 + panel * width * 4, transcendentals=0
        ),
        name="update",
    )(*operands)


def halve(value, axis):
    half = value.shape[0] // 2
    at = lax.axis_index(axis)
    mine = lax.dynamic_slice_in_dim(value, at * half, half, 0)
    return mine + swap(lax.dynamic_slice_in_dim(value, (1 - at) * half, half, 0), axis)


def double(value, axis):
    other = swap(value, axis)
    first = lax.axis_index(axis) == 0
    return jnp.concatenate([jnp.where(first, value, other), jnp.where(first, other, value)], axis=0)


def group_sum(gram):
    chips, z = lax.axis_size("z"), lax.axis_index("z")
    value = halve(halve(gram, "core"), "lo")
    parts = value.reshape(chips, value.shape[0] // chips, value.shape[1])
    total = lax.dynamic_index_in_dim(parts, z, 0, keepdims=False)
    for step in range(1, chips):
        part = lax.dynamic_index_in_dim(parts, (z + step) % chips, 0, keepdims=False)
        total = total + shift(part, "z", step)
    parts = jnp.stack([total] + [shift(total, "z", step) for step in range(1, chips)])
    value = jnp.take(parts, (z - jnp.arange(chips)) % chips, axis=0).reshape(value.shape)
    return double(double(value, "lo"), "core")


def spread_test(test_matrix, rows):
    row_count, chips = 2 * lax.axis_size("hi"), lax.axis_size("z")
    row, z, core = lax.axis_index("hi") * 2 + lax.axis_index("lo"), lax.axis_index("z"), lax.axis_index("core")
    piece = 2 * rows // row_count
    half = chips // 2
    received = []
    for turn in range(half):
        route = [
            (2 * at + h, 2 * (h * half + (at + turn) % half) + at // half) for at in range(chips) for h in range(2)
        ]
        start = (z + turn) % half * 2 * rows + row * piece
        part = lax.dynamic_slice_in_dim(test_matrix, start, piece, 0)
        received.append(lax.ppermute(part, ("z", "core"), route))
    stacked = jnp.stack(received)
    parts = []
    for turn in range(half):
        route = []
        for k in range(row_count):
            for at in range(chips):
                for e in range(2):
                    target = e * half + (turn + k) % half
                    route.append(((k * chips + at) * 2 + e, (target * chips + at) * 2 + k // half))
        which = (z - turn - row) % half
        parts.append(lax.ppermute(lax.dynamic_index_in_dim(stacked, which, 0, keepdims=False), ALL, route))
    parts = jnp.stack(parts)
    order = (row - jnp.arange(half)) % half
    return jnp.take(parts, order, axis=0).reshape(half * piece, -1)


def body(front_trailing, panel_columns, panel_rows, pivots, diag_inverse, test_matrix):
    hi_count, z_count = lax.axis_size("hi"), lax.axis_size("z")
    row_count, col_count = 2 * hi_count, 2 * z_count
    hi, lo, z, core = [lax.axis_index(name) for name in ALL]
    row, col = hi * 2 + lo, z * 2 + core
    height, width = front_trailing.shape
    depth, slot = panel_rows.shape[0], panel_columns.shape[1]
    panel = depth * row_count
    samples = test_matrix.shape[1]
    per = height // col_count
    ratio = col_count // row_count
    targets = col_count // ratio
    chunk = height // CHUNKS
    starts = list(range(0, height, chunk))
    leaf_count = per // LEAF
    row_leaf, col_leaf = row * (height // LEAF), col * (width // LEAF)

    levels = []
    for pair in range(0, CHUNKS, 2):
        first = [(pair, h) for h in range(1, z_count)]
        second = [(pair + 1, h) for h in range(1, z_count)]
        levels += [level for both in zip(first, second) for level in both]
    if CHUNKS == 4 and z_count == 4:
        levels = [(0, 1), (1, 1), (0, 2), (1, 2), (0, 3), (2, 1), (1, 3), (2, 2), (3, 1), (2, 3), (3, 2), (3, 3)]
    carried = {(j, 0): (panel_columns[at : at + chunk],) * 2 for j, at in enumerate(starts)}

    def send(index, *others):
        if index < len(levels):
            j, h = levels[index]
            right, left = after(carried[j, h - 1], *others)
            carried[j, h] = (hop(right, 1), hop(left, -1))

    def arrived(index):
        return carried[levels[index]] if index < len(levels) else ()

    def whole_chunk(j):
        parts = [
            jnp.where(z >= at, carried[j, at][0], carried[j, z_count - at][1]) for at in range(1, z_count)
        ]
        return jnp.concatenate(parts, axis=1)

    test = split_outside(test_matrix)
    send(0)
    send(1)
    beside = swap(panel_columns, "core")
    over_lo = swap(panel_rows, "lo")
    over_hi = [shift(panel_rows, "hi", step) for step in range(1, hi_count)]
    inner = lax.psum(high_dot(panel_rows, test_matrix), ("z", "core"))
    inner = lax.all_gather(inner, ("hi", "lo"), axis=0, tiled=False)

    token = ()
    halves = []
    at_level = 1
    for part in range(2):
        place = jnp.stack([(1 - core) if part == 0 else core, row_leaf, col_leaf])
        done = None
        for base, count in [(0, z_count // 2), (z_count // 2, z_count - z_count // 2)]:
            if part or base:
                send(at_level + 1, token, *arrived(at_level - 1))
                place = after(place, *arrived(at_level - 1))
                at_level += 1
            done = samples_part(front_trailing, test, place, per, base, count, z_count, done)
            token = done
        halves.append(done)
    sent, kept = swap(halves[0], "core"), halves[1]

    blocks, owners = [panel_rows, over_lo], [row, row ^ 1]
    for step, block in enumerate(over_hi, 1):
        far_hi = (hi - step) % hi_count
        blocks += [block, shift(over_lo[: depth // 2], "hi", step), swap(block[depth // 2 :], "lo")]
        owners += [far_hi * 2 + lo, far_hi * 2 + (1 - lo)]
    chips = [(z - at) % z_count for at in range(z_count)]
    order = [2 * chips[0] + core, 2 * chips[0] + 1 - core]
    order += [2 * chip + core for chip in chips[1:]] + [2 * chip + 1 - core for chip in chips[1:]]
    send(at_level + 1, token, *arrived(at_level - 1))
    inverse = after(diag_inverse.reshape(col_count, slot, panel), *arrived(at_level - 1))
    at_level += 1
    left = jnp.concatenate([lax.dynamic_index_in_dim(inverse, at, 0, keepdims=False) for at in order], axis=0)
    position = (jnp.stack(owners)[:, None] * depth + jnp.arange(depth, dtype=jnp.int32)[None, :]).reshape(panel)
    chosen = (pivots[:, None] == position[None, :]).astype(BF16)
    left_high, left_low = [
        jnp.dot(part, chosen, preferred_element_type=F32).astype(BF16) for part in split_outside(left)
    ]

    partial = (kept + sent).reshape(z_count, per, samples)
    right = left = None
    for step in range(1, z_count):
        right_part = lax.dynamic_index_in_dim(partial, jnp.minimum(z + z_count - step, z_count - 1), 0, keepdims=False)
        left_part = lax.dynamic_index_in_dim(partial, jnp.maximum(z - z_count + step, 0), 0, keepdims=False)
        right = hop(right_part if right is None else right_part + right, 1, step)
        left = hop(left_part if left is None else left_part + left, -1, step)
    sums = lax.dynamic_index_in_dim(partial, z, 0, keepdims=False) + right + left

    send(at_level + 1, left_high, *arrived(at_level - 1))
    left_high = after(left_high, *arrived(at_level - 1))
    at_level += 1
    weight = weights(left_high, left_low, blocks)

    half = col % ratio
    routes = [
        [(r * col_count + ratio * r + h, r * col_count + h * targets + m) for r in range(row_count) for h in range(ratio)]
        for m in range(targets)
    ]

    def to_owners(pieces):
        return sum(lax.ppermute(piece, ALL, route) for piece, route in zip(pieces, routes))

    def front_leaf(at):
        return lax.dynamic_slice(front_trailing, (half * width + at * LEAF, at * LEAF), (LEAF, LEAF))

    own_test = spread_test(after(test_matrix, left_low), per)
    own_front = to_owners(
        [
            after(jnp.concatenate([front_leaf(m * leaf_count + at) for at in range(leaf_count)], axis=0), left_low)
            for m in range(targets)
        ]
    )

    place = jnp.stack([core, row_leaf, col_leaf])
    schur, leaves, far = None, [], []
    token = weight[0]
    at_level -= 1
    for j, start in enumerate(starts):
        waited = [arrived(at_level), arrived(at_level + 1)]
        send(at_level + 2, token, *waited)
        send(at_level + 3, token, *waited)
        while (j, z_count - 1) not in carried or at_level + 4 < len(levels) and j == CHUNKS - 1:
            at_level += 2
            waited = [arrived(at_level), arrived(at_level + 1)]
            send(at_level + 2, token, *waited)
            send(at_level + 3, token, *waited)
        at_level += 2
        mine = whole_chunk(j)
        other = swap(mine, "core")
        far.append((mine, other))
        schur, leaf = update(after(place, *waited), panel_columns, beside, mine, other, weight, front_trailing, schur, start)
        token = leaf
        leaves.append(leaf)

    inner = jnp.concatenate([lax.dynamic_index_in_dim(inner, at, 0, keepdims=False) for at in owners], axis=0).reshape(panel, samples)
    middle = triple(left_high, left_low, *split_outside(inner))
    each = col_count // CHUNKS
    own_rows = [lax.dynamic_slice_in_dim(part, col * per, per, 0) for part in (panel_columns, beside)]
    for which in range(2):
        chosen_rows = 0.0
        for j in range(CHUNKS):
            rows = lax.dynamic_slice_in_dim(far[j][which], col % each * per, per, 0)
            chosen_rows = jnp.where(col // each == j, rows, chosen_rows)
        own_rows.append(chosen_rows)
    sums = sums - high_dot(jnp.concatenate(own_rows, axis=1), middle)

    def leaf_rows(start):
        return leaves[start // chunk][start % chunk : start % chunk + per]

    late = []
    for m in range(targets):
        piece = leaf_rows(m * per)
        for h in range(1, ratio):
            piece = jnp.where(half == h, leaf_rows(h * width + m * per), piece)
        late.append(piece)
    leaf_blocks = to_owners(late)
    change = (own_front - leaf_blocks).reshape(leaf_count, LEAF, LEAF)
    change = high_dot(change, own_test.reshape(leaf_count, LEAF, samples), (((2,), (1,)), ((0,), (0,))))
    off_samples = sums + change.reshape(per, samples)
    gram = high_dot(off_samples, off_samples, (((0,), (0,)), ((), ())))
    group_gram = (group_sum(gram) / (2 * height))[None]
    return (schur, off_samples, leaf_blocks, group_gram)


def solution(mesh):
    rows, cols = mesh.shape["row"], mesh.shape["col"]
    fine = Mesh(mesh.devices.reshape(rows // 2, 2, cols // 2, 2), ALL)
    row, col = ("hi", "lo"), ("z", "core")
    placed = (P(row, col), P(row, col), P(row, col), P(), P(), P(col, None))
    return jax.shard_map(
        body,
        mesh=fine,
        in_specs=placed,
        out_specs=(P(row, col), P(ALL, None), P(ALL, None), P(row, None, None)),
        check_vma=False,
    )
```

time: 576 us -> 558 us (0.969)
  waiting for transfers between devices: 213 us -> 141 us
  starting transfers between devices: 119 us -> 147 us
  Pallas kernels: 141 us -> 160 us
  other arithmetic: 32.5 us -> 39.8 us
    psum x1 -> x0, waiting for transfers between devices: 96.8 us -> none  [body(): group_gram = (lax.psum(gram, ('lo', 'z', 'core')) / (2 * height))[None]]
    psum x1, waiting for transfers between devices: 0.01 us -> 32.3 us  [body(): inner = lax.psum(high_dot(panel_rows, test_matrix), ('z', 'core'))]
    ppermute x8 -> x12, starting transfers between devices: 3.28 us -> 31.9 us  [swap(): return lax.ppermute(value, axis, [(0, 1), (1, 0)])]
    ppermute x8, waiting for transfers between devices: 46.1 us -> 21.9 us  [to_owners(): lax.ppermute(piece, ALL, route)]
    ppermute x8 -> x12, waiting for transfers between devices: 0.02 us -> 19.1 us  [swap(): return lax.ppermute(value, axis, [(0, 1), (1, 0)])]
    pallas_call x4, Pallas kernels: 82.3 us -> 92.4 us  [update(): pl.pallas_call(functools.partial(update_kernel, start // LEAF), out_shape...]
    pallas_call x2 -> x4, Pallas kernels: 39.5 us -> 49 us  [samples_part(): pl.pallas_call(functools.partial(samples_kernel, base), out_shape=jax.Sha...]
    ppermute x2 -> x8, starting transfers between devices: 2.1 us -> 10.6 us  [shift(): lax.ppermute(value, axis, [(at, (at + step) % count) for at in range(coun...]
  transfers between devices with their start and end apart: 51 -> 64, of which waited for: 17 -> 21; matrix products, arithmetic and copies ran while one was open for 12% -> 14% of each run, Pallas kernels for 25% -> 29%
where the time goes in v3:
time: 558 us; the launch traced here: 549 us
  Pallas kernels  160 us (29%)
  starting transfers between devices  147 us (26%)
  waiting for transfers between devices  141 us (25%)
  other arithmetic  39.8 us (7%)
  matrix products  23.8 us (4%)
  local copies, waits for them, and re-layouts  21.3 us (4%)
  between operations  15.9 us (3%)
    pallas_call x4, Pallas kernels, update(): pl.pallas_call(functools.partial(update_kernel, start // LEAF), out_shape...  92.4 us
    ppermute x30, starting transfers between devices, hop(): return lax.ppermute(value, 'z', route)  79.4 us
    ppermute x30, waiting for transfers between devices, hop(): return lax.ppermute(value, 'z', route)  54.8 us
    pallas_call x4, Pallas kernels, samples_part(): pl.pallas_call(functools.partial(samples_kernel, base), out_shape=jax.Sha...  49 us
    psum x1, waiting for transfers between devices, body(): inner = lax.psum(high_dot(panel_rows, test_matrix), ('z', 'core'))  32.3 us
    ppermute x12, starting transfers between devices, swap(): return lax.ppermute(value, axis, [(0, 1), (1, 0)])  31.9 us
    ppermute x8, waiting for transfers between devices, to_owners(): lax.ppermute(piece, ALL, route)  21.9 us
    ppermute x8, starting transfers between devices, to_owners(): lax.ppermute(piece, ALL, route)  21.7 us
  transfers between devices with their start and end apart: 64, of which 21 were waited for; matrix products, arithmetic and copies ran while one was open for 14% of the time, Pallas kernels for 29%

profile of v3, /device:TPU:0, one launch (start us, length us, event | category | flops | bytes accessed | tf_op | source)
XLA Modules:
  0.0 548.8 jit_solution(4573836909211222313)
XLA Ops:
  10.3 5.7 %collective-permute-start.2 = (f32[1024,128]{1,0:T(8,128)}, f32[1024,128]{1,0:T(8,128)}, u32[]{:S(2)}, u32[]{:S(2)}) collective-permute-start(f32[1024,128]{1,0:T(8,128)} %get-tuple-element.55), channel_id=1, source_target_pairs={{0,2},{2,4},{4,6},{1,3},{3,5},{5,7},{8,10},{10,12},{12,14},{9,11},... | collective-permute-start | bytes 1572872 | tf_op jit(solution)/shard_map/ppermute | solution.py:57
  29.5 5.0 fusion.4
  36.0 12.2 %samples.4.refs_0_ = f32[2048,512]{1,0:T(8,128)} custom-call(s32[3]{0:T(128)} %add_add_fusion.2.place, f32[4096,2048]{1,0:T(8,128)} %front.15, bf16[2048,512]{1,0:T(8,128)(2,1)} %get-tuple-element.125.test_high, bf16[2048,512]{1,0:T(8,128)(2,1)} %get-tuple-element.124.test_low), custom_call_target="tpu_custom_call" | custom-call | flops 6442450944 | bytes 8388608 | tf_op jit(solution)/shard_map/samples/pallas_call | solution.py:88
  55.4 32.3 %all-reduce.2.cloned.1.call-done = f32[1,256,512]{2,1,0:T(8,128)} async-done(((f32[1,256,512]{2,1,0:T(8,128)}), f32[1,256,512]{2,1,0:T(8,128)}) %all-reduce.2.cloned.1.call-update) | async-done | bytes 524304 | tf_op jit(solution)/shard_map/psum | solution.py:322
  87.8 12.3 %samples.5 = f32[2048,512]{1,0:T(8,128)} custom-call(s32[3]{0:T(128)} %add_add_fusion.2.place, f32[4096,2048]{1,0:T(8,128)} %front.15, bf16[2048,512]{1,0:T(8,128)(2,1)} %get-tuple-element.125.test_high, bf16[2048,512]{1,0:T(8,128)(2,1)} %get-tuple-element.124.test_low, f32[2048,512]{1,0:T(8,128)} %samples.4.refs_0_), custom_call_target="tpu_custom_call", output_to_operand_aliasing={{}: (4, {})} | custom-call | flops 6442450944 | bytes 8388608 | tf_op jit(solution)/shard_map/samples/pallas_call | solution.py:88
  103.7 5.4 collective-permute-start.6
  110.5 12.2 %samples.6.refs_0_ = f32[2048,512]{1,0:T(8,128)} custom-call(s32[3]{0:T(128)} %add_add_fusion.1.place, f32[4096,2048]{1,0:T(8,128)} %front.15, bf16[2048,512]{1,0:T(8,128)(2,1)} %get-tuple-element.125.test_high, bf16[2048,512]{1,0:T(8,128)(2,1)} %get-tuple-element.124.test_low), custom_call_target="tpu_custom_call" | custom-call | flops 6442450944 | bytes 8388608 | tf_op jit(solution)/shard_map/samples/pallas_call | solution.py:88
  132.5 12.3 %samples.7 = f32[2048,512]{1,0:T(8,128)} custom-call(s32[3]{0:T(128)} %add_add_fusion.1.place, f32[4096,2048]{1,0:T(8,128)} %front.15, bf16[2048,512]{1,0:T(8,128)(2,1)} %get-tuple-element.125.test_high, bf16[2048,512]{1,0:T(8,128)(2,1)} %get-tuple-element.124.test_low, f32[2048,512]{1,0:T(8,128)} %samples.6.refs_0_), custom_call_target="tpu_custom_call", output_to_operand_aliasing={{}: (4, {})} | custom-call | flops 6442450944 | bytes 8388608 | tf_op jit(solution)/shard_map/samples/pallas_call | solution.py:88
  162.5 4.9 collective-permute-done.14
  196.0 5.6 %collective-permute-done.17 = f32[1024,128]{1,0:T(8,128)S(1)} collective-permute-done((f32[1024,128]{1,0:T(8,128)S(1)}, f32[1024,128]{1,0:T(8,128)S(1)}, u32[]{:S(2)}, u32[]{:S(2)}) %collective-permute-start.17) | collective-permute-done | bytes 524320 | tf_op jit(solution)/shard_map/ppermute | solution.py:57
  204.8 16.5 %collective-permute-start.33 = (f32[2048,512]{1,0:T(8,128)}, f32[2048,512]{1,0:T(8,128)}, u32[]{:S(2)}, u32[]{:S(2)}) collective-permute-start(f32[2048,512]{1,0:T(8,128)} %samples.5), channel_id=1, source_target_pairs={{0,1},{1,0},{2,3},{3,2},{4,5},{5,4},{6,7},{7,6},{8,9},{9,8},{10,11... | collective-permute-start | bytes 12582920 | tf_op jit(solution)/shard_map/ppermute | solution.py:38
  231.2 18.5 %weights.1 = (bf16[1024,2048]{1,0:T(8,128)(2,1)}, bf16[1024,2048]{1,0:T(8,128)(2,1)}) custom-call(bf16[1024,1024]{1,0:T(8,128)(2,1)} %fusion.22.refs_0_, bf16[1024,1024]{1,0:T(8,128)(2,1)} %fusion.25.refs_1_, f32[256,2048]{1,0:T(8,128)} %refs_2_.1, f32[256,2048]{1,0:T(8,128)} %collective-permute-done.10.refs_3_, ...), custom_call_target="tpu_custom_call" | custom-call | flops 12884901888 | bytes 16777216 | tf_op jit(solution)/shard_map/weights/pallas_call | solution.py:119
  254.1 7.0 %collective-permute-start.18 = (f32[1024,128]{1,0:T(8,128)}, f32[1024,128]{1,0:T(8,128)}, u32[]{:S(2)}, u32[]{:S(2)}) collective-permute-start(f32[1024,128]{1,0:T(8,128)} %get-tuple-element.73), channel_id=1, source_target_pairs={{0,2},{2,4},{4,6},{1,3},{3,5},{5,7},{8,10},{10,12},{12,14},{9,11},... | collective-permute-start | bytes 1572872 | tf_op jit(solution)/shard_map/ppermute | solution.py:57
  261.2 23.0 %update.4 = (f32[4096,2048]{1,0:T(8,128)}, f32[1024,128]{1,0:T(8,128)}) custom-call(s32[3]{0:T(128)} %add_add_fusion.1.place, f32[4096,128]{1,0:T(8,128)} %own.7, f32[4096,128]{1,0:T(8,128)} %collective-permute-done.20.beside, f32[1024,384]{1,0:T(8,128)} %pad_maximum_fusion.1.mine, f32[1024,384]{1,0:T(8,128)} %collective-permute-done.21.other, ...), custom_call_target="tpu_custom_call" | custom-call | flops 12884901888 | bytes 25165824 | tf_op jit(solution)/shard_map/update/pallas_call | solution.py:194
  292.6 8.9 %collective-permute-done.19 = f32[1024,128]{1,0:T(8,128)S(1)} collective-permute-done((f32[1024,128]{1,0:T(8,128)}, f32[1024,128]{1,0:T(8,128)S(1)}, u32[]{:S(2)}, u32[]{:S(2)}) %collective-permute-start.19) | collective-permute-done | bytes 524320 | tf_op jit(solution)/shard_map/ppermute | solution.py:57
  312.8 23.2 %update.5 = (f32[4096,2048]{1,0:T(8,128)}, f32[1024,128]{1,0:T(8,128)}) custom-call(s32[3]{0:T(128)} %add_add_fusion.1.place, f32[4096,128]{1,0:T(8,128)} %own.7, f32[4096,128]{1,0:T(8,128)} %collective-permute-done.20.beside, f32[1024,384]{1,0:T(8,128)} %pad_maximum_fusion.2.mine, f32[1024,384]{1,0:T(8,128)} %copy-done.10, ...), custom_call_target="tpu_custom_call", output_to_operand_aliasing={{0}: (8, {})} | custom-call | flops 12884901888 | bytes 25165824 | tf_op jit(solution)/shard_map/update/pallas_call | solution.py:194
  348.2 4.7 collective-permute-start.34
  362.4 24.2 %collective-permute-done.29 = f32[1024,128]{1,0:T(8,128)S(1)} collective-permute-done((f32[1024,128]{1,0:T(8,128)S(1)}, f32[1024,128]{1,0:T(8,128)S(1)}, u32[]{:S(2)}, u32[]{:S(2)}) %collective-permute-start.29) | collective-permute-done | bytes 524320 | tf_op jit(solution)/shard_map/ppermute | solution.py:57
  396.4 23.2 %update.6 = (f32[4096,2048]{1,0:T(8,128)}, f32[1024,128]{1,0:T(8,128)}) custom-call(s32[3]{0:T(128)} %add_add_fusion.1.place, f32[4096,128]{1,0:T(8,128)} %own.7, f32[4096,128]{1,0:T(8,128)} %collective-permute-done.20.beside, f32[1024,384]{1,0:T(8,128)} %copy-done.3, f32[1024,384]{1,0:T(8,128)} %copy-done.12, ...), custom_call_target="tpu_custom_call", output_to_operand_aliasing={{0}: (8, {})} | custom-call | flops 12884901888 | bytes 25165824 | tf_op jit(solution)/shard_map/update/pallas_call | solution.py:194
  429.4 23.0 %update.7 = (f32[4096,2048]{1,0:T(8,128)}, f32[1024,128]{1,0:T(8,128)}) custom-call(s32[3]{0:T(128)} %add_add_fusion.1.place, f32[4096,128]{1,0:T(8,128)} %own.7, f32[4096,128]{1,0:T(8,128)} %collective-permute-done.20.beside, f32[1024,384]{1,0:T(8,128)} %copy-done.5, f32[1024,384]{1,0:T(8,128)} %collective-permute-done.31.other, ...), custom_call_target="tpu_custom_call", output_to_operand_aliasing={{0}: (8, {})} | custom-call | flops 12884901888 | bytes 25165824 | tf_op jit(solution)/shard_map/update/pallas_call | solution.py:194
  469.7 16.2 %collective-permute-done.46 = f32[512,128]{1,0:T(8,128)S(1)} collective-permute-done((f32[512,128]{1,0:T(8,128)S(1)}, f32[512,128]{1,0:T(8,128)S(1)}, u32[]{:S(2)}, u32[]{:S(2)}) %collective-permute-start.46) | collective-permute-done | bytes 262176 | tf_op jit(solution)/shard_map/ppermute | solution.py:380
  485.9 5.6 %collective-permute-done.47 = f32[512,128]{1,0:T(8,128)S(1)} collective-permute-done((f32[512,128]{1,0:T(8,128)S(1)}, f32[512,128]{1,0:T(8,128)S(1)}, u32[]{:S(2)}, u32[]{:S(2)}) %collective-permute-start.47) | collective-permute-done | bytes 262176 | tf_op jit(solution)/shard_map/ppermute | solution.py:380
  503.6 8.3 %collective-permute-done.53 = f32[128,512]{1,0:T(8,128)S(1)} collective-permute-done((f32[128,512]{1,0:T(8,128)S(1)}, f32[128,512]{1,0:T(8,128)S(1)}, u32[]{:S(2)}, u32[]{:S(2)}) %collective-permute-start.53) | collective-permute-done | bytes 262176 | tf_op jit(solution)/shard_map/ppermute | solution.py:38
  530.9 7.3 %collective-permute-done.60 = f32[128,512]{1,0:T(8,128)S(1)} collective-permute-done((f32[128,512]{1,0:T(8,128)S(1)}, f32[128,512]{1,0:T(8,128)S(1)}, u32[]{:S(2)}, u32[]{:S(2)}) %collective-permute-start.60) | collective-permute-done | bytes 262176 | tf_op jit(solution)/shard_map/ppermute | solution.py:38
  (286 shorter events, 215.3 us)
Async XLA Ops:
  7.2 80.6 %all-reduce.2.cloned.1.call-start = ((), (), s32[]{:S(2)}) async-start(), calls=%async_computation | async-start | bytes 1048576 | tf_op jit(solution)/shard_map/psum | solution.py:322
  10.3 77.5 %collective-permute-start.2 = (f32[1024,128]{1,0:T(8,128)}, f32[1024,128]{1,0:T(8,128)}, u32[]{:S(2)}, u32[]{:S(2)}) collective-permute-start(f32[1024,128]{1,0:T(8,128)} %get-tuple-element.55), channel_id=1, source_target_pairs={{0,2},{2,4},{4,6},{1,3},{3,5},{5,7},{8,10},{10,12},{12,14},{9,11},... | collective-permute-start | bytes 1572872 | tf_op jit(solution)/shard_map/ppermute | solution.py:57
  16.0 71.8 %collective-permute-start.3 = (f32[1024,128]{1,0:T(8,128)}, f32[1024,128]{1,0:T(8,128)}, u32[]{:S(2)}, u32[]{:S(2)}) collective-permute-start(f32[1024,128]{1,0:T(8,128)} %get-tuple-element.55), channel_id=1, source_target_pairs={{2,0},{4,2},{6,4},{3,1},{5,3},{7,5},{10,8},{12,10},{14,12},{11,9},... | collective-permute-start | bytes 1572872 | tf_op jit(solution)/shard_map/ppermute | solution.py:57
  17.3 82.8 %collective-permute-start = (f32[1024,128]{1,0:T(8,128)}, f32[1024,128]{1,0:T(8,128)S(1)}, u32[]{:S(2)}, u32[]{:S(2)}) collective-permute-start(f32[1024,128]{1,0:T(8,128)} %get-tuple-element.53), channel_id=1, source_target_pairs={{0,2},{2,4},{4,6},{1,3},{3,5},{5,7},{8,10},{10,12},{12,14},{9,11},... | collective-permute-start | bytes 1572872 | tf_op jit(solution)/shard_map/ppermute | solution.py:57
  21.8 78.2 %collective-permute-start.1 = (f32[1024,128]{1,0:T(8,128)}, f32[1024,128]{1,0:T(8,128)S(1)}, u32[]{:S(2)}, u32[]{:S(2)}) collective-permute-start(f32[1024,128]{1,0:T(8,128)} %get-tuple-element.53), channel_id=1, source_target_pairs={{2,0},{4,2},{6,4},{3,1},{5,3},{7,5},{10,8},{12,10},{14,12},{11,9},... | collective-permute-start | bytes 1572872 | tf_op jit(solution)/shard_map/ppermute | solution.py:57
  23.1 149.8 %collective-permute-start.10 = (f32[256,2048]{1,0:T(8,128)}, f32[256,2048]{1,0:T(8,128)}, u32[]{:S(2)}, u32[]{:S(2)}) collective-permute-start(f32[256,2048]{1,0:T(8,128)} %refs_2_.1), channel_id=1, source_target_pairs={{0,8},{8,0},{1,9},{9,1},{2,10},{10,2},{3,11},{11,3},{4,12},{12,4},... | collective-permute-start | bytes 6291464 | tf_op jit(solution)/shard_map/ppermute | solution.py:38
  29.4 254.8 %all-gather.2.cloned.1.call-start = ((), (), s32[]{:S(2)}) async-start(), calls=%async_computation.1 | async-start | bytes 2621440 | tf_op jit(solution)/shard_map/all_gather | solution.py:323
  122.8 53.9 %collective-permute-start.11 = (f32[256,2048]{1,0:T(8,128)}, f32[256,2048]{1,0:T(8,128)}, u32[]{:S(2)}, u32[]{:S(2)}) collective-permute-start(f32[256,2048]{1,0:T(8,128)} %refs_2_.1), channel_id=1, source_target_pairs={{0,16},{16,0},{1,17},{17,1},{2,18},{18,2},{3,19},{19,3},{4,20},{20... | collective-permute-start | bytes 6291464 | tf_op jit(solution)/shard_map/ppermute | solution.py:43
  124.3 105.8 %collective-permute-start.20 = (f32[4096,128]{1,0:T(8,128)S(1)}, f32[4096,128]{1,0:T(8,128)}, u32[]{:S(2)}, u32[]{:S(2)}) collective-permute-start(f32[4096,128]{1,0:T(8,128)S(1)} %copy-done), channel_id=1, source_target_pairs={{0,1},{1,0},{2,3},{3,2},{4,5},{5,4},{6,7},{7,6},{8,9},{9,8},{10,11... | collective-permute-start | bytes 6291464 | tf_op jit(solution)/shard_map/ppermute | solution.py:38
  185.3 45.8 %collective-permute-start.12 = (f32[128,2048]{1,0:T(8,128)}, f32[128,2048]{1,0:T(8,128)}, u32[]{:S(2)}, u32[]{:S(2)}) collective-permute-start(f32[128,2048]{1,0:T(8,128)} %slice.60), channel_id=1, source_target_pairs={{0,16},{16,0},{1,17},{17,1},{2,18},{18,2},{3,19},{19,3},{4,20},{20... | collective-permute-start | bytes 3145736 | tf_op jit(solution)/shard_map/ppermute | solution.py:43
  189.3 41.8 %collective-permute-start.13 = (f32[128,2048]{1,0:T(8,128)}, f32[128,2048]{1,0:T(8,128)}, u32[]{:S(2)}, u32[]{:S(2)}) collective-permute-start(f32[128,2048]{1,0:T(8,128)} %slice.61), channel_id=1, source_target_pairs={{0,8},{8,0},{1,9},{9,1},{2,10},{10,2},{3,11},{11,3},{4,12},{12,4},... | collective-permute-start | bytes 3145736 | tf_op jit(solution)/shard_map/ppermute | solution.py:38
  204.8 138.8 %collective-permute-start.33 = (f32[2048,512]{1,0:T(8,128)}, f32[2048,512]{1,0:T(8,128)}, u32[]{:S(2)}, u32[]{:S(2)}) collective-permute-start(f32[2048,512]{1,0:T(8,128)} %samples.5), channel_id=1, source_target_pairs={{0,1},{1,0},{2,3},{3,2},{4,5},{5,4},{6,7},{7,6},{8,9},{9,8},{10,11... | collective-permute-start | bytes 12582920 | tf_op jit(solution)/shard_map/ppermute | solution.py:38
  230.1 81.2 %collective-permute-start.26 = (f32[1024,384]{1,0:T(8,128)}, f32[1024,384]{1,0:T(8,128)S(1)}, u32[]{:S(2)}, u32[]{:S(2)}) collective-permute-start(f32[1024,384]{1,0:T(8,128)} %pad_maximum_fusion.2.mine), channel_id=1, source_target_pairs={{0,1},{1,0},{2,3},{3,2},{4,5},{5,4},{6,7},{7,6},{8,9},{9,8},{10,11... | collective-permute-start | bytes 4718600 | tf_op jit(solution)/shard_map/ppermute | solution.py:38
  252.8 39.8 %collective-permute-start.23 = (f32[1024,128]{1,0:T(8,128)S(1)}, f32[1024,128]{1,0:T(8,128)}, u32[]{:S(2)}, u32[]{:S(2)}) collective-permute-start(f32[1024,128]{1,0:T(8,128)S(1)} %copy-done.22), channel_id=1, source_target_pairs={{2,0},{4,2},{6,4},{3,1},{5,3},{7,5},{10,8},{12,10},{14,12},{11,9},... | collective-permute-start | bytes 1572872 | tf_op jit(solution)/shard_map/ppermute | solution.py:57
  254.1 38.5 %collective-permute-start.18 = (f32[1024,128]{1,0:T(8,128)}, f32[1024,128]{1,0:T(8,128)}, u32[]{:S(2)}, u32[]{:S(2)}) collective-permute-start(f32[1024,128]{1,0:T(8,128)} %get-tuple-element.73), channel_id=1, source_target_pairs={{0,2},{2,4},{4,6},{1,3},{3,5},{5,7},{8,10},{10,12},{12,14},{9,11},... | collective-permute-start | bytes 1572872 | tf_op jit(solution)/shard_map/ppermute | solution.py:57
  336.0 118.9 %collective-permute-start.40 = (f32[512,128]{1,0:T(8,128)}, f32[512,128]{1,0:T(8,128)}, u32[]{:S(2)}, u32[]{:S(2)}) collective-permute-start(f32[512,128]{1,0:T(8,128)} %get-tuple-element.93), channel_id=1, source_target_pairs={{0,0},{1,4},{10,8},{11,12},{20,16},{21,20},{30,24},{31,28}} | collective-permute-start | bytes 786440 | tf_op jit(solution)/shard_map/ppermute | solution.py:380
  341.2 49.6 %collective-permute-start.32 = (f32[1024,384]{1,0:T(8,128)S(1)}, f32[1024,384]{1,0:T(8,128)S(1)}, u32[]{:S(2)}, u32[]{:S(2)}) collective-permute-start(f32[1024,384]{1,0:T(8,128)S(1)} %pad_maximum_fusion.4.mine), channel_id=1, source_target_pairs={{0,1},{1,0},{2,3},{3,2},{4,5},{5,4},{6,7},{7,6},{8,9},{9,8},{10,11... | collective-permute-start | bytes 4718600 | tf_op jit(solution)/shard_map/ppermute | solution.py:38
  348.2 39.8 %collective-permute-start.34 = (f32[512,512]{1,0:T(8,128)S(1)}, f32[512,512]{1,0:T(8,128)S(1)}, u32[]{:S(2)}, u32[]{:S(2)}) collective-permute-start(f32[512,512]{1,0:T(8,128)S(1)} %get-tuple-element.120), channel_id=1, source_target_pairs={{0,2},{1,3},{8,10},{9,11},{16,18},{17,19},{24,26},{25,27}} | collective-permute-start | bytes 3145736 | tf_op jit(solution)/shard_map/ppermute | solution.py:57
  358.0 98.8 %collective-permute-start.41 = (f32[512,128]{1,0:T(8,128)}, f32[512,128]{1,0:T(8,128)}, u32[]{:S(2)}, u32[]{:S(2)}) collective-permute-start(f32[512,128]{1,0:T(8,128)} %get-tuple-element.94), channel_id=1, source_target_pairs={{0,1},{1,5},{10,9},{11,13},{20,17},{21,21},{30,25},{31,29}} | collective-permute-start | bytes 786440 | tf_op jit(solution)/shard_map/ppermute | solution.py:380
  386.8 41.9 %collective-permute-start.31 = (f32[1024,384]{1,0:T(8,128)S(1)}, f32[1024,384]{1,0:T(8,128)}, u32[]{:S(2)}, u32[]{:S(2)}) collective-permute-start(f32[1024,384]{1,0:T(8,128)S(1)} %pad_maximum_fusion.3.mine), channel_id=1, source_target_pairs={{0,1},{1,0},{2,3},{3,2},{4,5},{5,4},{6,7},{7,6},{8,9},{9,8},{10,11... | collective-permute-start | bytes 4718600 | tf_op jit(solution)/shard_map/ppermute | solution.py:38
  421.5 37.7 %collective-permute-start.42 = (f32[512,128]{1,0:T(8,128)}, f32[512,128]{1,0:T(8,128)}, u32[]{:S(2)}, u32[]{:S(2)}) collective-permute-start(f32[512,128]{1,0:T(8,128)} %get-tuple-element.95), channel_id=1, source_target_pairs={{0,2},{1,6},{10,10},{11,14},{20,18},{21,22},{30,26},{31,30}} | collective-permute-start | bytes 786440 | tf_op jit(solution)/shard_map/ppermute | solution.py:380
  424.1 37.7 %collective-permute-start.43 = (f32[512,128]{1,0:T(8,128)}, f32[512,128]{1,0:T(8,128)}, u32[]{:S(2)}, u32[]{:S(2)}) collective-permute-start(f32[512,128]{1,0:T(8,128)} %get-tuple-element.96), channel_id=1, source_target_pairs={{0,3},{1,7},{10,11},{11,15},{20,19},{21,23},{30,27},{31,31}} | collective-permute-start | bytes 786440 | tf_op jit(solution)/shard_map/ppermute | solution.py:380
  454.9 39.3 %collective-permute-start.36 = (f32[512,512]{1,0:T(8,128)S(1)}, f32[512,512]{1,0:T(8,128)S(1)}, u32[]{:S(2)}, u32[]{:S(2)}) collective-permute-start(f32[512,512]{1,0:T(8,128)S(1)} %copy-done.18), channel_id=1, source_target_pairs={{0,2},{2,4},{4,6},{1,3},{3,5},{5,7},{8,10},{10,12},{12,14},{9,11},... | collective-permute-start | bytes 3145736 | tf_op jit(solution)/shard_map/ppermute | solution.py:57
  456.8 37.4 %collective-permute-start.39 = (f32[512,512]{1,0:T(8,128)S(1)}, f32[512,512]{1,0:T(8,128)S(1)}, u32[]{:S(2)}, u32[]{:S(2)}) collective-permute-start(f32[512,512]{1,0:T(8,128)S(1)} %bitcast_add_fusion.2), channel_id=1, source_target_pairs={{2,0},{4,2},{6,4},{3,1},{5,3},{7,5},{10,8},{12,10},{14,12},{11,9},... | collective-permute-start | bytes 3145736 | tf_op jit(solution)/shard_map/ppermute | solution.py:57
  (83 other events, 1239.6 us)
Sparse Core Ops, SparseCore 0:
  29.5 58.1 all-reduce.1
  89.7 34.2 all-gather.1

commit v4 on v2

v4 whole, which is shorter than its diff:
```python
import functools

import jax
import jax.numpy as jnp
from jax import lax
from jax.experimental import pallas as pl
from jax.experimental.pallas import tpu as pltpu
from jax.sharding import Mesh, PartitionSpec as P

LEAF = 128
VMEM = 56 * 1024 * 1024
F32 = jnp.float32
BF16 = jnp.bfloat16
ALL = ("hi", "lo", "z", "core")


def split(value):
    high = value.astype(BF16)
    return high, (value - high.astype(F32)).astype(BF16)


def split_outside(value):
    high = lax.reduce_precision(value, exponent_bits=8, mantissa_bits=7)
    return high.astype(BF16), (value - high).astype(BF16)


def triple(left_high, left_low, right_high, right_low):
    dot = functools.partial(jnp.dot, preferred_element_type=F32)
    return dot(left_high, right_high) + (dot(left_high, right_low) + dot(left_low, right_high))


def high_dot(left, right, dims=(((1,), (0,)), ((), ()))):
    return lax.dot_general(left, right, dims, precision=lax.Precision.HIGH, preferred_element_type=F32)


def swap(value, axis):
    return lax.ppermute(value, axis, [(0, 1), (1, 0)])


def shift(value, axis, step):
    count = lax.axis_size(axis)
    return lax.ppermute(value, axis, [(at, (at + step) % count) for at in range(count)])


def after(value, *others):
    return lax.optimization_barrier((value, others))[0]


def samples_kernel(place, front, test, out, test_high, test_low):
    step = pl.program_id(0)

    @pl.when(step == 0)
    def _():
        test_high[...], test_low[...] = split(test[...])

    rows, width = front.shape
    row_leaf = place[0] + step * (rows // LEAF) + lax.broadcasted_iota(jnp.int32, (rows, 1), 0) // LEAF
    col_leaf = place[1] + lax.broadcasted_iota(jnp.int32, (1, width), 1) // LEAF
    high, low = split(jnp.where(row_leaf == col_leaf, 0.0, front[...]))
    out[...] = triple(high, low, test_high[...], test_low[...])


def front_samples(place, front, test):
    height, width = front.shape
    samples = test.shape[1]
    rows = 512
    return pl.pallas_call(
        samples_kernel,
        out_shape=jax.ShapeDtypeStruct((height, samples), F32),
        grid_spec=pltpu.PrefetchScalarGridSpec(
            num_scalar_prefetch=1,
            grid=(height // rows,),
            in_specs=[
                pl.BlockSpec((rows, width), lambda s, place: (s, 0)),
                pl.BlockSpec((width, samples), lambda s, place: (0, 0), pipeline_mode=pl.Buffered(1)),
            ],
            out_specs=pl.BlockSpec((rows, samples), lambda s, place: (s, 0)),
            scratch_shapes=[pltpu.VMEM((width, samples), BF16)] * 2,
        ),
        compiler_params=pltpu.CompilerParams(vmem_limit_bytes=VMEM),
        cost_estimate=pl.CostEstimate(
            flops=6 * height * width * samples, bytes_accessed=height * width * 4, transcendentals=0
        ),
        name="samples",
    )(place, front, test)


def weights_kernel(parts, *refs):
    left_high, left_low, test = refs[:3]
    out_high, out_low, product_high, product_low, total = refs[3 + parts :]
    step = pl.program_id(0)
    high, low = split(jnp.concatenate([ref[...] for ref in refs[3 : 3 + parts]], axis=0))
    high, low = split(triple(left_high[...], left_low[...], high, low))
    out_high[...] = high
    out_low[...] = low
    part = triple(high, low, *split(test[...]))

    @pl.when(step == 0)
    def _():
        total[...] = part

    @pl.when(step > 0)
    def _():
        total[...] += part

    @pl.when(step == pl.num_programs(0) - 1)
    def _():
        product_high[...], product_low[...] = split(total[...])


def weights(left_high, left_low, test, blocks):
    panel = left_high.shape[0]
    width, samples = test.shape
    tile = min(width, 512)
    whole = pl.BlockSpec((panel, panel), lambda n: (0, 0), pipeline_mode=pl.Buffered(1))
    product = pl.BlockSpec((panel, samples), lambda n: (0, 0))
    return pl.pallas_call(
        functools.partial(weights_kernel, len(blocks)),
        out_shape=[jax.ShapeDtypeStruct((panel, width), BF16)] * 2 + [jax.ShapeDtypeStruct((panel, samples), BF16)] * 2,
        grid=(width // tile,),
        in_specs=[whole, whole, pl.BlockSpec((tile, samples), lambda n: (n, 0))]
        + [pl.BlockSpec((b.shape[0], tile), lambda n: (0, n)) for b in blocks],
        out_specs=[pl.BlockSpec((panel, tile), lambda n: (0, n))] * 2 + [product, product],
        scratch_shapes=[pltpu.VMEM((panel, samples), F32)],
        compiler_params=pltpu.CompilerParams(vmem_limit_bytes=VMEM),
        cost_estimate=pl.CostEstimate(
            flops=6 * panel * (panel + samples) * width, bytes_accessed=panel * width * 8, transcendentals=0
        ),
        name="weights",
    )(left_high, left_low, test, *blocks)


def terms_kernel(place, columns, partial, product_high, product_low, high, low, test, out):
    slots, rows, _ = columns.shape
    width = high.shape[1]
    left_high, left_low = split(jnp.concatenate([columns[at] for at in range(slots)], axis=1))
    out[...] = partial[...] - triple(left_high, left_low, product_high[...], product_low[...])
    leaf = place[0] - place[1] + pl.program_id(0) * (rows // LEAF)
    for at in range(rows // LEAF):

        @pl.when((leaf + at >= 0) & (leaf + at < width // LEAF))
        def _():
            piece = slice(at * LEAF, (at + 1) * LEAF)
            column = pl.multiple_of((leaf + at) * LEAF, LEAF)
            block = triple(
                left_high[piece], left_low[piece], high[:, pl.ds(column, LEAF)], low[:, pl.ds(column, LEAF)]
            )
            out[piece] += triple(*split(block), *split(test[pl.ds(column, LEAF)]))


def terms(place, columns, partial, weight, product, test):
    slots, height, slot = columns.shape
    panel, width = weight[0].shape
    samples = test.shape[1]
    tile = 512

    def whole(array):
        return pl.BlockSpec(array.shape, lambda i, place: (0, 0), pipeline_mode=pl.Buffered(1))

    return pl.pallas_call(
        terms_kernel,
        out_shape=jax.ShapeDtypeStruct(partial.shape, F32),
        grid_spec=pltpu.PrefetchScalarGridSpec(
            num_scalar_prefetch=1,
            grid=(height // tile,),
            in_specs=[
                pl.BlockSpec((slots, tile, slot), lambda i, place: (0, i, 0)),
                pl.BlockSpec((tile, samples), lambda i, place: (i, 0)),
                *map(whole, product),
                *map(whole, weight),
                whole(test),
            ],
            out_specs=pl.BlockSpec((tile, samples), lambda i, place: (i, 0)),
        ),
        compiler_params=pltpu.CompilerParams(vmem_limit_bytes=VMEM),
        cost_estimate=pl.CostEstimate(
            flops=6 * height * panel * samples, bytes_accessed=height * (panel + 2 * samples) * 4, transcendentals=0
        ),
        name="terms",
    )(place, columns, partial, *product, *weight, test)


def update_kernel(place, columns, high, low, front, out, leaves):
    slots = columns.shape[0]
    left_high, left_low = split(jnp.concatenate([columns[at] for at in range(slots)], axis=1))
    out[...] = front[...] - triple(left_high, left_low, high[...], low[...])
    rows, width = out.shape
    leaf = place[0] - place[1] + pl.program_id(0) * (rows // LEAF)
    for at in range(rows // LEAF):
        column = jnp.clip(leaf + at, 0, width // LEAF - 1) * LEAF
        piece = pl.ds(at * LEAF, LEAF)
        leaves[piece, :] = out[piece, pl.ds(pl.multiple_of(column, LEAF), LEAF)]


def update(place, columns, weight, front):
    slots, height, slot = columns.shape
    panel, width = weight[0].shape
    tile = 256
    whole = pl.BlockSpec((panel, width), lambda i, place: (0, 0), pipeline_mode=pl.Buffered(1))
    return pl.pallas_call(
        update_kernel,
        out_shape=[jax.ShapeDtypeStruct((height, width), F32), jax.ShapeDtypeStruct((height, LEAF), F32)],
        grid_spec=pltpu.PrefetchScalarGridSpec(
            num_scalar_prefetch=1,
            grid=(height // tile,),
            in_specs=[
                pl.BlockSpec((slots, tile, slot), lambda i, place: (0, i, 0)),
                whole,
                whole,
                pl.BlockSpec((tile, width), lambda i, place: (i, 0)),
            ],
            out_specs=[
                pl.BlockSpec((tile, width), lambda i, place: (i, 0)),
                pl.BlockSpec((tile, LEAF), lambda i, place: (i, 0)),
            ],
        ),
        compiler_params=pltpu.CompilerParams(vmem_limit_bytes=VMEM),
        cost_estimate=pl.CostEstimate(
            flops=6 * height * panel * width, bytes_accessed=height * width * 8 + panel * width * 4, transcendentals=0
        ),
        name="update",
    )(place, columns, *weight, front)


def halve(value, axis):
    half = value.shape[0] // 2
    at = lax.axis_index(axis)
    mine = lax.dynamic_slice_in_dim(value, at * half, half, 0)
    return mine + swap(lax.dynamic_slice_in_dim(value, (1 - at) * half, half, 0), axis)


def double(value, axis):
    other = swap(value, axis)
    first = lax.axis_index(axis) == 0
    return jnp.concatenate([jnp.where(first, value, other), jnp.where(first, other, value)], axis=0)


def group_sum(gram):
    chips, z = lax.axis_size("z"), lax.axis_index("z")
    value = halve(halve(gram, "core"), "lo")
    parts = value.reshape(chips, value.shape[0] // chips, value.shape[1])
    total = lax.dynamic_index_in_dim(parts, z, 0, keepdims=False)
    for step in range(1, chips):
        part = lax.dynamic_index_in_dim(parts, (z + step) % chips, 0, keepdims=False)
        total = total + shift(part, "z", step)
    parts = jnp.stack([total] + [shift(total, "z", step) for step in range(1, chips)])
    value = jnp.take(parts, (z - jnp.arange(chips)) % chips, axis=0).reshape(value.shape)
    return double(double(value, "lo"), "core")


def body(front_trailing, panel_columns, panel_rows, pivots, diag_inverse, test_matrix):
    hi_count, z_count = lax.axis_size("hi"), lax.axis_size("z")
    row_count, col_count = 2 * hi_count, 2 * z_count
    hi, lo, z, core = [lax.axis_index(name) for name in ALL]
    row, col = hi * 2 + lo, z * 2 + core
    height, width = front_trailing.shape
    depth = panel_rows.shape[0]
    panel = depth * row_count
    per = height // col_count
    ratio = col_count // row_count
    targets = col_count // ratio
    place = jnp.stack([row * (height // LEAF), col * (width // LEAF)])

    columns = lax.all_gather(panel_columns, ("z", "core"), axis=0, tiled=False)

    over_lo = swap(panel_rows, "lo")
    over_hi = [shift(panel_rows, "hi", step) for step in range(1, hi_count)]
    partial = front_samples(place, front_trailing, test_matrix)
    over_lo, *over_hi = after([over_lo, *over_hi], partial)
    blocks, owners = [panel_rows, over_lo], [row, row ^ 1]
    for step, block in enumerate(over_hi, 1):
        far_hi = (hi - step) % hi_count
        blocks += [block, shift(over_lo[: depth // 2], "hi", step), swap(block[depth // 2 :], "lo")]
        owners += [far_hi * 2 + lo, far_hi * 2 + (1 - lo)]

    position = (jnp.stack(owners)[:, None] * depth + jnp.arange(depth, dtype=jnp.int32)[None, :]).reshape(panel)
    chosen = (pivots[:, None] == position[None, :]).astype(BF16)
    left_high, left_low = [
        jnp.dot(part, chosen, preferred_element_type=F32).astype(BF16)
        for part in split_outside(after(diag_inverse, partial))
    ]
    high, low, *product = weights(left_high, left_low, test_matrix, blocks)

    partial = terms(place, columns, partial, (high, low), product, test_matrix)
    off_samples = lax.psum_scatter(partial, ("z", "core"), scatter_dimension=0, tiled=True)
    schur, leaves = update(after(place, partial), columns, (high, low), front_trailing)

    half = col % ratio
    leaf_blocks = 0
    for m in range(targets):
        piece = lax.dynamic_slice_in_dim(leaves, (half * targets + m) * per, per, 0)
        route = [
            (r * col_count + ratio * r + h, r * col_count + h * targets + m)
            for r in range(row_count)
            for h in range(ratio)
        ]
        leaf_blocks = leaf_blocks + lax.ppermute(piece, ALL, route)

    gram = high_dot(after(off_samples, leaf_blocks), off_samples, (((0,), (0,)), ((), ())))
    group_gram = (group_sum(gram) / (2 * height))[None]
    return (schur, off_samples, leaf_blocks, group_gram)


def solution(mesh):
    rows, cols = mesh.shape["row"], mesh.shape["col"]
    fine = Mesh(mesh.devices.reshape(rows // 2, 2, cols // 2, 2), ALL)
    row, col = ("hi", "lo"), ("z", "core")
    placed = (P(row, col), P(row, col), P(row, col), P(), P(), P(col, None))
    return jax.shard_map(
        body,
        mesh=fine,
        in_specs=placed,
        out_specs=(P(row, col), P(ALL, None), P(ALL, None), P(row, None, None)),
        check_vma=False,
    )
```

time: 458 us -> 348 us (0.76)
  starting transfers between devices: 71.9 us -> 24.5 us
  waiting for transfers between devices: 171 us -> 133 us
  other arithmetic: 37.2 us -> 3.14 us
  Pallas kernels: 132 us -> 157 us
  local copies, waits for them, and re-layouts: 21.5 us -> 4.47 us
    all_gather x3 -> x1, waiting for transfers between devices: 121 us -> 50.5 us  [body(): columns = lax.all_gather(panel_columns, ('z', 'core'), axis=0, tiled=False)]
    ppermute x22 -> x4, starting transfers between devices: 51 us -> 5.43 us  [body(): leaf_blocks = leaf_blocks + lax.ppermute(piece, ALL, route)]
    ppermute x12 -> x6, waiting for transfers between devices: 13.5 us -> 41.2 us  [swap(): return lax.ppermute(value, axis, [(0, 1), (1, 0)])]
    add x16 -> x1, other arithmetic: 27.4 us -> 0.75 us  [body(): leaf_blocks = leaf_blocks + lax.ppermute(piece, ALL, route)]
    pallas_call x3, Pallas kernels: 113 us -> 129 us  [the longest x1 62.5 us: update(): pl.pallas_call(update_kernel, out_shape=[jax.ShapeDtypeStruct((height, wi...]
    pallas_call x1, Pallas kernels: 18.9 us -> 27.5 us  [weights(): pl.pallas_call(functools.partial(weights_kernel, len(blocks)), out_shape=...]
    reduce_scatter x0 -> x1, waiting for transfers between devices: none -> 6.21 us  [body(): lax.psum_scatter(partial, ('z', 'core'), scatter_dimension=0, tiled=True)]
    convert_element_type x2 -> x0, other arithmetic: 5.83 us -> none  [split_outside(): return (high.astype(BF16), (value - high).astype(BF16))]
  transfers between devices with their start and end apart: 45 -> 20, of which waited for: 18 -> 18; matrix products, arithmetic and copies ran while one was open for 12% -> 3% of each run, Pallas kernels for 29% -> 36%
where the time goes in v4:
time: 348 us; the launch traced here: 346 us
  Pallas kernels  157 us (45%)
  waiting for transfers between devices  133 us (38%)
  starting transfers between devices  24.5 us (7%)
  between operations  14.3 us (4%)
  matrix products  10.2 us (3%)
  local copies, waits for them, and re-layouts  4.47 us (1%)
    pallas_call x1, Pallas kernels, update(): pl.pallas_call(update_kernel, out_shape=[jax.ShapeDtypeStruct((height, wi...  62.5 us
    all_gather x1, waiting for transfers between devices, body(): columns = lax.all_gather(panel_columns, ('z', 'core'), axis=0, tiled=False)  50.5 us
    ppermute x6, waiting for transfers between devices, swap(): return lax.ppermute(value, axis, [(0, 1), (1, 0)])  41.2 us
    pallas_call x1, Pallas kernels, front_samples(): pl.pallas_call(samples_kernel, out_shape=jax.ShapeDtypeStruct((height, sa...  33.4 us
    pallas_call x1, Pallas kernels, terms(): pl.pallas_call(terms_kernel, out_shape=jax.ShapeDtypeStruct(partial.shape...  33.4 us
    pallas_call x1, Pallas kernels, weights(): pl.pallas_call(functools.partial(weights_kernel, len(blocks)), out_shape=...  27.5 us
    ppermute x4, waiting for transfers between devices, body(): leaf_blocks = leaf_blocks + lax.ppermute(piece, ALL, route)  21.7 us
    ppermute x8, waiting for transfers between devices, shift(): lax.ppermute(value, axis, [(at, (at + step) % count) for at in range(coun...  12.5 us
  transfers between devices with their start and end apart: 20, of which 18 were waited for; matrix products, arithmetic and copies ran while one was open for 3% of the time, Pallas kernels for 36%

profile of v4, /device:TPU:0, one launch (start us, length us, event | category | flops | bytes accessed | tf_op | source)
XLA Modules:
  0.0 346.1 jit_solution(9831651276865643943)
XLA Ops:
  7.9 3.0 collective-permute-start
  13.3 33.4 %samples.1.partial = f32[4096,512]{1,0:T(8,128)} custom-call(s32[2]{0:T(128)} %pad_add_fusion.place, f32[4096,2048]{1,0:T(8,128)} %front.3, f32[2048,512]{1,0:T(8,128)} %test.3), custom_call_target="tpu_custom_call" | custom-call | flops 25769803776 | bytes 33554432 | tf_op jit(solution)/shard_map/samples/pallas_call | solution.py:67
  46.7 10.1 %collective-permute-done.refs_4_ = f32[256,2048]{1,0:T(8,128)S(1)} collective-permute-done((f32[256,2048]{1,0:T(8,128)}, f32[256,2048]{1,0:T(8,128)S(1)}, u32[]{:S(2)}, u32[]{:S(2)}) %collective-permute-start) | collective-permute-done | bytes 2097184 | tf_op jit(solution)/shard_map/ppermute | solution.py:37
  62.2 3.8 %fusion.10.refs_0_ = bf16[1024,1024]{1,0:T(8,128)(2,1)} fusion(s32[1024]{0:T(1024)S(1)} %bitcast.47, s32[1024]{0:T(1024)S(1)} %copy-done.4, f32[1024,1024]{1,0:T(8,128)S(1)} %copy-done.1), kind=kOutput, calls=%fused_computation.12 | convolution fusion | flops 2151677952 | bytes 6299648 | tf_op jit(solution)/shard_map/dot_general | solution.py:279
  65.9 3.8 %fusion.13.refs_1_ = bf16[1024,1024]{1,0:T(8,128)(2,1)} fusion(s32[1024]{0:T(1024)S(1)} %bitcast.48, s32[1024]{0:T(1024)S(1)} %copy-done.4, f32[1024,1024]{1,0:T(8,128)S(1)} %copy-done.1), kind=kOutput, calls=%fused_computation.13 | convolution fusion | flops 2152726528 | bytes 6299648 | tf_op jit(solution)/shard_map/dot_general | solution.py:279
  69.8 13.7 %collective-permute-done.3.refs_7_ = f32[128,2048]{1,0:T(8,128)S(1)} collective-permute-done((f32[128,2048]{1,0:T(8,128)S(1)}, f32[128,2048]{1,0:T(8,128)S(1)}, u32[]{:S(2)}, u32[]{:S(2)}) %collective-permute-start.3) | collective-permute-done | bytes 1048608 | tf_op jit(solution)/shard_map/ppermute | solution.py:37
  85.5 27.5 %weights.1 = (bf16[1024,2048]{1,0:T(8,128)(2,1)}, bf16[1024,2048]{1,0:T(8,128)(2,1)}, bf16[1024,512]{1,0:T(8,128)(2,1)}, bf16[1024,512]{1,0:T(8,128)(2,1)}) custom-call(bf16[1024,1024]{1,0:T(8,128)(2,1)} %fusion.10.refs_0_, bf16[1024,1024]{1,0:T(8,128)(2,1)} %fusion.13.refs_1_, f32[2048,512]{1,0:T(8,128)} %test.3, f32[256,2048]{1,0:T(8,128)} %refs_3_.1, ...), custom_call_target="tpu_custom_call" | custom-call | flops 19327352832 | bytes 16777216 | tf_op jit(solution)/shard_map/weights/pallas_call | solution.py:117
  113.0 50.5 %all-gather.3.cloned.1.call-done = f32[32768,128]{1,0:T(8,128)} async-done(((f32[4096,128]{1,0:T(8,128)}), f32[32768,128]{1,0:T(8,128)}) %all-gather.3.cloned.1.call-update) | async-done | bytes 16777232 | tf_op jit(solution)/shard_map/all_gather | solution.py:264
  163.4 33.4 %terms.1 = f32[4096,512]{1,0:T(8,128)} custom-call(s32[2]{0:T(128)} %pad_add_fusion.place, f32[8,4096,128]{2,1,0:T(8,128)} %bitcast.39, f32[4096,512]{1,0:T(8,128)} %samples.1.partial, bf16[1024,512]{1,0:T(8,128)(2,1)} %get-tuple-element.18.product_high, bf16[1024,512]{1,0:T(8,128)(2,1)} %get-tuple-element.19.product_low, ...), custom_call_target="tpu_custom_call" | custom-call | flops 12884901888 | bytes 33554432 | tf_op jit(solution)/shard_map/terms/pallas_call | solution.py:160
  196.9 62.5 %update.1 = (f32[4096,2048]{1,0:T(8,128)}, f32[4096,128]{1,0:T(8,128)}) custom-call(s32[2]{0:T(128)} %pad_add_fusion.place, f32[8,4096,128]{2,1,0:T(8,128)} %bitcast.40, bf16[1024,2048]{1,0:T(8,128)(2,1)} %get-tuple-element.20.high, bf16[1024,2048]{1,0:T(8,128)(2,1)} %get-tuple-element.21.low, f32[4096,2048]{1,0:T(8,128)} %front.3), custom_call_target="tpu_custom_call" | custom-call | flops 51539607552 | bytes 75497472 | tf_op jit(solution)/shard_map/update/pallas_call | solution.py:200
  260.6 2.1 collective-permute-start.5
  266.1 10.4 %collective-permute-done.7 = f32[512,128]{1,0:T(8,128)S(1)} collective-permute-done((f32[512,128]{1,0:T(8,128)S(1)}, f32[512,128]{1,0:T(8,128)S(1)}, u32[]{:S(2)}, u32[]{:S(2)}) %collective-permute-start.7) | collective-permute-done | bytes 262176 | tf_op jit(solution)/shard_map/ppermute | solution.py:297
  276.5 11.2 %collective-permute-done.6 = f32[512,128]{1,0:T(8,128)S(1)} collective-permute-done((f32[512,128]{1,0:T(8,128)S(1)}, f32[512,128]{1,0:T(8,128)S(1)}, u32[]{:S(2)}, u32[]{:S(2)}) %collective-permute-start.6) | collective-permute-done | bytes 262176 | tf_op jit(solution)/shard_map/ppermute | solution.py:297
  288.5 6.2 %reduce-scatter.2.cloned.1.call-done = f32[512,512]{1,0:T(8,128)} async-done(((f32[4096,512]{1,0:T(8,128)}), f32[512,512]{1,0:T(8,128)}) %reduce-scatter.2.cloned.1.call-update) | async-done | bytes 1048592 | tf_op jit(solution)/shard_map/reduce_scatter | solution.py:285
  294.7 2.6 fusion.23
  297.3 2.6 collective-permute-start.8
  301.9 8.3 %collective-permute-done.9 = f32[128,512]{1,0:T(8,128)S(1)} collective-permute-done((f32[128,512]{1,0:T(8,128)S(1)}, f32[128,512]{1,0:T(8,128)S(1)}, u32[]{:S(2)}, u32[]{:S(2)}) %collective-permute-start.9) | collective-permute-done | bytes 262176 | tf_op jit(solution)/shard_map/ppermute | solution.py:37
  310.4 3.8 %collective-permute-start.12 = (f32[32,512]{1,0:T(8,128)S(1)}, f32[32,512]{1,0:T(8,128)S(1)}, u32[]{:S(2)}, u32[]{:S(2)}) collective-permute-start(f32[32,512]{1,0:T(8,128)S(1)} %get-tuple-element.35), channel_id=1, source_target_pairs={{0,6},{2,0},{4,2},{6,4},{1,7},{3,1},{5,3},{7,5},{8,14},{10,8},{12,... | collective-permute-start | bytes 196616 | tf_op jit(solution)/shard_map/ppermute | solution.py:42
  314.2 1.6 collective-permute-start.11
  317.2 3.1 collective-permute-done.11
  320.3 2.5 collective-permute-start.15
  324.9 3.0 collective-permute-done.14
  330.4 5.6 %collective-permute-done.16 = f32[128,512]{1,0:T(8,128)S(1)} collective-permute-done((f32[128,512]{1,0:T(8,128)S(1)}, f32[128,512]{1,0:T(8,128)S(1)}, u32[]{:S(2)}, u32[]{:S(2)}) %collective-permute-start.16) | collective-permute-done | bytes 262176 | tf_op jit(solution)/shard_map/ppermute | solution.py:37
  336.2 1.9 collective-permute-done.17
  (61 shorter events, 25.1 us)
Async XLA Ops:
  7.2 156.3 %all-gather.3.cloned.1.call-start = ((), (), s32[]{:S(2)}) async-start(), calls=%async_computation.2 | async-start | bytes 18874368 | tf_op jit(solution)/shard_map/all_gather | solution.py:264
  7.9 286.8 %reduce-scatter.2.cloned.1.call-start = ((), (), s32[]{:S(2)}) async-start(), calls=%async_computation.1 | async-start | bytes 9437184 | tf_op jit(solution)/shard_map/reduce_scatter | solution.py:285
  7.9 48.8 %collective-permute-start = (f32[256,2048]{1,0:T(8,128)}, f32[256,2048]{1,0:T(8,128)S(1)}, u32[]{:S(2)}, u32[]{:S(2)}) collective-permute-start(f32[256,2048]{1,0:T(8,128)} %refs_3_.1), channel_id=1, source_target_pairs={{0,8},{8,0},{1,9},{9,1},{2,10},{10,2},{3,11},{11,3},{4,12},{12,4},... | collective-permute-start | bytes 6291464 | tf_op jit(solution)/shard_map/ppermute | solution.py:37
  10.9 47.4 %collective-permute-start.1 = (f32[256,2048]{1,0:T(8,128)}, f32[256,2048]{1,0:T(8,128)}, u32[]{:S(2)}, u32[]{:S(2)}) collective-permute-start(f32[256,2048]{1,0:T(8,128)} %refs_3_.1), channel_id=1, source_target_pairs={{0,16},{16,0},{1,17},{17,1},{2,18},{18,2},{3,19},{19,3},{4,20},{20... | collective-permute-start | bytes 6291464 | tf_op jit(solution)/shard_map/ppermute | solution.py:42
  13.3 48.9 %copy-start.4 = (s32[1024]{0:T(1024)S(1)}, s32[1024]{0:T(1024)}, u32[]{:S(2)}) copy-start(s32[1024]{0:T(1024)} %param.9) | copy-start | bytes 12292
  46.7 15.5 %copy-start.1 = (f32[1024,1024]{1,0:T(8,128)S(1)}, f32[1024,1024]{1,0:T(8,128)}, u32[]{:S(2)}) copy-start(f32[1024,1024]{1,0:T(8,128)} %param.10) | copy-start | bytes 12582916
  56.8 9.2 %copy-start = (f32[256,2048]{1,0:T(8,128)}, f32[256,2048]{1,0:T(8,128)S(1)}, u32[]{:S(2)}) copy-start(f32[256,2048]{1,0:T(8,128)S(1)} %collective-permute-done.refs_4_) | copy-start | bytes 6291460
  59.8 23.8 %collective-permute-start.3 = (f32[128,2048]{1,0:T(8,128)S(1)}, f32[128,2048]{1,0:T(8,128)S(1)}, u32[]{:S(2)}, u32[]{:S(2)}) collective-permute-start(f32[128,2048]{1,0:T(8,128)S(1)} %slice.7), channel_id=1, source_target_pairs={{0,8},{8,0},{1,9},{9,1},{2,10},{10,2},{3,11},{11,3},{4,12},{12,4},... | collective-permute-start | bytes 3145736 | tf_op jit(solution)/shard_map/ppermute | solution.py:37
  60.6 23.9 %collective-permute-start.2 = (f32[128,2048]{1,0:T(8,128)S(1)}, f32[128,2048]{1,0:T(8,128)S(1)}, u32[]{:S(2)}, u32[]{:S(2)}) collective-permute-start(f32[128,2048]{1,0:T(8,128)S(1)} %slice.6), channel_id=1, source_target_pairs={{0,16},{16,0},{1,17},{17,1},{2,18},{18,2},{3,19},{19,3},{4,20},{20... | collective-permute-start | bytes 3145736 | tf_op jit(solution)/shard_map/ppermute | solution.py:42
  83.5 1.0 copy-start.2
  260.6 5.5 %collective-permute-start.5 = (f32[512,128]{1,0:T(8,128)S(1)}, f32[512,128]{1,0:T(8,128)S(1)}, u32[]{:S(2)}, u32[]{:S(2)}) collective-permute-start(f32[512,128]{1,0:T(8,128)S(1)} %get-tuple-element.26), channel_id=1, source_target_pairs={{0,1},{1,5},{10,9},{11,13},{20,17},{21,21},{30,25},{31,29}} | collective-permute-start | bytes 786440 | tf_op jit(solution)/shard_map/ppermute | solution.py:297
  262.8 13.8 %collective-permute-start.7 = (f32[512,128]{1,0:T(8,128)S(1)}, f32[512,128]{1,0:T(8,128)S(1)}, u32[]{:S(2)}, u32[]{:S(2)}) collective-permute-start(f32[512,128]{1,0:T(8,128)S(1)} %get-tuple-element.27), channel_id=1, source_target_pairs={{0,3},{1,7},{10,11},{11,15},{20,19},{21,23},{30,27},{31,31}} | collective-permute-start | bytes 786440 | tf_op jit(solution)/shard_map/ppermute | solution.py:297
  264.1 23.7 %collective-permute-start.6 = (f32[512,128]{1,0:T(8,128)S(1)}, f32[512,128]{1,0:T(8,128)S(1)}, u32[]{:S(2)}, u32[]{:S(2)}) collective-permute-start(f32[512,128]{1,0:T(8,128)S(1)} %get-tuple-element.28), channel_id=1, source_target_pairs={{0,2},{1,6},{10,10},{11,14},{20,18},{21,22},{30,26},{31,30}} | collective-permute-start | bytes 786440 | tf_op jit(solution)/shard_map/ppermute | solution.py:297
  265.4 22.4 %collective-permute-start.4 = (f32[512,128]{1,0:T(8,128)S(1)}, f32[512,128]{1,0:T(8,128)S(1)}, u32[]{:S(2)}, u32[]{:S(2)}) collective-permute-start(f32[512,128]{1,0:T(8,128)S(1)} %get-tuple-element.29), channel_id=1, source_target_pairs={{0,0},{1,4},{10,8},{11,12},{20,16},{21,20},{30,24},{31,28}} | collective-permute-start | bytes 786440 | tf_op jit(solution)/shard_map/ppermute | solution.py:297
  297.3 4.1 %collective-permute-start.8 = (f32[256,512]{1,0:T(8,128)S(1)}, f32[256,512]{1,0:T(8,128)S(1)}, u32[]{:S(2)}, u32[]{:S(2)}) collective-permute-start(f32[256,512]{1,0:T(8,128)S(1)} %constant_dynamic-slice_fusion.1), channel_id=1, source_target_pairs={{0,1},{1,0},{2,3},{3,2},{4,5},{5,4},{6,7},{7,6},{8,9},{9,8},{10,11... | collective-permute-start | bytes 1572872 | tf_op jit(solution)/shard_map/ppermute | solution.py:37
  301.6 8.7 %collective-permute-start.9 = (f32[128,512]{1,0:T(8,128)S(1)}, f32[128,512]{1,0:T(8,128)S(1)}, u32[]{:S(2)}, u32[]{:S(2)}) collective-permute-start(f32[128,512]{1,0:T(8,128)S(1)} %constant_dynamic-slice_fusion), channel_id=1, source_target_pairs={{0,8},{8,0},{1,9},{9,1},{2,10},{10,2},{3,11},{11,3},{4,12},{12,4},... | collective-permute-start | bytes 786440 | tf_op jit(solution)/shard_map/ppermute | solution.py:37
  310.3 6.7 %collective-permute-start.10 = (f32[32,512]{1,0:T(8,128)S(1)}, f32[32,512]{1,0:T(8,128)S(1)}, u32[]{:S(2)}, u32[]{:S(2)}) collective-permute-start(f32[32,512]{1,0:T(8,128)S(1)} %get-tuple-element.34), channel_id=1, source_target_pairs={{0,2},{2,4},{4,6},{6,0},{1,3},{3,5},{5,7},{7,1},{8,10},{10,12},{12... | collective-permute-start | bytes 196616 | tf_op jit(solution)/shard_map/ppermute | solution.py:42
  310.4 6.9 %collective-permute-start.12 = (f32[32,512]{1,0:T(8,128)S(1)}, f32[32,512]{1,0:T(8,128)S(1)}, u32[]{:S(2)}, u32[]{:S(2)}) collective-permute-start(f32[32,512]{1,0:T(8,128)S(1)} %get-tuple-element.35), channel_id=1, source_target_pairs={{0,6},{2,0},{4,2},{6,4},{1,7},{3,1},{5,3},{7,5},{8,14},{10,8},{12,... | collective-permute-start | bytes 196616 | tf_op jit(solution)/shard_map/ppermute | solution.py:42
  314.2 6.1 %collective-permute-start.11 = (f32[32,512]{1,0:T(8,128)S(1)}, f32[32,512]{1,0:T(8,128)S(1)}, u32[]{:S(2)}, u32[]{:S(2)}) collective-permute-start(f32[32,512]{1,0:T(8,128)S(1)} %get-tuple-element.36), channel_id=1, source_target_pairs={{0,4},{2,6},{4,0},{6,2},{1,5},{3,7},{5,1},{7,3},{8,12},{10,14},{12... | collective-permute-start | bytes 196616 | tf_op jit(solution)/shard_map/ppermute | solution.py:42
  320.3 4.6 %collective-permute-start.15 = (f32[32,512]{1,0:T(8,128)S(1)}, f32[32,512]{1,0:T(8,128)S(1)}, u32[]{:S(2)}, u32[]{:S(2)}) collective-permute-start(f32[32,512]{1,0:T(8,128)S(1)} %fusion.19), channel_id=1, source_target_pairs={{0,6},{2,0},{4,2},{6,4},{1,7},{3,1},{5,3},{7,5},{8,14},{10,8},{12,... | collective-permute-start | bytes 196616 | tf_op jit(solution)/shard_map/ppermute | solution.py:42
  322.8 5.2 %collective-permute-start.14 = (f32[32,512]{1,0:T(8,128)S(1)}, f32[32,512]{1,0:T(8,128)S(1)}, u32[]{:S(2)}, u32[]{:S(2)}) collective-permute-start(f32[32,512]{1,0:T(8,128)S(1)} %fusion.19), channel_id=1, source_target_pairs={{0,4},{2,6},{4,0},{6,2},{1,5},{3,7},{5,1},{7,3},{8,12},{10,14},{12... | collective-permute-start | bytes 196616 | tf_op jit(solution)/shard_map/ppermute | solution.py:42
  322.8 6.1 %collective-permute-start.13 = (f32[32,512]{1,0:T(8,128)S(1)}, f32[32,512]{1,0:T(8,128)S(1)}, u32[]{:S(2)}, u32[]{:S(2)}) collective-permute-start(f32[32,512]{1,0:T(8,128)S(1)} %fusion.19), channel_id=1, source_target_pairs={{0,2},{2,4},{4,6},{6,0},{1,3},{3,5},{5,7},{7,1},{8,10},{10,12},{12... | collective-permute-start | bytes 196616 | tf_op jit(solution)/shard_map/ppermute | solution.py:42
  329.6 6.4 %collective-permute-start.16 = (f32[128,512]{1,0:T(8,128)S(1)}, f32[128,512]{1,0:T(8,128)S(1)}, u32[]{:S(2)}, u32[]{:S(2)}) collective-permute-start(f32[128,512]{1,0:T(8,128)S(1)} %bitcast_select_fusion), channel_id=1, source_target_pairs={{0,8},{8,0},{1,9},{9,1},{2,10},{10,2},{3,11},{11,3},{4,12},{12,4},... | collective-permute-start | bytes 786440 | tf_op jit(solution)/shard_map/ppermute | solution.py:37
  336.1 2.0 collective-permute-start.17
  (1 other events, 1.0 us)
Sparse Core Ops, SparseCore 0:
  9.6 153.7 all-gather.2
  196.9 97.7 reduce-scatter.1

commit v5 on v4

--- a/solution.py
+++ b/solution.py
@@ -27,10 +27,6 @@
 def triple(left_high, left_low, right_high, right_low):
     dot = functools.partial(jnp.dot, preferred_element_type=F32)
     return dot(left_high, right_high) + (dot(left_high, right_low) + dot(left_low, right_high))
-
-
-def high_dot(left, right, dims=(((1,), (0,)), ((), ()))):
-    return lax.dot_general(left, right, dims, precision=lax.Precision.HIGH, preferred_element_type=F32)
 
 
 def swap(value, axis):
@@ -130,81 +126,88 @@
     )(left_high, left_low, test, *blocks)
 
 
-def terms_kernel(place, columns, partial, product_high, product_low, high, low, test, out):
+def terms_kernel(base, place, columns, partial, product_high, product_low, high, low, test, out):
     slots, rows, _ = columns.shape
-    width = high.shape[1]
     left_high, left_low = split(jnp.concatenate([columns[at] for at in range(slots)], axis=1))
     out[...] = partial[...] - triple(left_high, left_low, product_high[...], product_low[...])
-    leaf = place[0] - place[1] + pl.program_id(0) * (rows // LEAF)
-    for at in range(rows // LEAF):
-
-        @pl.when((leaf + at >= 0) & (leaf + at < width // LEAF))
-        def _():
+    tile = place[2] + base + pl.program_id(0)
+
+    @pl.when((tile >= 0) & (tile < place[3]))
+    def _():
+        for at in range(rows // LEAF):
             piece = slice(at * LEAF, (at + 1) * LEAF)
-            column = pl.multiple_of((leaf + at) * LEAF, LEAF)
-            block = triple(
-                left_high[piece], left_low[piece], high[:, pl.ds(column, LEAF)], low[:, pl.ds(column, LEAF)]
-            )
-            out[piece] += triple(*split(block), *split(test[pl.ds(column, LEAF)]))
-
-
-def terms(place, columns, partial, weight, product, test):
-    slots, height, slot = columns.shape
+            block = triple(left_high[piece], left_low[piece], high[:, piece], low[:, piece])
+            out[piece] += triple(*split(block), *split(test[piece]))
+
+
+def terms(place, columns, partial, weight, product, test, start, tile):
+    slots, rows, slot = columns.shape
     panel, width = weight[0].shape
     samples = test.shape[1]
-    tile = 512
-
-    def whole(array):
-        return pl.BlockSpec(array.shape, lambda i, place: (0, 0), pipeline_mode=pl.Buffered(1))
-
-    return pl.pallas_call(
-        terms_kernel,
+    base = start // tile
+    last = width // tile - 1
+
+    def diagonal(i, place):
+        return jnp.clip(place[2] + base + i, 0, last)
+
+    whole = pl.BlockSpec((panel, samples), lambda i, place: (0, 0), pipeline_mode=pl.Buffered(1))
+    strip = pl.BlockSpec((panel, tile), lambda i, place: (0, diagonal(i, place)))
+    return pl.pallas_call(
+        functools.partial(terms_kernel, base),
         out_shape=jax.ShapeDtypeStruct(partial.shape, F32),
         grid_spec=pltpu.PrefetchScalarGridSpec(
             num_scalar_prefetch=1,
-            grid=(height // tile,),
+            grid=(rows // tile,),
             in_specs=[
                 pl.BlockSpec((slots, tile, slot), lambda i, place: (0, i, 0)),
-                pl.BlockSpec((tile, samples), lambda i, place: (i, 0)),
-                *map(whole, product),
-                *map(whole, weight),
-                whole(test),
+                pl.BlockSpec((tile, samples), lambda i, place: (base + i, 0)),
+                whole,
+                whole,
+                strip,
+                strip,
+                pl.BlockSpec((tile, samples), lambda i, place: (diagonal(i, place), 0)),
             ],
-            out_specs=pl.BlockSpec((tile, samples), lambda i, place: (i, 0)),
-        ),
+            out_specs=pl.BlockSpec((tile, samples), lambda i, place: (base + i, 0)),
+        ),
+        input_output_aliases={2: 0},
         compiler_params=pltpu.CompilerParams(vmem_limit_bytes=VMEM),
         cost_estimate=pl.CostEstimate(
-            flops=6 * height * panel * samples, bytes_accessed=height * (panel + 2 * samples) * 4, transcendentals=0
+            flops=6 * rows * panel * samples, bytes_accessed=rows * (panel + 2 * samples) * 4, transcendentals=0
         ),
         name="terms",
     )(place, columns, partial, *product, *weight, test)
 
 
-def update_kernel(place, columns, high, low, front, out, leaves):
-    slots = columns.shape[0]
-    left_high, left_low = split(jnp.concatenate([columns[at] for at in range(slots)], axis=1))
+def update_kernel(tiles, place, first, second, high, low, front, out, leaves):
+    slots = first.shape[0]
+    step = pl.program_id(0)
+    columns = [jnp.where(step < tiles, first[at], second[at]) for at in range(slots)]
+    left_high, left_low = split(jnp.concatenate(columns, axis=1))
     out[...] = front[...] - triple(left_high, left_low, high[...], low[...])
     rows, width = out.shape
-    leaf = place[0] - place[1] + pl.program_id(0) * (rows // LEAF)
+    leaf = place[0] - place[1] + step * (rows // LEAF)
     for at in range(rows // LEAF):
         column = jnp.clip(leaf + at, 0, width // LEAF - 1) * LEAF
         piece = pl.ds(at * LEAF, LEAF)
         leaves[piece, :] = out[piece, pl.ds(pl.multiple_of(column, LEAF), LEAF)]
 
 
-def update(place, columns, weight, front):
-    slots, height, slot = columns.shape
-    panel, width = weight[0].shape
+def update(place, chunks, weight, front):
+    slots, _, slot = chunks[0].shape
+    height, width = front.shape
+    panel = weight[0].shape[0]
     tile = 256
+    tiles = chunks[0].shape[1] // tile
     whole = pl.BlockSpec((panel, width), lambda i, place: (0, 0), pipeline_mode=pl.Buffered(1))
     return pl.pallas_call(
-        update_kernel,
+        functools.partial(update_kernel, tiles),
         out_shape=[jax.ShapeDtypeStruct((height, width), F32), jax.ShapeDtypeStruct((height, LEAF), F32)],
         grid_spec=pltpu.PrefetchScalarGridSpec(
             num_scalar_prefetch=1,
             grid=(height // tile,),
             in_specs=[
-                pl.BlockSpec((slots, tile, slot), lambda i, place: (0, i, 0)),
+                pl.BlockSpec((slots, tile, slot), lambda i, place: (0, jnp.minimum(i, tiles - 1), 0)),
+                pl.BlockSpec((slots, tile, slot), lambda i, place: (0, jnp.maximum(i - tiles, 0), 0)),
                 whole,
                 whole,
                 pl.BlockSpec((tile, width), lambda i, place: (i, 0)),
@@ -219,7 +222,7 @@
             flops=6 * height * panel * width, bytes_accessed=height * width * 8 + panel * width * 4, transcendentals=0
         ),
         name="update",
-    )(place, columns, *weight, front)
+    )(place, *chunks, *weight, front)
 
 
 def halve(value, axis):
@@ -248,6 +251,94 @@
     return double(double(value, "lo"), "core")
 
 
+def pack_kernel(rows, out):
+    high, low = split(rows[...])
+    dot = functools.partial(
+        lax.dot_general, dimension_numbers=(((0,), (0,)), ((), ())), preferred_element_type=F32
+    )
+    size = rows.shape[1]
+    at = 0
+    for start in range(0, size, LEAF):
+        part, rest = slice(start, start + LEAF), slice(start, size)
+        value = dot(high[:, part], high[:, rest]) + (dot(high[:, part], low[:, rest]) + dot(low[:, part], high[:, rest]))
+        for column in range(0, size - start, LEAF):
+            out[at : at + LEAF] = value[:, column : column + LEAF]
+            at += LEAF
+
+
+def packed_gram(rows):
+    size = rows.shape[1]
+    count = size // LEAF
+    return pl.pallas_call(
+        pack_kernel,
+        out_shape=jax.ShapeDtypeStruct((count * (count + 1) // 2 * LEAF, LEAF), F32),
+        compiler_params=pltpu.CompilerParams(vmem_limit_bytes=VMEM),
+        name="gram",
+    )(rows)
+
+
+def unpack_kernel(divisor, blocks, out):
+    size = out.shape[0]
+    at = 0
+    for i in range(0, size, LEAF):
+        for j in range(i, size, LEAF):
+            block = blocks[at : at + LEAF] / divisor
+            out[i : i + LEAF, j : j + LEAF] = block
+            if j > i:
+                out[j : j + LEAF, i : i + LEAF] = block.T
+            at += LEAF
+
+
+def unpacked(blocks, size, divisor):
+    return pl.pallas_call(
+        functools.partial(unpack_kernel, float(divisor)),
+        out_shape=jax.ShapeDtypeStruct((size, size), F32),
+        compiler_params=pltpu.CompilerParams(vmem_limit_bytes=VMEM),
+        name="unpack",
+    )(blocks)
+
+
+def spread_leaves(leaves, rows):
+    row_count, chips = 2 * lax.axis_size("hi"), lax.axis_size("z")
+    row, z, core = lax.axis_index("hi") * 2 + lax.axis_index("lo"), lax.axis_index("z"), lax.axis_index("core")
+    piece = 2 * rows // row_count
+    half = chips // 2
+    width = half * 2 * rows
+    region = lax.dynamic_slice_in_dim(leaves, core * width, width, 0).reshape(half, row_count, piece, LEAF)
+
+    def part(step):
+        return lax.dynamic_index_in_dim(region, (row + step) % row_count, 1, keepdims=False)
+
+    share = jnp.where(row == z, part(0), 0.0)
+    for step in range(1, row_count):
+        route = []
+        for r in range(row_count):
+            for h in range(2):
+                route.append(((r * chips + r) * 2 + h, ((r + step) % row_count * chips + r) * 2 + h))
+        share = share + lax.ppermute(part(step), ALL, route)
+    received = []
+    for turn in range(half):
+        route = [
+            (2 * at + h, 2 * (h * half + (at + turn) % half) + at // half) for at in range(chips) for h in range(2)
+        ]
+        sent = lax.dynamic_index_in_dim(share, (z + turn) % half, 0, keepdims=False)
+        received.append(lax.ppermute(sent, ("z", "core"), route))
+    stacked = jnp.stack(received)
+    parts = []
+    for turn in range(half):
+        route = []
+        for k in range(row_count):
+            for at in range(chips):
+                for e in range(2):
+                    target = e * half + (turn + k) % half
+                    route.append(((k * chips + at) * 2 + e, (target * chips + at) * 2 + k // half))
+        which = (z - turn - row) % half
+        parts.append(lax.ppermute(lax.dynamic_index_in_dim(stacked, which, 0, keepdims=False), ALL, route))
+    stacked = jnp.stack(parts)
+    ordered = [lax.dynamic_index_in_dim(stacked, (row - at) % half, 0, keepdims=False) for at in range(half)]
+    return jnp.concatenate(ordered, axis=0)
+
+
 def body(front_trailing, panel_columns, panel_rows, pivots, diag_inverse, test_matrix):
     hi_count, z_count = lax.axis_size("hi"), lax.axis_size("z")
     row_count, col_count = 2 * hi_count, 2 * z_count
@@ -257,15 +348,22 @@
     depth = panel_rows.shape[0]
     panel = depth * row_count
     per = height // col_count
-    ratio = col_count // row_count
-    targets = col_count // ratio
-    place = jnp.stack([row * (height // LEAF), col * (width // LEAF)])
-
-    columns = lax.all_gather(panel_columns, ("z", "core"), axis=0, tiled=False)
-
+    tile = height // 8
+    cut = height - tile
+    place = jnp.stack(
+        [
+            row * (height // LEAF),
+            col * (width // LEAF),
+            row * (height // tile) - col * (width // tile),
+            jnp.int32(width // tile),
+        ]
+    )
+
+    first = lax.all_gather(panel_columns[:cut], ("z", "core"), axis=0, tiled=False)
     over_lo = swap(panel_rows, "lo")
     over_hi = [shift(panel_rows, "hi", step) for step in range(1, hi_count)]
     partial = front_samples(place, front_trailing, test_matrix)
+    second = lax.all_gather(after(panel_columns[cut:], over_lo), ("z", "core"), axis=0, tiled=False)
     over_lo, *over_hi = after([over_lo, *over_hi], partial)
     blocks, owners = [panel_rows, over_lo], [row, row ^ 1]
     for step, block in enumerate(over_hi, 1):
@@ -281,23 +379,15 @@
     ]
     high, low, *product = weights(left_high, left_low, test_matrix, blocks)
 
-    partial = terms(place, columns, partial, (high, low), product, test_matrix)
+    weight = (high, low)
+    partial = terms(place, first, partial, weight, product, test_matrix, 0, tile)
+    partial = terms(place, second, partial, weight, product, test_matrix, cut, tile)
     off_samples = lax.psum_scatter(partial, ("z", "core"), scatter_dimension=0, tiled=True)
-    schur, leaves = update(after(place, partial), columns, (high, low), front_trailing)
-
-    half = col % ratio
-    leaf_blocks = 0
-    for m in range(targets):
-        piece = lax.dynamic_slice_in_dim(leaves, (half * targets + m) * per, per, 0)
-        route = [
-            (r * col_count + ratio * r + h, r * col_count + h * targets + m)
-            for r in range(row_count)
-            for h in range(ratio)
-        ]
-        leaf_blocks = leaf_blocks + lax.ppermute(piece, ALL, route)
-
-    gram = high_dot(after(off_samples, leaf_blocks), off_samples, (((0,), (0,)), ((), ())))
-    group_gram = (group_sum(gram) / (2 * height))[None]
+    schur, leaves = update(after(place, partial), (first, second), weight, front_trailing)
+    leaf_blocks = spread_leaves(leaves, per)
+    samples = after(off_samples, leaf_blocks)
+    gram = group_sum(packed_gram(samples))
+    group_gram = unpacked(gram, samples.shape[1], 2 * height)[None]
     return (schur, off_samples, leaf_blocks, group_gram)
 
 

time: 348 us -> 334 us (0.960)
  waiting for transfers between devices: 133 us -> 98.9 us
  starting transfers between devices: 24.5 us -> 34.8 us
  Pallas kernels: 157 us -> 162 us
  local copies, waits for them, and re-layouts: 4.47 us -> 9.16 us
    all_gather x1 -> x2, waiting for transfers between devices: 50.5 us -> 35.5 us  [the longest x1 31.9 us: body(): lax.all_gather(panel_columns[:cut], ('z', 'core'), axis=0, tiled=False)]
    ppermute x6, waiting for transfers between devices: 41.2 us -> 31.5 us  [swap(): return lax.ppermute(value, axis, [(0, 1), (1, 0)])]
    ppermute x6, starting transfers between devices: 7.43 us -> 14.3 us  [swap(): return lax.ppermute(value, axis, [(0, 1), (1, 0)])]
    reduce_scatter x1, waiting for transfers between devices: 6.21 us -> 0.01 us  [body(): lax.psum_scatter(partial, ('z', 'core'), scatter_dimension=0, tiled=True)]
    ppermute x4 -> x7, starting transfers between devices: 5.43 us -> 11.2 us  [the longest x3 6.28 us: spread_leaves(): share = share + lax.ppermute(part(step), ALL, route)]
    pallas_call x2 -> x5, Pallas kernels: 95.8 us -> 101 us  [the longest x1 62.5 us: update(): pl.pallas_call(functools.partial(update_kernel, tiles), out_shape=[jax.Sh...]
    slice x0 -> x2, local copies, waits for them, and re-layouts: none -> 4.57 us  [the longest x1 2.9 us: body(): panel_columns[:cut]]
    ppermute x4 -> x7, waiting for transfers between devices: 21.7 us -> 19.3 us  [the longest x3 8.6 us: spread_leaves(): share = share + lax.ppermute(part(step), ALL, route)]
  transfers between devices with their start and end apart: 20 -> 24, of which waited for: 18 -> 19; matrix products, arithmetic and copies ran while one was open for 3% -> 5% of each run, Pallas kernels for 36% -> 45%
where the time goes in v5:
time: 334 us; the launch traced here: 333 us
  Pallas kernels  162 us (49%)
  waiting for transfers between devices  98.9 us (30%)
  starting transfers between devices  34.8 us (10%)
  between operations  14.2 us (4%)
  matrix products  9.91 us (3%)
  local copies, waits for them, and re-layouts  9.16 us (3%)
  other arithmetic  3.96 us (1%)
    pallas_call x1, Pallas kernels, update(): pl.pallas_call(functools.partial(update_kernel, tiles), out_shape=[jax.Sh...  62.5 us
    pallas_call x1, Pallas kernels, front_samples(): pl.pallas_call(samples_kernel, out_shape=jax.ShapeDtypeStruct((height, sa...  34.1 us
    pallas_call x2, Pallas kernels, terms(): pl.pallas_call(functools.partial(terms_kernel, base), out_shape=jax.Shape...  33.1 us
    all_gather x1, waiting for transfers between devices, body(): lax.all_gather(panel_columns[:cut], ('z', 'core'), axis=0, tiled=False)  31.9 us
    ppermute x6, waiting for transfers between devices, swap(): return lax.ppermute(value, axis, [(0, 1), (1, 0)])  31.5 us
    pallas_call x1, Pallas kernels, weights(): pl.pallas_call(functools.partial(weights_kernel, len(blocks)), out_shape=...  27.4 us
    ppermute x6, starting transfers between devices, swap(): return lax.ppermute(value, axis, [(0, 1), (1, 0)])  14.3 us
    ppermute x8, waiting for transfers between devices, shift(): lax.ppermute(value, axis, [(at, (at + step) % count) for at in range(coun...  12.6 us
  transfers between devices with their start and end apart: 24, of which 19 were waited for; matrix products, arithmetic and copies ran while one was open for 5% of the time, Pallas kernels for 45%

profile of v5, /device:TPU:0, one launch (start us, length us, event | category | flops | bytes accessed | tf_op | source)
XLA Modules:
  0.0 333.2 jit_solution(17539026529990053476)
XLA Ops:
  7.2 2.9 slice.13
  10.2 3.0 collective-permute-start
  17.2 34.1 %samples.1.partial = f32[4096,512]{1,0:T(8,128)} custom-call(s32[4]{0:T(128)} %pad_add_fusion.place, f32[4096,2048]{1,0:T(8,128)} %front.3, f32[2048,512]{1,0:T(8,128)} %test.5), custom_call_target="tpu_custom_call" | custom-call | flops 25769803776 | bytes 33554432 | tf_op jit(solution)/shard_map/samples/pallas_call | solution.py:63
  51.3 7.7 %collective-permute-done.refs_4_ = f32[256,2048]{1,0:T(8,128)S(1)} collective-permute-done((f32[256,2048]{1,0:T(8,128)}, f32[256,2048]{1,0:T(8,128)S(1)}, u32[]{:S(2)}, u32[]{:S(2)}) %collective-permute-start) | collective-permute-done | bytes 2097184 | tf_op jit(solution)/shard_map/ppermute | solution.py:33
  65.4 6.1 %fusion.10.refs_0_ = bf16[1024,1024]{1,0:T(8,128)(2,1)} fusion(s32[1024]{0:T(1024)S(1)} %bitcast.82, s32[1024]{0:T(1024)S(1)} %copy-done.3, f32[1024,1024]{1,0:T(8,128)} %param.10), kind=kOutput, calls=%fused_computation.12 | convolution fusion | flops 2151677952 | bytes 6299648 | tf_op jit(solution)/shard_map/dot_general | solution.py:377
  71.5 3.8 %fusion.13.refs_1_ = bf16[1024,1024]{1,0:T(8,128)(2,1)} fusion(s32[1024]{0:T(1024)S(1)} %bitcast.83, s32[1024]{0:T(1024)S(1)} %copy-done.3, f32[1024,1024]{1,0:T(8,128)S(1)} %copy-done.1), kind=kOutput, calls=%fused_computation.13 | convolution fusion | flops 2152726528 | bytes 6299648 | tf_op jit(solution)/shard_map/dot_general | solution.py:377
  75.3 11.0 %collective-permute-done.3.refs_7_ = f32[128,2048]{1,0:T(8,128)S(1)} collective-permute-done((f32[128,2048]{1,0:T(8,128)S(1)}, f32[128,2048]{1,0:T(8,128)S(1)}, u32[]{:S(2)}, u32[]{:S(2)}) %collective-permute-start.3) | collective-permute-done | bytes 1048608 | tf_op jit(solution)/shard_map/ppermute | solution.py:33
  87.6 27.4 %weights.1 = (bf16[1024,2048]{1,0:T(8,128)(2,1)}, bf16[1024,2048]{1,0:T(8,128)(2,1)}, bf16[1024,512]{1,0:T(8,128)(2,1)}, bf16[1024,512]{1,0:T(8,128)(2,1)}) custom-call(bf16[1024,1024]{1,0:T(8,128)(2,1)} %fusion.10.refs_0_, bf16[1024,1024]{1,0:T(8,128)(2,1)} %fusion.13.refs_1_, f32[2048,512]{1,0:T(8,128)} %test.5, f32[256,2048]{1,0:T(8,128)} %refs_3_.1, ...), custom_call_target="tpu_custom_call" | custom-call | flops 19327352832 | bytes 16777216 | tf_op jit(solution)/shard_map/weights/pallas_call | solution.py:113
  115.0 31.9 %all-gather.7.cloned.1.call-done = f32[28672,128]{1,0:T(8,128)} async-done(((f32[3584,128]{1,0:T(8,128)}), f32[28672,128]{1,0:T(8,128)}) %all-gather.7.cloned.1.call-update) | async-done | bytes 14680080 | tf_op jit(solution)/shard_map/all_gather | solution.py:362
  146.9 26.0 %terms.2.partial = f32[4096,512]{1,0:T(8,128)} custom-call(s32[4]{0:T(128)} %pad_add_fusion.place, f32[8,3584,128]{2,1,0:T(8,128)} %bitcast.65, f32[4096,512]{1,0:T(8,128)} %samples.1.partial, bf16[1024,512]{1,0:T(8,128)(2,1)} %get-tuple-element.20.product_high, bf16[1024,512]{1,0:T(8,128)(2,1)} %get-tuple-element.21.product_low, ...), custom_call_target="tpu_custom_call", output_to_operand_aliasing={{}: (2, {})} | custom-call | flops 11274289152 | bytes 29360128 | tf_op jit(solution)/shard_map/terms/pallas_call | solution.py:155
  172.9 3.5 %all-gather.5.cloned.1.call-done = f32[4096,128]{1,0:T(8,128)} async-done(((f32[512,128]{1,0:T(8,128)}), f32[4096,128]{1,0:T(8,128)}) %all-gather.5.cloned.1.call-update) | async-done | bytes 2097168 | tf_op jit(solution)/shard_map/all_gather | solution.py:366
  176.4 7.1 %terms.3 = f32[4096,512]{1,0:T(8,128)} custom-call(s32[4]{0:T(128)} %pad_add_fusion.place, f32[8,512,128]{2,1,0:T(8,128)} %bitcast.69, f32[4096,512]{1,0:T(8,128)} %terms.2.partial, bf16[1024,512]{1,0:T(8,128)(2,1)} %get-tuple-element.20.product_high, bf16[1024,512]{1,0:T(8,128)(2,1)} %get-tuple-element.21.product_low, ...), custom_call_target="tpu_custom_call", output_to_operand_aliasing={{}: (2, {})} | custom-call | flops 1610612736 | bytes 4194304 | tf_op jit(solution)/shard_map/terms/pallas_call | solution.py:155
  183.6 62.5 %update.1 = (f32[4096,2048]{1,0:T(8,128)}, f32[4096,128]{1,0:T(8,128)}) custom-call(s32[4]{0:T(128)} %pad_add_fusion.place, f32[8,3584,128]{2,1,0:T(8,128)} %bitcast.66, f32[8,512,128]{2,1,0:T(8,128)} %bitcast.70, bf16[1024,2048]{1,0:T(8,128)(2,1)} %get-tuple-element.22.high, bf16[1024,2048]{1,0:T(8,128)(2,1)} %get-tuple-element.23.low, f32[4096,2048]{1,0:T(8,128)} %front.3), custom_call_target="tpu_custom_call" | custom-call | flops 51539607552 | bytes 75497472 | tf_op jit(solution)/shard_map/update/pallas_call | solution.py:202
  247.5 3.4 %collective-permute-start.4 = (f32[2,256,128]{2,1,0:T(8,128)S(1)}, f32[2,256,128]{2,1,0:T(8,128)S(1)}, u32[]{:S(2)}, u32[]{:S(2)}) collective-permute-start(f32[2,256,128]{2,1,0:T(8,128)S(1)} %get-tuple-element.28), channel_id=1, source_target_pairs={{0,8},{1,9},{10,18},{11,19},{20,28},{21,29},{30,6},{31,7}} | collective-permute-start | bytes 786440 | tf_op jit(solution)/shard_map/ppermute | solution.py:318
  253.9 3.7 %collective-permute-done.4 = f32[2,256,128]{2,1,0:T(8,128)S(1)} collective-permute-done((f32[2,256,128]{2,1,0:T(8,128)S(1)}, f32[2,256,128]{2,1,0:T(8,128)S(1)}, u32[]{:S(2)}, u32[]{:S(2)}) %collective-permute-start.4) | collective-permute-done | bytes 262176 | tf_op jit(solution)/shard_map/ppermute | solution.py:318
  257.6 4.9 %collective-permute-done.6 = f32[2,256,128]{2,1,0:T(8,128)S(1)} collective-permute-done((f32[2,256,128]{2,1,0:T(8,128)S(1)}, f32[2,256,128]{2,1,0:T(8,128)S(1)}, u32[]{:S(2)}, u32[]{:S(2)}) %collective-permute-start.6) | collective-permute-done | bytes 262176 | tf_op jit(solution)/shard_map/ppermute | solution.py:318
  262.6 3.5 %collective-permute-start.8 = (f32[256,128]{1,0:T(8,128)S(1)}, f32[256,128]{1,0:T(8,128)S(1)}, u32[]{:S(2)}, u32[]{:S(2)}) collective-permute-start(f32[256,128]{1,0:T(8,128)S(1)} %get-tuple-element.39), channel_id=1, source_target_pairs={{0,2},{1,6},{2,0},{3,4},{4,3},{5,7},{6,1},{7,5},{8,10},{9,14},{10,... | collective-permute-start | bytes 393224 | tf_op jit(solution)/shard_map/ppermute | solution.py:325
  266.8 6.5 %collective-permute-done.8 = f32[256,128]{1,0:T(8,128)S(1)} collective-permute-done((f32[256,128]{1,0:T(8,128)S(1)}, f32[256,128]{1,0:T(8,128)S(1)}, u32[]{:S(2)}, u32[]{:S(2)}) %collective-permute-start.8) | collective-permute-done | bytes 131104 | tf_op jit(solution)/shard_map/ppermute | solution.py:325
  274.1 4.2 %collective-permute-done.10 = f32[256,128]{1,0:T(8,128)S(1)} collective-permute-done((f32[256,128]{1,0:T(8,128)S(1)}, f32[256,128]{1,0:T(8,128)S(1)}, u32[]{:S(2)}, u32[]{:S(2)}) %collective-permute-start.10) | collective-permute-done | bytes 131104 | tf_op jit(solution)/shard_map/ppermute | solution.py:336
  283.0 7.6 %collective-permute-start.11 = (f32[640,128]{1,0:T(8,128)S(1)}, f32[640,128]{1,0:T(8,128)S(1)}, u32[]{:S(2)}, u32[]{:S(2)}) collective-permute-start(f32[640,128]{1,0:T(8,128)S(1)} %constant_dynamic-slice_fusion.1), channel_id=1, source_target_pairs={{0,1},{1,0},{2,3},{3,2},{4,5},{5,4},{6,7},{7,6},{8,9},{9,8},{10,11... | collective-permute-start | bytes 983048 | tf_op jit(solution)/shard_map/ppermute | solution.py:33
  293.9 5.5 %collective-permute-done.12 = f32[320,128]{1,0:T(8,128)S(1)} collective-permute-done((f32[320,128]{1,0:T(8,128)S(1)}, f32[320,128]{1,0:T(8,128)S(1)}, u32[]{:S(2)}, u32[]{:S(2)}) %collective-permute-start.12) | collective-permute-done | bytes 163872 | tf_op jit(solution)/shard_map/ppermute | solution.py:33
  299.6 3.8 %collective-permute-start.15 = (f32[80,128]{1,0:T(8,128)S(1)}, f32[80,128]{1,0:T(8,128)S(1)}, u32[]{:S(2)}, u32[]{:S(2)}) collective-permute-start(f32[80,128]{1,0:T(8,128)S(1)} %get-tuple-element.42), channel_id=1, source_target_pairs={{0,6},{2,0},{4,2},{6,4},{1,7},{3,1},{5,3},{7,5},{8,14},{10,8},{12,... | collective-permute-start | bytes 122888 | tf_op jit(solution)/shard_map/ppermute | solution.py:38
  305.4 3.3 collective-permute-done.14
  317.2 4.4 %collective-permute-done.19 = f32[320,128]{1,0:T(8,128)S(1)} collective-permute-done((f32[320,128]{1,0:T(8,128)S(1)}, f32[320,128]{1,0:T(8,128)S(1)}, u32[]{:S(2)}, u32[]{:S(2)}) %collective-permute-start.19) | collective-permute-done | bytes 163872 | tf_op jit(solution)/shard_map/ppermute | solution.py:33
  (77 shorter events, 41.1 us)
Async XLA Ops:
  7.2 139.8 %all-gather.7.cloned.1.call-start = ((), (), s32[]{:S(2)}) async-start(), calls=%async_computation.3 | async-start | bytes 16515072 | tf_op jit(solution)/shard_map/all_gather | solution.py:362
  10.1 166.3 %all-gather.5.cloned.1.call-start = ((), (), s32[]{:S(2)}) async-start(), calls=%async_computation.2 | async-start | bytes 2359296 | tf_op jit(solution)/shard_map/all_gather | solution.py:366
  10.2 48.8 %collective-permute-start = (f32[256,2048]{1,0:T(8,128)}, f32[256,2048]{1,0:T(8,128)S(1)}, u32[]{:S(2)}, u32[]{:S(2)}) collective-permute-start(f32[256,2048]{1,0:T(8,128)} %refs_3_.1), channel_id=1, source_target_pairs={{0,8},{8,0},{1,9},{9,1},{2,10},{10,2},{3,11},{11,3},{4,12},{12,4},... | collective-permute-start | bytes 6291464 | tf_op jit(solution)/shard_map/ppermute | solution.py:33
  13.2 47.4 %collective-permute-start.1 = (f32[256,2048]{1,0:T(8,128)}, f32[256,2048]{1,0:T(8,128)}, u32[]{:S(2)}, u32[]{:S(2)}) collective-permute-start(f32[256,2048]{1,0:T(8,128)} %refs_3_.1), channel_id=1, source_target_pairs={{0,16},{16,0},{1,17},{17,1},{2,18},{18,2},{3,19},{19,3},{4,20},{20... | collective-permute-start | bytes 6291464 | tf_op jit(solution)/shard_map/ppermute | solution.py:38
  62.0 24.3 %collective-permute-start.3 = (f32[128,2048]{1,0:T(8,128)S(1)}, f32[128,2048]{1,0:T(8,128)S(1)}, u32[]{:S(2)}, u32[]{:S(2)}) collective-permute-start(f32[128,2048]{1,0:T(8,128)S(1)} %slice.15), channel_id=1, source_target_pairs={{0,8},{8,0},{1,9},{9,1},{2,10},{10,2},{3,11},{11,3},{4,12},{12,4},... | collective-permute-start | bytes 3145736 | tf_op jit(solution)/shard_map/ppermute | solution.py:33
  63.6 24.0 %collective-permute-start.2 = (f32[128,2048]{1,0:T(8,128)S(1)}, f32[128,2048]{1,0:T(8,128)}, u32[]{:S(2)}, u32[]{:S(2)}) collective-permute-start(f32[128,2048]{1,0:T(8,128)S(1)} %slice.14), channel_id=1, source_target_pairs={{0,16},{16,0},{1,17},{17,1},{2,18},{18,2},{3,19},{19,3},{4,20},{20... | collective-permute-start | bytes 3145736 | tf_op jit(solution)/shard_map/ppermute | solution.py:38
  65.1 214.0 %reduce-scatter.2.cloned.1.call-start = ((), (), s32[]{:S(2)}) async-start(), calls=%async_computation.1 | async-start | bytes 9437184 | tf_op jit(solution)/shard_map/reduce_scatter | solution.py:385
  247.5 10.0 %collective-permute-start.4 = (f32[2,256,128]{2,1,0:T(8,128)S(1)}, f32[2,256,128]{2,1,0:T(8,128)S(1)}, u32[]{:S(2)}, u32[]{:S(2)}) collective-permute-start(f32[2,256,128]{2,1,0:T(8,128)S(1)} %get-tuple-element.28), channel_id=1, source_target_pairs={{0,8},{1,9},{10,18},{11,19},{20,28},{21,29},{30,6},{31,7}} | collective-permute-start | bytes 786440 | tf_op jit(solution)/shard_map/ppermute | solution.py:318
  251.0 11.5 %collective-permute-start.6 = (f32[2,256,128]{2,1,0:T(8,128)S(1)}, f32[2,256,128]{2,1,0:T(8,128)S(1)}, u32[]{:S(2)}, u32[]{:S(2)}) collective-permute-start(f32[2,256,128]{2,1,0:T(8,128)S(1)} %get-tuple-element.29), channel_id=1, source_target_pairs={{0,24},{1,25},{10,2},{11,3},{20,12},{21,13},{30,22},{31,23}} | collective-permute-start | bytes 786440 | tf_op jit(solution)/shard_map/ppermute | solution.py:318
  252.5 10.0 %collective-permute-start.5 = (f32[2,256,128]{2,1,0:T(8,128)S(1)}, f32[2,256,128]{2,1,0:T(8,128)S(1)}, u32[]{:S(2)}, u32[]{:S(2)}) collective-permute-start(f32[2,256,128]{2,1,0:T(8,128)S(1)} %get-tuple-element.30), channel_id=1, source_target_pairs={{0,16},{1,17},{10,26},{11,27},{20,4},{21,5},{30,14},{31,15}} | collective-permute-start | bytes 786440 | tf_op jit(solution)/shard_map/ppermute | solution.py:318
  262.6 10.6 %collective-permute-start.8 = (f32[256,128]{1,0:T(8,128)S(1)}, f32[256,128]{1,0:T(8,128)S(1)}, u32[]{:S(2)}, u32[]{:S(2)}) collective-permute-start(f32[256,128]{1,0:T(8,128)S(1)} %get-tuple-element.39), channel_id=1, source_target_pairs={{0,2},{1,6},{2,0},{3,4},{4,3},{5,7},{6,1},{7,5},{8,10},{9,14},{10,... | collective-permute-start | bytes 393224 | tf_op jit(solution)/shard_map/ppermute | solution.py:325
  266.1 7.2 %collective-permute-start.7 = (f32[256,128]{1,0:T(8,128)S(1)}, f32[256,128]{1,0:T(8,128)S(1)}, u32[]{:S(2)}, u32[]{:S(2)}) collective-permute-start(f32[256,128]{1,0:T(8,128)S(1)} %get-tuple-element.40), channel_id=1, source_target_pairs={{0,0},{1,4},{2,2},{3,6},{4,1},{5,5},{6,3},{7,7},{8,8},{9,12},{10,1... | collective-permute-start | bytes 393224 | tf_op jit(solution)/shard_map/ppermute | solution.py:325
  273.3 5.0 %collective-permute-start.10 = (f32[256,128]{1,0:T(8,128)S(1)}, f32[256,128]{1,0:T(8,128)S(1)}, u32[]{:S(2)}, u32[]{:S(2)}) collective-permute-start(f32[256,128]{1,0:T(8,128)S(1)} %get-tuple-element.37), channel_id=1, source_target_pairs={{0,8},{1,24},{2,10},{3,26},{4,12},{5,28},{6,14},{7,30},{8,0},{9,16... | collective-permute-start | bytes 393224 | tf_op jit(solution)/shard_map/ppermute | solution.py:336
  273.4 5.0 %collective-permute-start.9 = (f32[256,128]{1,0:T(8,128)S(1)}, f32[256,128]{1,0:T(8,128)S(1)}, u32[]{:S(2)}, u32[]{:S(2)}) collective-permute-start(f32[256,128]{1,0:T(8,128)S(1)} %get-tuple-element.38), channel_id=1, source_target_pairs={{0,0},{1,16},{2,2},{3,18},{4,4},{5,20},{6,6},{7,22},{8,8},{9,24},{... | collective-permute-start | bytes 393224 | tf_op jit(solution)/shard_map/ppermute | solution.py:336
  283.0 8.9 %collective-permute-start.11 = (f32[640,128]{1,0:T(8,128)S(1)}, f32[640,128]{1,0:T(8,128)S(1)}, u32[]{:S(2)}, u32[]{:S(2)}) collective-permute-start(f32[640,128]{1,0:T(8,128)S(1)} %constant_dynamic-slice_fusion.1), channel_id=1, source_target_pairs={{0,1},{1,0},{2,3},{3,2},{4,5},{5,4},{6,7},{7,6},{8,9},{9,8},{10,11... | collective-permute-start | bytes 983048 | tf_op jit(solution)/shard_map/ppermute | solution.py:33
  292.9 6.5 %collective-permute-start.12 = (f32[320,128]{1,0:T(8,128)S(1)}, f32[320,128]{1,0:T(8,128)S(1)}, u32[]{:S(2)}, u32[]{:S(2)}) collective-permute-start(f32[320,128]{1,0:T(8,128)S(1)} %constant_dynamic-slice_fusion), channel_id=1, source_target_pairs={{0,8},{8,0},{1,9},{9,1},{2,10},{10,2},{3,11},{11,3},{4,12},{12,4},... | collective-permute-start | bytes 491528 | tf_op jit(solution)/shard_map/ppermute | solution.py:33
  299.5 5.9 %collective-permute-start.13 = (f32[80,128]{1,0:T(8,128)S(1)}, f32[80,128]{1,0:T(8,128)S(1)}, u32[]{:S(2)}, u32[]{:S(2)}) collective-permute-start(f32[80,128]{1,0:T(8,128)S(1)} %get-tuple-element.41), channel_id=1, source_target_pairs={{0,2},{2,4},{4,6},{6,0},{1,3},{3,5},{5,7},{7,1},{8,10},{10,12},{12... | collective-permute-start | bytes 122888 | tf_op jit(solution)/shard_map/ppermute | solution.py:38
  299.6 5.8 %collective-permute-start.15 = (f32[80,128]{1,0:T(8,128)S(1)}, f32[80,128]{1,0:T(8,128)S(1)}, u32[]{:S(2)}, u32[]{:S(2)}) collective-permute-start(f32[80,128]{1,0:T(8,128)S(1)} %get-tuple-element.42), channel_id=1, source_target_pairs={{0,6},{2,0},{4,2},{6,4},{1,7},{3,1},{5,3},{7,5},{8,14},{10,8},{12,... | collective-permute-start | bytes 122888 | tf_op jit(solution)/shard_map/ppermute | solution.py:38
  303.4 5.3 %collective-permute-start.14 = (f32[80,128]{1,0:T(8,128)S(1)}, f32[80,128]{1,0:T(8,128)S(1)}, u32[]{:S(2)}, u32[]{:S(2)}) collective-permute-start(f32[80,128]{1,0:T(8,128)S(1)} %get-tuple-element.43), channel_id=1, source_target_pairs={{0,4},{2,6},{4,0},{6,2},{1,5},{3,7},{5,1},{7,3},{8,12},{10,14},{12... | collective-permute-start | bytes 122888 | tf_op jit(solution)/shard_map/ppermute | solution.py:38
  308.7 4.2 %collective-permute-start.18 = (f32[80,128]{1,0:T(8,128)S(1)}, f32[80,128]{1,0:T(8,128)S(1)}, u32[]{:S(2)}, u32[]{:S(2)}) collective-permute-start(f32[80,128]{1,0:T(8,128)S(1)} %fusion.29), channel_id=1, source_target_pairs={{0,6},{2,0},{4,2},{6,4},{1,7},{3,1},{5,3},{7,5},{8,14},{10,8},{12,... | collective-permute-start | bytes 122888 | tf_op jit(solution)/shard_map/ppermute | solution.py:38
  309.3 4.9 %collective-permute-start.17 = (f32[80,128]{1,0:T(8,128)S(1)}, f32[80,128]{1,0:T(8,128)S(1)}, u32[]{:S(2)}, u32[]{:S(2)}) collective-permute-start(f32[80,128]{1,0:T(8,128)S(1)} %fusion.29), channel_id=1, source_target_pairs={{0,4},{2,6},{4,0},{6,2},{1,5},{3,7},{5,1},{7,3},{8,12},{10,14},{12... | collective-permute-start | bytes 122888 | tf_op jit(solution)/shard_map/ppermute | solution.py:38
  309.3 6.3 %collective-permute-start.16 = (f32[80,128]{1,0:T(8,128)S(1)}, f32[80,128]{1,0:T(8,128)S(1)}, u32[]{:S(2)}, u32[]{:S(2)}) collective-permute-start(f32[80,128]{1,0:T(8,128)S(1)} %fusion.29), channel_id=1, source_target_pairs={{0,2},{2,4},{4,6},{6,0},{1,3},{3,5},{5,7},{7,1},{8,10},{10,12},{12... | collective-permute-start | bytes 122888 | tf_op jit(solution)/shard_map/ppermute | solution.py:38
  316.2 5.4 %collective-permute-start.19 = (f32[320,128]{1,0:T(8,128)S(1)}, f32[320,128]{1,0:T(8,128)S(1)}, u32[]{:S(2)}, u32[]{:S(2)}) collective-permute-start(f32[320,128]{1,0:T(8,128)S(1)} %bitcast_select_fusion), channel_id=1, source_target_pairs={{0,8},{8,0},{1,9},{9,1},{2,10},{10,2},{3,11},{11,3},{4,12},{12,4},... | collective-permute-start | bytes 491528 | tf_op jit(solution)/shard_map/ppermute | solution.py:33
  321.8 1.7 collective-permute-start.20
  (4 other events, 23.0 us)
Sparse Core Ops, SparseCore 0:
  10.3 136.6 all-gather.6
  149.1 27.3 all-gather.4
  183.7 95.0 reduce-scatter.1

commit v6 on v5

--- a/solution.py
+++ b/solution.py
@@ -126,7 +126,8 @@
     )(left_high, left_low, test, *blocks)
 
 
-def terms_kernel(base, place, columns, partial, product_high, product_low, high, low, test, out):
+def terms_kernel(base, place, columns, partial, product_high, product_low, high, low, test, *refs):
+    out, blocks = refs[-2:]
     slots, rows, _ = columns.shape
     left_high, left_low = split(jnp.concatenate([columns[at] for at in range(slots)], axis=1))
     out[...] = partial[...] - triple(left_high, left_low, product_high[...], product_low[...])
@@ -138,9 +139,10 @@
             piece = slice(at * LEAF, (at + 1) * LEAF)
             block = triple(left_high[piece], left_low[piece], high[:, piece], low[:, piece])
             out[piece] += triple(*split(block), *split(test[piece]))
-
-
-def terms(place, columns, partial, weight, product, test, start, tile):
+            blocks[piece] = block
+
+
+def terms(place, columns, partial, blocks, weight, product, test, start, tile):
     slots, rows, slot = columns.shape
     panel, width = weight[0].shape
     samples = test.shape[1]
@@ -152,77 +154,104 @@
 
     whole = pl.BlockSpec((panel, samples), lambda i, place: (0, 0), pipeline_mode=pl.Buffered(1))
     strip = pl.BlockSpec((panel, tile), lambda i, place: (0, diagonal(i, place)))
+    operands = [place, columns, partial, *product, *weight, test]
+    specs = [
+        pl.BlockSpec((slots, tile, slot), lambda i, place: (0, i, 0)),
+        pl.BlockSpec((tile, samples), lambda i, place: (base + i, 0)),
+        whole,
+        whole,
+        strip,
+        strip,
+        pl.BlockSpec((tile, samples), lambda i, place: (diagonal(i, place), 0)),
+    ]
+    aliases = {2: 0}
+    if blocks is not None:
+        aliases[len(operands)] = 1
+        operands.append(blocks)
+        specs.append(pl.BlockSpec(memory_space=pl.ANY))
     return pl.pallas_call(
         functools.partial(terms_kernel, base),
-        out_shape=jax.ShapeDtypeStruct(partial.shape, F32),
+        out_shape=[
+            jax.ShapeDtypeStruct(partial.shape, F32),
+            jax.ShapeDtypeStruct((partial.shape[0], LEAF), F32),
+        ],
         grid_spec=pltpu.PrefetchScalarGridSpec(
             num_scalar_prefetch=1,
             grid=(rows // tile,),
-            in_specs=[
-                pl.BlockSpec((slots, tile, slot), lambda i, place: (0, i, 0)),
+            in_specs=specs,
+            out_specs=[
                 pl.BlockSpec((tile, samples), lambda i, place: (base + i, 0)),
-                whole,
-                whole,
-                strip,
-                strip,
-                pl.BlockSpec((tile, samples), lambda i, place: (diagonal(i, place), 0)),
+                pl.BlockSpec((tile, LEAF), lambda i, place: (base + i, 0)),
             ],
-            out_specs=pl.BlockSpec((tile, samples), lambda i, place: (base + i, 0)),
-        ),
-        input_output_aliases={2: 0},
+        ),
+        input_output_aliases=aliases,
         compiler_params=pltpu.CompilerParams(vmem_limit_bytes=VMEM),
         cost_estimate=pl.CostEstimate(
             flops=6 * rows * panel * samples, bytes_accessed=rows * (panel + 2 * samples) * 4, transcendentals=0
         ),
         name="terms",
-    )(place, columns, partial, *product, *weight, test)
-
-
-def update_kernel(tiles, place, first, second, high, low, front, out, leaves):
+    )(*operands)
+
+
+def leaves_kernel(place, front, blocks, out):
+    for at in range(0, out.shape[0], LEAF):
+        piece = slice(at, at + LEAF)
+        out[piece] = front[piece, piece] - blocks[piece]
+
+
+def leaf_blocks_here(place, front, blocks, tile):
+    width = front.shape[1]
+    return pl.pallas_call(
+        leaves_kernel,
+        out_shape=jax.ShapeDtypeStruct((width, LEAF), F32),
+        grid_spec=pltpu.PrefetchScalarGridSpec(
+            num_scalar_prefetch=1,
+            grid=(width // tile,),
+            in_specs=[
+                pl.BlockSpec((tile, tile), lambda i, place: (place[4] + i, i)),
+                pl.BlockSpec((tile, LEAF), lambda i, place: (place[4] + i, 0)),
+            ],
+            out_specs=pl.BlockSpec((tile, LEAF), lambda i, place: (i, 0)),
+        ),
+        compiler_params=pltpu.CompilerParams(vmem_limit_bytes=VMEM),
+        cost_estimate=pl.CostEstimate(flops=width * LEAF, bytes_accessed=width * tile * 4, transcendentals=0),
+        name="leaves",
+    )(place, front, blocks)
+
+
+def update_kernel(tiles, first, second, high, low, front, out):
     slots = first.shape[0]
     step = pl.program_id(0)
     columns = [jnp.where(step < tiles, first[at], second[at]) for at in range(slots)]
     left_high, left_low = split(jnp.concatenate(columns, axis=1))
     out[...] = front[...] - triple(left_high, left_low, high[...], low[...])
-    rows, width = out.shape
-    leaf = place[0] - place[1] + step * (rows // LEAF)
-    for at in range(rows // LEAF):
-        column = jnp.clip(leaf + at, 0, width // LEAF - 1) * LEAF
-        piece = pl.ds(at * LEAF, LEAF)
-        leaves[piece, :] = out[piece, pl.ds(pl.multiple_of(column, LEAF), LEAF)]
-
-
-def update(place, chunks, weight, front):
+
+
+def update(chunks, weight, front):
     slots, _, slot = chunks[0].shape
     height, width = front.shape
     panel = weight[0].shape[0]
     tile = 256
     tiles = chunks[0].shape[1] // tile
-    whole = pl.BlockSpec((panel, width), lambda i, place: (0, 0), pipeline_mode=pl.Buffered(1))
+    whole = pl.BlockSpec((panel, width), lambda i: (0, 0), pipeline_mode=pl.Buffered(1))
     return pl.pallas_call(
         functools.partial(update_kernel, tiles),
-        out_shape=[jax.ShapeDtypeStruct((height, width), F32), jax.ShapeDtypeStruct((height, LEAF), F32)],
-        grid_spec=pltpu.PrefetchScalarGridSpec(
-            num_scalar_prefetch=1,
-            grid=(height // tile,),
-            in_specs=[
-                pl.BlockSpec((slots, tile, slot), lambda i, place: (0, jnp.minimum(i, tiles - 1), 0)),
-                pl.BlockSpec((slots, tile, slot), lambda i, place: (0, jnp.maximum(i - tiles, 0), 0)),
-                whole,
-                whole,
-                pl.BlockSpec((tile, width), lambda i, place: (i, 0)),
-            ],
-            out_specs=[
-                pl.BlockSpec((tile, width), lambda i, place: (i, 0)),
-                pl.BlockSpec((tile, LEAF), lambda i, place: (i, 0)),
-            ],
-        ),
+        out_shape=jax.ShapeDtypeStruct((height, width), F32),
+        grid=(height // tile,),
+        in_specs=[
+            pl.BlockSpec((slots, tile, slot), lambda i: (0, jnp.minimum(i, tiles - 1), 0)),
+            pl.BlockSpec((slots, tile, slot), lambda i: (0, jnp.maximum(i - tiles, 0), 0)),
+            whole,
+            whole,
+            pl.BlockSpec((tile, width), lambda i: (i, 0)),
+        ],
+        out_specs=pl.BlockSpec((tile, width), lambda i: (i, 0)),
         compiler_params=pltpu.CompilerParams(vmem_limit_bytes=VMEM),
         cost_estimate=pl.CostEstimate(
             flops=6 * height * panel * width, bytes_accessed=height * width * 8 + panel * width * 4, transcendentals=0
         ),
         name="update",
-    )(place, *chunks, *weight, front)
+    )(*chunks, *weight, front)
 
 
 def halve(value, axis):
@@ -240,15 +269,16 @@
 
 def group_sum(gram):
     chips, z = lax.axis_size("z"), lax.axis_index("z")
-    value = halve(halve(gram, "core"), "lo")
+    value = halve(gram, "core")
     parts = value.reshape(chips, value.shape[0] // chips, value.shape[1])
     total = lax.dynamic_index_in_dim(parts, z, 0, keepdims=False)
     for step in range(1, chips):
         part = lax.dynamic_index_in_dim(parts, (z + step) % chips, 0, keepdims=False)
         total = total + shift(part, "z", step)
+    total = total + swap(total, "lo")
     parts = jnp.stack([total] + [shift(total, "z", step) for step in range(1, chips)])
     value = jnp.take(parts, (z - jnp.arange(chips)) % chips, axis=0).reshape(value.shape)
-    return double(double(value, "lo"), "core")
+    return double(value, "core")
 
 
 def pack_kernel(rows, out):
@@ -298,13 +328,12 @@
     )(blocks)
 
 
-def spread_leaves(leaves, rows):
+def spread_leaves(region, schur, rows):
     row_count, chips = 2 * lax.axis_size("hi"), lax.axis_size("z")
-    row, z, core = lax.axis_index("hi") * 2 + lax.axis_index("lo"), lax.axis_index("z"), lax.axis_index("core")
+    row, z = lax.axis_index("hi") * 2 + lax.axis_index("lo"), lax.axis_index("z")
     piece = 2 * rows // row_count
     half = chips // 2
-    width = half * 2 * rows
-    region = lax.dynamic_slice_in_dim(leaves, core * width, width, 0).reshape(half, row_count, piece, LEAF)
+    region = region.reshape(half, row_count, piece, LEAF)
 
     def part(step):
         return lax.dynamic_index_in_dim(region, (row + step) % row_count, 1, keepdims=False)
@@ -316,6 +345,7 @@
             for h in range(2):
                 route.append(((r * chips + r) * 2 + h, ((r + step) % row_count * chips + r) * 2 + h))
         share = share + lax.ppermute(part(step), ALL, route)
+    share = after(share, schur)
     received = []
     for turn in range(half):
         route = [
@@ -356,6 +386,7 @@
             col * (width // LEAF),
             row * (height // tile) - col * (width // tile),
             jnp.int32(width // tile),
+            col % (col_count // row_count) * (width // tile),
         ]
     )
 
@@ -380,11 +411,13 @@
     high, low, *product = weights(left_high, left_low, test_matrix, blocks)
 
     weight = (high, low)
-    partial = terms(place, first, partial, weight, product, test_matrix, 0, tile)
-    partial = terms(place, second, partial, weight, product, test_matrix, cut, tile)
+    partial, blocks = terms(place, first, partial, None, weight, product, test_matrix, 0, tile)
+    partial, blocks = terms(place, second, partial, blocks, weight, product, test_matrix, cut, tile)
     off_samples = lax.psum_scatter(partial, ("z", "core"), scatter_dimension=0, tiled=True)
-    schur, leaves = update(after(place, partial), (first, second), weight, front_trailing)
-    leaf_blocks = spread_leaves(leaves, per)
+
+    leaves = leaf_blocks_here(place, front_trailing, blocks, tile)
+    schur = update((first, second), (after(high, partial), low), front_trailing)
+    leaf_blocks = spread_leaves(leaves, schur, per)
     samples = after(off_samples, leaf_blocks)
     gram = group_sum(packed_gram(samples))
     group_gram = unpacked(gram, samples.shape[1], 2 * height)[None]

time: 334 us -> 327 us (0.979)
  starting transfers between devices: 34.8 us -> 28.9 us
  waiting for transfers between devices: 98.9 us -> 93.5 us
  Pallas kernels: 162 us -> 166 us
    ppermute x3, waiting for transfers between devices: 8.6 us -> 0.01 us  [spread_leaves(): share = share + lax.ppermute(part(step), ALL, route)]
    ppermute x6 -> x5, waiting for transfers between devices: 31.5 us -> 25.1 us  [swap(): return lax.ppermute(value, axis, [(0, 1), (1, 0)])]
    ppermute x2, waiting for transfers between devices: 6.45 us -> 10.6 us  [spread_leaves(): received.append(lax.ppermute(sent, ('z', 'core'), route))]
    pallas_call x3 -> x4, Pallas kernels: 95.6 us -> 99.7 us  [the longest x1 61.6 us: update(): pl.pallas_call(functools.partial(update_kernel, tiles), out_shape=jax.Sha...]
    ppermute x2, starting transfers between devices: 4.13 us -> 0.74 us  [spread_leaves(): received.append(lax.ppermute(sent, ('z', 'core'), route))]
    ppermute x6 -> x5, starting transfers between devices: 14.3 us -> 11.2 us  [swap(): return lax.ppermute(value, axis, [(0, 1), (1, 0)])]
  transfers between devices with their start and end apart: 24 -> 23, of which waited for: 19 -> 16; matrix products, arithmetic and copies ran while one was open for 5% -> 5% of each run, Pallas kernels for 45% -> 47%
where the time goes in v6:
time: 327 us
  Pallas kernels  166 us (51%)
  waiting for transfers between devices  93.5 us (29%)
  starting transfers between devices  28.9 us (9%)
  between operations  14.1 us (4%)
  matrix products  9.9 us (3%)
  local copies, waits for them, and re-layouts  9.54 us (3%)
  other arithmetic  4.3 us (1%)
    pallas_call x1, Pallas kernels, update(): pl.pallas_call(functools.partial(update_kernel, tiles), out_shape=jax.Sha...  61.6 us
    pallas_call x1, Pallas kernels, front_samples(): pl.pallas_call(samples_kernel, out_shape=jax.ShapeDtypeStruct((height, sa...  34.1 us
    pallas_call x2, Pallas kernels, terms(): pl.pallas_call(functools.partial(terms_kernel, base), out_shape=[jax.Shap...  33.3 us
    all_gather x1, waiting for transfers between devices, body(): lax.all_gather(panel_columns[:cut], ('z', 'core'), axis=0, tiled=False)  31.9 us
    pallas_call x1, Pallas kernels, weights(): pl.pallas_call(functools.partial(weights_kernel, len(blocks)), out_shape=...  27.4 us
    ppermute x5, waiting for transfers between devices, swap(): return lax.ppermute(value, axis, [(0, 1), (1, 0)])  25.1 us
    ppermute x8, waiting for transfers between devices, shift(): lax.ppermute(value, axis, [(at, (at + step) % count) for at in range(coun...  15.3 us
    ppermute x5, starting transfers between devices, swap(): return lax.ppermute(value, axis, [(0, 1), (1, 0)])  11.2 us
  transfers between devices with their start and end apart: 23, of which 16 were waited for; matrix products, arithmetic and copies ran while one was open for 5% of the time, Pallas kernels for 47%

profile of v6, /device:TPU:0, one launch (start us, length us, event | category | flops | bytes accessed | tf_op | source)
XLA Modules:
  0.0 326.6 jit_solution(6613271742141142807)
XLA Ops:
  7.2 2.9 slice.12
  10.2 3.0 collective-permute-start
  17.1 34.1 %samples.1.partial = f32[4096,512]{1,0:T(8,128)} custom-call(s32[5]{0:T(128)} %stack.67.place, f32[4096,2048]{1,0:T(8,128)} %front.5, f32[2048,512]{1,0:T(8,128)} %test.5), custom_call_target="tpu_custom_call" | custom-call | flops 25769803776 | bytes 33554432 | tf_op jit(solution)/shard_map/samples/pallas_call | solution.py:63
  51.3 7.8 %collective-permute-done.refs_4_ = f32[256,2048]{1,0:T(8,128)S(1)} collective-permute-done((f32[256,2048]{1,0:T(8,128)}, f32[256,2048]{1,0:T(8,128)S(1)}, u32[]{:S(2)}, u32[]{:S(2)}) %collective-permute-start) | collective-permute-done | bytes 2097184 | tf_op jit(solution)/shard_map/ppermute | solution.py:33
  65.4 6.1 %fusion.10.refs_0_ = bf16[1024,1024]{1,0:T(8,128)(2,1)} fusion(s32[1024]{0:T(1024)S(1)} %bitcast.81, s32[1024]{0:T(1024)S(1)} %copy-done.3, f32[1024,1024]{1,0:T(8,128)} %param.10), kind=kOutput, calls=%fused_computation.12 | convolution fusion | flops 2151677952 | bytes 6299648 | tf_op jit(solution)/shard_map/dot_general | solution.py:408
  71.5 3.8 %fusion.13.refs_1_ = bf16[1024,1024]{1,0:T(8,128)(2,1)} fusion(s32[1024]{0:T(1024)S(1)} %bitcast.82, s32[1024]{0:T(1024)S(1)} %copy-done.3, f32[1024,1024]{1,0:T(8,128)S(1)} %copy-done.1), kind=kOutput, calls=%fused_computation.13 | convolution fusion | flops 2152726528 | bytes 6299648 | tf_op jit(solution)/shard_map/dot_general | solution.py:408
  75.3 11.0 %collective-permute-done.3.refs_7_ = f32[128,2048]{1,0:T(8,128)S(1)} collective-permute-done((f32[128,2048]{1,0:T(8,128)S(1)}, f32[128,2048]{1,0:T(8,128)S(1)}, u32[]{:S(2)}, u32[]{:S(2)}) %collective-permute-start.3) | collective-permute-done | bytes 1048608 | tf_op jit(solution)/shard_map/ppermute | solution.py:33
  87.6 27.4 %weights.1 = (bf16[1024,2048]{1,0:T(8,128)(2,1)}, bf16[1024,2048]{1,0:T(8,128)(2,1)}, bf16[1024,512]{1,0:T(8,128)(2,1)}, bf16[1024,512]{1,0:T(8,128)(2,1)}) custom-call(bf16[1024,1024]{1,0:T(8,128)(2,1)} %fusion.10.refs_0_, bf16[1024,1024]{1,0:T(8,128)(2,1)} %fusion.13.refs_1_, f32[2048,512]{1,0:T(8,128)} %test.5, f32[256,2048]{1,0:T(8,128)} %refs_3_.1, ...), custom_call_target="tpu_custom_call" | custom-call | flops 19327352832 | bytes 16777216 | tf_op jit(solution)/shard_map/weights/pallas_call | solution.py:113
  115.0 31.9 %all-gather.5.cloned.1.call-done = f32[28672,128]{1,0:T(8,128)} async-done(((f32[3584,128]{1,0:T(8,128)}), f32[28672,128]{1,0:T(8,128)}) %all-gather.5.cloned.1.call-update) | async-done | bytes 14680080 | tf_op jit(solution)/shard_map/all_gather | solution.py:393
  146.9 26.1 %terms.2 = (f32[4096,512]{1,0:T(8,128)}, f32[4096,128]{1,0:T(8,128)}) custom-call(s32[5]{0:T(128)} %stack.67.place, f32[8,3584,128]{2,1,0:T(8,128)} %bitcast.83, f32[4096,512]{1,0:T(8,128)} %samples.1.partial, bf16[1024,512]{1,0:T(8,128)(2,1)} %get-tuple-element.24.product_high, ...), custom_call_target="tpu_custom_call", output_to_operand_aliasing={{0}: (2, {})} | custom-call | flops 11274289152 | bytes 29360128 | tf_op jit(solution)/shard_map/terms/pallas_call | solution.py:172
  173.0 3.4 %all-gather.7.cloned.1.call-done = f32[4096,128]{1,0:T(8,128)} async-done(((f32[512,128]{1,0:T(8,128)}), f32[4096,128]{1,0:T(8,128)}) %all-gather.7.cloned.1.call-update) | async-done | bytes 2097168 | tf_op jit(solution)/shard_map/all_gather | solution.py:397
  176.5 7.1 %terms.3 = (f32[4096,512]{1,0:T(8,128)}, f32[4096,128]{1,0:T(8,128)}) custom-call(s32[5]{0:T(128)} %stack.67.place, f32[8,512,128]{2,1,0:T(8,128)} %bitcast.68, f32[4096,512]{1,0:T(8,128)} %get-tuple-element.27.partial, bf16[1024,512]{1,0:T(8,128)(2,1)} %get-tuple-element.24.product_high, ...), custom_call_target="tpu_custom_call", output_to_operand_aliasing={{0}: (2, {}), {1}: (8, {})} | custom-call | flops 1610612736 | bytes 4194304 | tf_op jit(solution)/shard_map/terms/pallas_call | solution.py:172
  183.7 4.8 %leaves.1 = f32[2048,128]{1,0:T(8,128)} custom-call(s32[5]{0:T(128)} %stack.67.place, f32[4096,2048]{1,0:T(8,128)} %front.5, f32[4096,128]{1,0:T(8,128)} %get-tuple-element.31.blocks), custom_call_target="tpu_custom_call" | custom-call | flops 262144 | bytes 4194304 | tf_op jit(solution)/shard_map/leaves/pallas_call | solution.py:204
  189.6 3.4 %collective-permute-start.4 = (f32[2,256,128]{2,1,0:T(8,128)S(1)}, f32[2,256,128]{2,1,0:T(8,128)S(1)}, u32[]{:S(2)}, u32[]{:S(2)}) collective-permute-start(f32[2,256,128]{2,1,0:T(8,128)S(1)} %get-tuple-element.34), channel_id=1, source_target_pairs={{0,8},{1,9},{10,18},{11,19},{20,28},{21,29},{30,6},{31,7}} | collective-permute-start | bytes 786440 | tf_op jit(solution)/shard_map/ppermute | solution.py:347
  195.9 61.6 %update.1 = f32[4096,2048]{1,0:T(8,128)} custom-call(f32[8,3584,128]{2,1,0:T(8,128)} %bitcast.84, f32[8,512,128]{2,1,0:T(8,128)} %bitcast.69, bf16[1024,2048]{1,0:T(8,128)(2,1)} %get-tuple-element.30.high, bf16[1024,2048]{1,0:T(8,128)(2,1)} %get-tuple-element.26.low, f32[4096,2048]{1,0:T(8,128)} %front.5), custom_call_target="tpu_custom_call" | custom-call | flops 51539607552 | bytes 75497472 | tf_op jit(solution)/shard_map/update/pallas_call | solution.py:237
  259.5 10.6 %collective-permute-done.8 = f32[256,128]{1,0:T(8,128)S(1)} collective-permute-done((f32[256,128]{1,0:T(8,128)S(1)}, f32[256,128]{1,0:T(8,128)S(1)}, u32[]{:S(2)}, u32[]{:S(2)}) %collective-permute-start.8) | collective-permute-done | bytes 131104 | tf_op jit(solution)/shard_map/ppermute | solution.py:355
  270.9 4.2 %collective-permute-done.10 = f32[256,128]{1,0:T(8,128)S(1)} collective-permute-done((f32[256,128]{1,0:T(8,128)S(1)}, f32[256,128]{1,0:T(8,128)S(1)}, u32[]{:S(2)}, u32[]{:S(2)}) %collective-permute-start.10) | collective-permute-done | bytes 131104 | tf_op jit(solution)/shard_map/ppermute | solution.py:366
  278.8 2.9 gram.1
  282.7 5.4 %collective-permute-start.11 = (f32[640,128]{1,0:T(8,128)S(1)}, f32[640,128]{1,0:T(8,128)S(1)}, u32[]{:S(2)}, u32[]{:S(2)}) collective-permute-start(f32[640,128]{1,0:T(8,128)S(1)} %constant_dynamic-slice_fusion), channel_id=1, source_target_pairs={{0,1},{1,0},{2,3},{3,2},{4,5},{5,4},{6,7},{7,6},{8,9},{9,8},{10,11... | collective-permute-start | bytes 983048 | tf_op jit(solution)/shard_map/ppermute | solution.py:33
  290.5 3.8 %collective-permute-start.14 = (f32[160,128]{1,0:T(8,128)S(1)}, f32[160,128]{1,0:T(8,128)S(1)}, u32[]{:S(2)}, u32[]{:S(2)}) collective-permute-start(f32[160,128]{1,0:T(8,128)S(1)} %get-tuple-element.40), channel_id=1, source_target_pairs={{0,6},{2,0},{4,2},{6,4},{1,7},{3,1},{5,3},{7,5},{8,14},{10,8},{12,... | collective-permute-start | bytes 245768 | tf_op jit(solution)/shard_map/ppermute | solution.py:38
  294.5 3.0 collective-permute-done.12
  297.6 3.6 %collective-permute-done.13 = f32[160,128]{1,0:T(8,128)S(1)} collective-permute-done((f32[160,128]{1,0:T(8,128)S(1)}, f32[160,128]{1,0:T(8,128)S(1)}, u32[]{:S(2)}, u32[]{:S(2)}) %collective-permute-start.13) | collective-permute-done | bytes 81952 | tf_op jit(solution)/shard_map/ppermute | solution.py:38
  302.3 3.4 %collective-permute-done.15 = f32[160,128]{1,0:T(8,128)S(1)} collective-permute-done((f32[160,128]{1,0:T(8,128)S(1)}, f32[160,128]{1,0:T(8,128)S(1)}, u32[]{:S(2)}, u32[]{:S(2)}) %collective-permute-start.15) | collective-permute-done | bytes 81952 | tf_op jit(solution)/shard_map/ppermute | solution.py:33
  310.9 3.3 %collective-permute-done.17 = f32[160,128]{1,0:T(8,128)S(1)} collective-permute-done((f32[160,128]{1,0:T(8,128)S(1)}, f32[160,128]{1,0:T(8,128)S(1)}, u32[]{:S(2)}, u32[]{:S(2)}) %collective-permute-start.17) | collective-permute-done | bytes 81952 | tf_op jit(solution)/shard_map/ppermute | solution.py:38
  (72 shorter events, 37.6 us)
Async XLA Ops:
  7.2 139.8 %all-gather.5.cloned.1.call-start = ((), (), s32[]{:S(2)}) async-start(), calls=%async_computation.2 | async-start | bytes 16515072 | tf_op jit(solution)/shard_map/all_gather | solution.py:393
  10.1 166.3 %all-gather.7.cloned.1.call-start = ((), (), s32[]{:S(2)}) async-start(), calls=%async_computation.3 | async-start | bytes 2359296 | tf_op jit(solution)/shard_map/all_gather | solution.py:397
  10.2 48.8 %collective-permute-start = (f32[256,2048]{1,0:T(8,128)}, f32[256,2048]{1,0:T(8,128)S(1)}, u32[]{:S(2)}, u32[]{:S(2)}) collective-permute-start(f32[256,2048]{1,0:T(8,128)} %refs_3_.1), channel_id=1, source_target_pairs={{0,8},{8,0},{1,9},{9,1},{2,10},{10,2},{3,11},{11,3},{4,12},{12,4},... | collective-permute-start | bytes 6291464 | tf_op jit(solution)/shard_map/ppermute | solution.py:33
  13.2 47.4 %collective-permute-start.1 = (f32[256,2048]{1,0:T(8,128)}, f32[256,2048]{1,0:T(8,128)}, u32[]{:S(2)}, u32[]{:S(2)}) collective-permute-start(f32[256,2048]{1,0:T(8,128)} %refs_3_.1), channel_id=1, source_target_pairs={{0,16},{16,0},{1,17},{17,1},{2,18},{18,2},{3,19},{19,3},{4,20},{20... | collective-permute-start | bytes 6291464 | tf_op jit(solution)/shard_map/ppermute | solution.py:38
  51.3 14.1 %copy-start.3 = (s32[1024]{0:T(1024)S(1)}, s32[1024]{0:T(1024)}, u32[]{:S(2)}) copy-start(s32[1024]{0:T(1024)} %param.9) | copy-start | bytes 12292
  62.0 24.3 %collective-permute-start.3 = (f32[128,2048]{1,0:T(8,128)S(1)}, f32[128,2048]{1,0:T(8,128)S(1)}, u32[]{:S(2)}, u32[]{:S(2)}) collective-permute-start(f32[128,2048]{1,0:T(8,128)S(1)} %slice.15), channel_id=1, source_target_pairs={{0,8},{8,0},{1,9},{9,1},{2,10},{10,2},{3,11},{11,3},{4,12},{12,4},... | collective-permute-start | bytes 3145736 | tf_op jit(solution)/shard_map/ppermute | solution.py:33
  63.6 24.0 %collective-permute-start.2 = (f32[128,2048]{1,0:T(8,128)S(1)}, f32[128,2048]{1,0:T(8,128)}, u32[]{:S(2)}, u32[]{:S(2)}) collective-permute-start(f32[128,2048]{1,0:T(8,128)S(1)} %slice.14), channel_id=1, source_target_pairs={{0,16},{16,0},{1,17},{17,1},{2,18},{18,2},{3,19},{19,3},{4,20},{20... | collective-permute-start | bytes 3145736 | tf_op jit(solution)/shard_map/ppermute | solution.py:38
  65.1 213.7 %reduce-scatter.2.cloned.1.call-start = ((), (), s32[]{:S(2)}) async-start(), calls=%async_computation.1 | async-start | bytes 9437184 | tf_op jit(solution)/shard_map/reduce_scatter | solution.py:416
  189.6 67.9 %collective-permute-start.4 = (f32[2,256,128]{2,1,0:T(8,128)S(1)}, f32[2,256,128]{2,1,0:T(8,128)S(1)}, u32[]{:S(2)}, u32[]{:S(2)}) collective-permute-start(f32[2,256,128]{2,1,0:T(8,128)S(1)} %get-tuple-element.34), channel_id=1, source_target_pairs={{0,8},{1,9},{10,18},{11,19},{20,28},{21,29},{30,6},{31,7}} | collective-permute-start | bytes 786440 | tf_op jit(solution)/shard_map/ppermute | solution.py:347
  193.0 64.5 %collective-permute-start.6 = (f32[2,256,128]{2,1,0:T(8,128)S(1)}, f32[2,256,128]{2,1,0:T(8,128)S(1)}, u32[]{:S(2)}, u32[]{:S(2)}) collective-permute-start(f32[2,256,128]{2,1,0:T(8,128)S(1)} %get-tuple-element.35), channel_id=1, source_target_pairs={{0,24},{1,25},{10,2},{11,3},{20,12},{21,13},{30,22},{31,23}} | collective-permute-start | bytes 786440 | tf_op jit(solution)/shard_map/ppermute | solution.py:347
  194.6 63.0 %collective-permute-start.5 = (f32[2,256,128]{2,1,0:T(8,128)S(1)}, f32[2,256,128]{2,1,0:T(8,128)S(1)}, u32[]{:S(2)}, u32[]{:S(2)}) collective-permute-start(f32[2,256,128]{2,1,0:T(8,128)S(1)} %get-tuple-element.36), channel_id=1, source_target_pairs={{0,16},{1,17},{10,26},{11,27},{20,4},{21,5},{30,14},{31,15}} | collective-permute-start | bytes 786440 | tf_op jit(solution)/shard_map/ppermute | solution.py:347
  258.7 11.4 %collective-permute-start.8 = (f32[256,128]{1,0:T(8,128)S(1)}, f32[256,128]{1,0:T(8,128)S(1)}, u32[]{:S(2)}, u32[]{:S(2)}) collective-permute-start(f32[256,128]{1,0:T(8,128)S(1)} %get-tuple-element.46), channel_id=1, source_target_pairs={{0,2},{1,6},{2,0},{3,4},{4,3},{5,7},{6,1},{7,5},{8,10},{9,14},{10,... | collective-permute-start | bytes 393224 | tf_op jit(solution)/shard_map/ppermute | solution.py:355
  258.7 11.3 %collective-permute-start.7 = (f32[256,128]{1,0:T(8,128)S(1)}, f32[256,128]{1,0:T(8,128)S(1)}, u32[]{:S(2)}, u32[]{:S(2)}) collective-permute-start(f32[256,128]{1,0:T(8,128)S(1)} %get-tuple-element.47), channel_id=1, source_target_pairs={{0,0},{1,4},{2,2},{3,6},{4,1},{5,5},{6,3},{7,7},{8,8},{9,12},{10,1... | collective-permute-start | bytes 393224 | tf_op jit(solution)/shard_map/ppermute | solution.py:355
  270.1 5.0 %collective-permute-start.10 = (f32[256,128]{1,0:T(8,128)S(1)}, f32[256,128]{1,0:T(8,128)S(1)}, u32[]{:S(2)}, u32[]{:S(2)}) collective-permute-start(f32[256,128]{1,0:T(8,128)S(1)} %get-tuple-element.44), channel_id=1, source_target_pairs={{0,8},{1,24},{2,10},{3,26},{4,12},{5,28},{6,14},{7,30},{8,0},{9,16... | collective-permute-start | bytes 393224 | tf_op jit(solution)/shard_map/ppermute | solution.py:366
  270.2 5.0 %collective-permute-start.9 = (f32[256,128]{1,0:T(8,128)S(1)}, f32[256,128]{1,0:T(8,128)S(1)}, u32[]{:S(2)}, u32[]{:S(2)}) collective-permute-start(f32[256,128]{1,0:T(8,128)S(1)} %get-tuple-element.45), channel_id=1, source_target_pairs={{0,0},{1,16},{2,2},{3,18},{4,4},{5,20},{6,6},{7,22},{8,8},{9,24},{... | collective-permute-start | bytes 393224 | tf_op jit(solution)/shard_map/ppermute | solution.py:366
  282.7 6.7 %collective-permute-start.11 = (f32[640,128]{1,0:T(8,128)S(1)}, f32[640,128]{1,0:T(8,128)S(1)}, u32[]{:S(2)}, u32[]{:S(2)}) collective-permute-start(f32[640,128]{1,0:T(8,128)S(1)} %constant_dynamic-slice_fusion), channel_id=1, source_target_pairs={{0,1},{1,0},{2,3},{3,2},{4,5},{5,4},{6,7},{7,6},{8,9},{9,8},{10,11... | collective-permute-start | bytes 983048 | tf_op jit(solution)/shard_map/ppermute | solution.py:33
  290.4 7.1 %collective-permute-start.12 = (f32[160,128]{1,0:T(8,128)S(1)}, f32[160,128]{1,0:T(8,128)S(1)}, u32[]{:S(2)}, u32[]{:S(2)}) collective-permute-start(f32[160,128]{1,0:T(8,128)S(1)} %get-tuple-element.39), channel_id=1, source_target_pairs={{0,2},{2,4},{4,6},{6,0},{1,3},{3,5},{5,7},{7,1},{8,10},{10,12},{12... | collective-permute-start | bytes 245768 | tf_op jit(solution)/shard_map/ppermute | solution.py:38
  290.5 7.1 %collective-permute-start.14 = (f32[160,128]{1,0:T(8,128)S(1)}, f32[160,128]{1,0:T(8,128)S(1)}, u32[]{:S(2)}, u32[]{:S(2)}) collective-permute-start(f32[160,128]{1,0:T(8,128)S(1)} %get-tuple-element.40), channel_id=1, source_target_pairs={{0,6},{2,0},{4,2},{6,4},{1,7},{3,1},{5,3},{7,5},{8,14},{10,8},{12,... | collective-permute-start | bytes 245768 | tf_op jit(solution)/shard_map/ppermute | solution.py:38
  294.3 6.8 %collective-permute-start.13 = (f32[160,128]{1,0:T(8,128)S(1)}, f32[160,128]{1,0:T(8,128)S(1)}, u32[]{:S(2)}, u32[]{:S(2)}) collective-permute-start(f32[160,128]{1,0:T(8,128)S(1)} %get-tuple-element.41), channel_id=1, source_target_pairs={{0,4},{2,6},{4,0},{6,2},{1,5},{3,7},{5,1},{7,3},{8,12},{10,14},{12... | collective-permute-start | bytes 245768 | tf_op jit(solution)/shard_map/ppermute | solution.py:38
  301.1 4.5 %collective-permute-start.15 = (f32[160,128]{1,0:T(8,128)S(1)}, f32[160,128]{1,0:T(8,128)S(1)}, u32[]{:S(2)}, u32[]{:S(2)}) collective-permute-start(f32[160,128]{1,0:T(8,128)S(1)} %fusion.29), channel_id=1, source_target_pairs={{0,8},{8,0},{1,9},{9,1},{2,10},{10,2},{3,11},{11,3},{4,12},{12,4},... | collective-permute-start | bytes 245768 | tf_op jit(solution)/shard_map/ppermute | solution.py:33
  305.7 5.3 %collective-permute-start.18 = (f32[160,128]{1,0:T(8,128)S(1)}, f32[160,128]{1,0:T(8,128)S(1)}, u32[]{:S(2)}, u32[]{:S(2)}) collective-permute-start(f32[160,128]{1,0:T(8,128)S(1)} %add.264), channel_id=1, source_target_pairs={{0,6},{2,0},{4,2},{6,4},{1,7},{3,1},{5,3},{7,5},{8,14},{10,8},{12,... | collective-permute-start | bytes 245768 | tf_op jit(solution)/shard_map/ppermute | solution.py:38
  307.8 6.5 %collective-permute-start.17 = (f32[160,128]{1,0:T(8,128)S(1)}, f32[160,128]{1,0:T(8,128)S(1)}, u32[]{:S(2)}, u32[]{:S(2)}) collective-permute-start(f32[160,128]{1,0:T(8,128)S(1)} %add.264), channel_id=1, source_target_pairs={{0,4},{2,6},{4,0},{6,2},{1,5},{3,7},{5,1},{7,3},{8,12},{10,14},{12... | collective-permute-start | bytes 245768 | tf_op jit(solution)/shard_map/ppermute | solution.py:38
  307.8 6.5 %collective-permute-start.16 = (f32[160,128]{1,0:T(8,128)S(1)}, f32[160,128]{1,0:T(8,128)S(1)}, u32[]{:S(2)}, u32[]{:S(2)}) collective-permute-start(f32[160,128]{1,0:T(8,128)S(1)} %add.264), channel_id=1, source_target_pairs={{0,2},{2,4},{4,6},{6,0},{1,3},{3,5},{5,7},{7,1},{8,10},{10,12},{12... | collective-permute-start | bytes 245768 | tf_op jit(solution)/shard_map/ppermute | solution.py:38
  315.0 1.7 collective-permute-start.19
  (3 other events, 9.0 us)
Sparse Core Ops, SparseCore 0:
  10.3 136.6 all-gather.4
  149.1 27.3 all-gather.6
  183.7 95.0 reduce-scatter.1

commit v7 on v6

--- a/solution.py
+++ b/solution.py
@@ -254,22 +254,8 @@
     )(*chunks, *weight, front)
 
 
-def halve(value, axis):
-    half = value.shape[0] // 2
-    at = lax.axis_index(axis)
-    mine = lax.dynamic_slice_in_dim(value, at * half, half, 0)
-    return mine + swap(lax.dynamic_slice_in_dim(value, (1 - at) * half, half, 0), axis)
-
-
-def double(value, axis):
-    other = swap(value, axis)
-    first = lax.axis_index(axis) == 0
-    return jnp.concatenate([jnp.where(first, value, other), jnp.where(first, other, value)], axis=0)
-
-
-def group_sum(gram):
+def chips_sum(value):
     chips, z = lax.axis_size("z"), lax.axis_index("z")
-    value = halve(gram, "core")
     parts = value.reshape(chips, value.shape[0] // chips, value.shape[1])
     total = lax.dynamic_index_in_dim(parts, z, 0, keepdims=False)
     for step in range(1, chips):
@@ -277,11 +263,10 @@
         total = total + shift(part, "z", step)
     total = total + swap(total, "lo")
     parts = jnp.stack([total] + [shift(total, "z", step) for step in range(1, chips)])
-    value = jnp.take(parts, (z - jnp.arange(chips)) % chips, axis=0).reshape(value.shape)
-    return double(value, "core")
-
-
-def pack_kernel(rows, out):
+    return jnp.take(parts, (z - jnp.arange(chips)) % chips, axis=0).reshape(value.shape)
+
+
+def pack_kernel(core, rows, mine, other, blocks):
     high, low = split(rows[...])
     dot = functools.partial(
         lax.dot_general, dimension_numbers=(((0,), (0,)), ((), ())), preferred_element_type=F32
@@ -292,43 +277,56 @@
         part, rest = slice(start, start + LEAF), slice(start, size)
         value = dot(high[:, part], high[:, rest]) + (dot(high[:, part], low[:, rest]) + dot(low[:, part], high[:, rest]))
         for column in range(0, size - start, LEAF):
-            out[at : at + LEAF] = value[:, column : column + LEAF]
+            blocks[at : at + LEAF] = value[:, column : column + LEAF]
             at += LEAF
-
-
-def packed_gram(rows):
+    half = at // 2
+    first = core[0] == 0
+    mine[...] = jnp.where(first, blocks[:half], blocks[half:])
+    other[...] = jnp.where(first, blocks[half:], blocks[:half])
+
+
+def packed_gram(core, rows):
     size = rows.shape[1]
     count = size // LEAF
+    total = count * (count + 1) // 2 * LEAF
     return pl.pallas_call(
         pack_kernel,
-        out_shape=jax.ShapeDtypeStruct((count * (count + 1) // 2 * LEAF, LEAF), F32),
+        out_shape=[jax.ShapeDtypeStruct((total // 2, LEAF), F32)] * 2,
+        in_specs=[pl.BlockSpec(memory_space=pltpu.SMEM), pl.BlockSpec(memory_space=pltpu.VMEM)],
+        out_specs=[pl.BlockSpec(memory_space=pltpu.VMEM)] * 2,
+        scratch_shapes=[pltpu.VMEM((total, LEAF), F32)],
         compiler_params=pltpu.CompilerParams(vmem_limit_bytes=VMEM),
         name="gram",
-    )(rows)
-
-
-def unpack_kernel(divisor, blocks, out):
-    size = out.shape[0]
+    )(core, rows)
+
+
+def unpack_kernel(divisor, core, mine, other, out):
+    size, half = out.shape[0], mine.shape[0]
+    first = core[0] == 0
     at = 0
     for i in range(0, size, LEAF):
         for j in range(i, size, LEAF):
-            block = blocks[at : at + LEAF] / divisor
+            low = at < half
+            piece = slice(at % half, at % half + LEAF)
+            block = jnp.where(first == low, mine[piece], other[piece]) / divisor
             out[i : i + LEAF, j : j + LEAF] = block
             if j > i:
                 out[j : j + LEAF, i : i + LEAF] = block.T
             at += LEAF
 
 
-def unpacked(blocks, size, divisor):
+def unpacked(core, mine, other, size, divisor):
     return pl.pallas_call(
         functools.partial(unpack_kernel, float(divisor)),
         out_shape=jax.ShapeDtypeStruct((size, size), F32),
+        in_specs=[pl.BlockSpec(memory_space=pltpu.SMEM)] + [pl.BlockSpec(memory_space=pltpu.VMEM)] * 2,
+        out_specs=pl.BlockSpec(memory_space=pltpu.VMEM),
         compiler_params=pltpu.CompilerParams(vmem_limit_bytes=VMEM),
         name="unpack",
-    )(blocks)
-
-
-def spread_leaves(region, schur, rows):
+    )(core, mine, other)
+
+
+def leaves_to_rows(region, rows):
     row_count, chips = 2 * lax.axis_size("hi"), lax.axis_size("z")
     row, z = lax.axis_index("hi") * 2 + lax.axis_index("lo"), lax.axis_index("z")
     piece = 2 * rows // row_count
@@ -345,7 +343,12 @@
             for h in range(2):
                 route.append(((r * chips + r) * 2 + h, ((r + step) % row_count * chips + r) * 2 + h))
         share = share + lax.ppermute(part(step), ALL, route)
-    share = after(share, schur)
+    return share
+
+
+def leaves_along(share):
+    chips, z = lax.axis_size("z"), lax.axis_index("z")
+    half = chips // 2
     received = []
     for turn in range(half):
         route = [
@@ -353,6 +356,13 @@
         ]
         sent = lax.dynamic_index_in_dim(share, (z + turn) % half, 0, keepdims=False)
         received.append(lax.ppermute(sent, ("z", "core"), route))
+    return received
+
+
+def leaves_across(received):
+    row_count, chips = 2 * lax.axis_size("hi"), lax.axis_size("z")
+    row, z = lax.axis_index("hi") * 2 + lax.axis_index("lo"), lax.axis_index("z")
+    half = chips // 2
     stacked = jnp.stack(received)
     parts = []
     for turn in range(half):
@@ -416,11 +426,15 @@
     off_samples = lax.psum_scatter(partial, ("z", "core"), scatter_dimension=0, tiled=True)
 
     leaves = leaf_blocks_here(place, front_trailing, blocks, tile)
-    schur = update((first, second), (after(high, partial), low), front_trailing)
-    leaf_blocks = spread_leaves(leaves, schur, per)
-    samples = after(off_samples, leaf_blocks)
-    gram = group_sum(packed_gram(samples))
-    group_gram = unpacked(gram, samples.shape[1], 2 * height)[None]
+    share = leaves_to_rows(leaves, per)
+    received = leaves_along(share)
+    schur = update((first, second), (after(high, partial, share), low), front_trailing)
+    received = after(received, schur)
+    leaf_blocks = leaves_across(received)
+    cores = core.reshape(1)
+    mine, other = packed_gram(cores, after(off_samples, leaf_blocks))
+    mine = chips_sum(mine + swap(other, "core"))
+    group_gram = unpacked(cores, mine, swap(mine, "core"), off_samples.shape[1], 2 * height)[None]
     return (schur, off_samples, leaf_blocks, group_gram)
 
 

time: 327 us -> 324 us (level)
    ppermute x7, starting transfers between devices: 7.76 us -> 11.1 us  [the longest x3 6.29 us: leaves_to_rows(): share = share + lax.ppermute(part(step), ALL, route)]
  transfers between devices with their start and end apart: 23 -> 23, of which waited for: 16 -> 17; matrix products, arithmetic and copies ran while one was open for 5% -> 5% of each run, Pallas kernels for 47% -> 48%
where the time goes in v7:
time: 324 us; the launch traced here: 323 us
  Pallas kernels  166 us (51%)
  waiting for transfers between devices  91 us (28%)
  starting transfers between devices  29.6 us (9%)
  between operations  14.1 us (4%)
  matrix products  9.9 us (3%)
  local copies, waits for them, and re-layouts  9.32 us (3%)
  other arithmetic  3.24 us (1%)
    pallas_call x1, Pallas kernels, update(): pl.pallas_call(functools.partial(update_kernel, tiles), out_shape=jax.Sha...  61.5 us
    pallas_call x1, Pallas kernels, front_samples(): pl.pallas_call(samples_kernel, out_shape=jax.ShapeDtypeStruct((height, sa...  34.1 us
    pallas_call x2, Pallas kernels, terms(): pl.pallas_call(functools.partial(terms_kernel, base), out_shape=[jax.Shap...  33.3 us
    all_gather x1, waiting for transfers between devices, body(): lax.all_gather(panel_columns[:cut], ('z', 'core'), axis=0, tiled=False)  31.9 us
    pallas_call x1, Pallas kernels, weights(): pl.pallas_call(functools.partial(weights_kernel, len(blocks)), out_shape=...  27.4 us
    ppermute x5, waiting for transfers between devices, swap(): return lax.ppermute(value, axis, [(0, 1), (1, 0)])  24.8 us
    ppermute x8, waiting for transfers between devices, shift(): lax.ppermute(value, axis, [(at, (at + step) % count) for at in range(coun...  16.4 us
    dot_general x2, matrix products, body(): jnp.dot(part, chosen, preferred_element_type=F32).astype(BF16)  9.9 us
  transfers between devices with their start and end apart: 23, of which 17 were waited for; matrix products, arithmetic and copies ran while one was open for 5% of the time, Pallas kernels for 48%

profile of v7, /device:TPU:0, one launch (start us, length us, event | category | flops | bytes accessed | tf_op | source)
XLA Modules:
  0.0 323.4 jit_solution(7032565511908227805)
XLA Ops:
  7.2 2.9 slice.12
  10.2 3.0 collective-permute-start
  17.2 34.1 %samples.1.partial = f32[4096,512]{1,0:T(8,128)} custom-call(s32[5]{0:T(128)} %stack.67.place, f32[4096,2048]{1,0:T(8,128)} %front.5, f32[2048,512]{1,0:T(8,128)} %test.5), custom_call_target="tpu_custom_call" | custom-call | flops 25769803776 | bytes 33554432 | tf_op jit(solution)/shard_map/samples/pallas_call | solution.py:63
  51.3 7.7 %collective-permute-done.refs_4_ = f32[256,2048]{1,0:T(8,128)S(1)} collective-permute-done((f32[256,2048]{1,0:T(8,128)}, f32[256,2048]{1,0:T(8,128)S(1)}, u32[]{:S(2)}, u32[]{:S(2)}) %collective-permute-start) | collective-permute-done | bytes 2097184 | tf_op jit(solution)/shard_map/ppermute | solution.py:33
  65.4 6.1 %fusion.10.refs_0_ = bf16[1024,1024]{1,0:T(8,128)(2,1)} fusion(s32[1024]{0:T(1024)S(1)} %bitcast.80, s32[1024]{0:T(1024)S(1)} %copy-done.5, f32[1024,1024]{1,0:T(8,128)} %param.10), kind=kOutput, calls=%fused_computation.12 | convolution fusion | flops 2151677952 | bytes 6299648 | tf_op jit(solution)/shard_map/dot_general | solution.py:418
  71.5 3.8 %fusion.13.refs_1_ = bf16[1024,1024]{1,0:T(8,128)(2,1)} fusion(s32[1024]{0:T(1024)S(1)} %bitcast.81, s32[1024]{0:T(1024)S(1)} %copy-done.5, f32[1024,1024]{1,0:T(8,128)S(1)} %copy-done.3), kind=kOutput, calls=%fused_computation.13 | convolution fusion | flops 2152726528 | bytes 6299648 | tf_op jit(solution)/shard_map/dot_general | solution.py:418
  75.3 11.0 %collective-permute-done.3.refs_7_ = f32[128,2048]{1,0:T(8,128)S(1)} collective-permute-done((f32[128,2048]{1,0:T(8,128)S(1)}, f32[128,2048]{1,0:T(8,128)S(1)}, u32[]{:S(2)}, u32[]{:S(2)}) %collective-permute-start.3) | collective-permute-done | bytes 1048608 | tf_op jit(solution)/shard_map/ppermute | solution.py:33
  87.6 27.4 %weights.1 = (bf16[1024,2048]{1,0:T(8,128)(2,1)}, bf16[1024,2048]{1,0:T(8,128)(2,1)}, bf16[1024,512]{1,0:T(8,128)(2,1)}, bf16[1024,512]{1,0:T(8,128)(2,1)}) custom-call(bf16[1024,1024]{1,0:T(8,128)(2,1)} %fusion.10.refs_0_, bf16[1024,1024]{1,0:T(8,128)(2,1)} %fusion.13.refs_1_, f32[2048,512]{1,0:T(8,128)} %test.5, f32[256,2048]{1,0:T(8,128)} %refs_3_.1, ...), custom_call_target="tpu_custom_call" | custom-call | flops 19327352832 | bytes 16777216 | tf_op jit(solution)/shard_map/weights/pallas_call | solution.py:113
  115.0 31.9 %all-gather.5.cloned.1.call-done = f32[28672,128]{1,0:T(8,128)} async-done(((f32[3584,128]{1,0:T(8,128)}), f32[28672,128]{1,0:T(8,128)}) %all-gather.5.cloned.1.call-update) | async-done | bytes 14680080 | tf_op jit(solution)/shard_map/all_gather | solution.py:403
  146.9 26.1 %terms.2 = (f32[4096,512]{1,0:T(8,128)}, f32[4096,128]{1,0:T(8,128)}) custom-call(s32[5]{0:T(128)} %stack.67.place, f32[8,3584,128]{2,1,0:T(8,128)} %bitcast.82, f32[4096,512]{1,0:T(8,128)} %samples.1.partial, bf16[1024,512]{1,0:T(8,128)(2,1)} %get-tuple-element.27.product_high, ...), custom_call_target="tpu_custom_call", output_to_operand_aliasing={{0}: (2, {})} | custom-call | flops 11274289152 | bytes 29360128 | tf_op jit(solution)/shard_map/terms/pallas_call | solution.py:172
  173.0 3.4 %all-gather.7.cloned.1.call-done = f32[4096,128]{1,0:T(8,128)} async-done(((f32[512,128]{1,0:T(8,128)}), f32[4096,128]{1,0:T(8,128)}) %all-gather.7.cloned.1.call-update) | async-done | bytes 2097168 | tf_op jit(solution)/shard_map/all_gather | solution.py:407
  176.4 7.1 %terms.3 = (f32[4096,512]{1,0:T(8,128)}, f32[4096,128]{1,0:T(8,128)}) custom-call(s32[5]{0:T(128)} %stack.67.place, f32[8,512,128]{2,1,0:T(8,128)} %bitcast.67, f32[4096,512]{1,0:T(8,128)} %get-tuple-element.30.partial, bf16[1024,512]{1,0:T(8,128)(2,1)} %get-tuple-element.27.product_high, ...), custom_call_target="tpu_custom_call", output_to_operand_aliasing={{0}: (2, {}), {1}: (8, {})} | custom-call | flops 1610612736 | bytes 4194304 | tf_op jit(solution)/shard_map/terms/pallas_call | solution.py:172
  183.6 4.8 %leaves.1 = f32[2048,128]{1,0:T(8,128)} custom-call(s32[5]{0:T(128)} %stack.67.place, f32[4096,2048]{1,0:T(8,128)} %front.5, f32[4096,128]{1,0:T(8,128)} %get-tuple-element.33.blocks), custom_call_target="tpu_custom_call" | custom-call | flops 262144 | bytes 4194304 | tf_op jit(solution)/shard_map/leaves/pallas_call | solution.py:204
  189.6 3.4 %collective-permute-start.4 = (f32[2,256,128]{2,1,0:T(8,128)S(1)}, f32[2,256,128]{2,1,0:T(8,128)S(1)}, u32[]{:S(2)}, u32[]{:S(2)}) collective-permute-start(f32[2,256,128]{2,1,0:T(8,128)S(1)} %get-tuple-element.40), channel_id=1, source_target_pairs={{0,8},{1,9},{10,18},{11,19},{20,28},{21,29},{30,6},{31,7}} | collective-permute-start | bytes 786440 | tf_op jit(solution)/shard_map/ppermute | solution.py:345
  196.0 3.6 %collective-permute-done.4 = f32[2,256,128]{2,1,0:T(8,128)S(1)} collective-permute-done((f32[2,256,128]{2,1,0:T(8,128)S(1)}, f32[2,256,128]{2,1,0:T(8,128)S(1)}, u32[]{:S(2)}, u32[]{:S(2)}) %collective-permute-start.4) | collective-permute-done | bytes 262176 | tf_op jit(solution)/shard_map/ppermute | solution.py:345
  199.6 5.2 %collective-permute-done.6 = f32[2,256,128]{2,1,0:T(8,128)S(1)} collective-permute-done((f32[2,256,128]{2,1,0:T(8,128)S(1)}, f32[2,256,128]{2,1,0:T(8,128)S(1)}, u32[]{:S(2)}, u32[]{:S(2)}) %collective-permute-start.6) | collective-permute-done | bytes 262176 | tf_op jit(solution)/shard_map/ppermute | solution.py:345
  205.9 3.4 %collective-permute-start.8 = (f32[256,128]{1,0:T(8,128)S(1)}, f32[256,128]{1,0:T(8,128)S(1)}, u32[]{:S(2)}, u32[]{:S(2)}) collective-permute-start(f32[256,128]{1,0:T(8,128)S(1)} %get-tuple-element.50), channel_id=1, source_target_pairs={{0,2},{1,6},{2,0},{3,4},{4,3},{5,7},{6,1},{7,5},{8,10},{9,14},{10,... | collective-permute-start | bytes 393224 | tf_op jit(solution)/shard_map/ppermute | solution.py:358
  210.0 61.5 %update.1 = f32[4096,2048]{1,0:T(8,128)} custom-call(f32[8,3584,128]{2,1,0:T(8,128)} %bitcast.83, f32[8,512,128]{2,1,0:T(8,128)} %bitcast.68, bf16[1024,2048]{1,0:T(8,128)(2,1)} %get-tuple-element.34.high, bf16[1024,2048]{1,0:T(8,128)(2,1)} %get-tuple-element.29.low, f32[4096,2048]{1,0:T(8,128)} %front.5), custom_call_target="tpu_custom_call" | custom-call | flops 51539607552 | bytes 75497472 | tf_op jit(solution)/shard_map/update/pallas_call | solution.py:237
  272.4 5.3 %collective-permute-done.10 = f32[256,128]{1,0:T(8,128)S(1)} collective-permute-done((f32[256,128]{1,0:T(8,128)S(1)}, f32[256,128]{1,0:T(8,128)S(1)}, u32[]{:S(2)}, u32[]{:S(2)}) %collective-permute-start.10) | collective-permute-done | bytes 131104 | tf_op jit(solution)/shard_map/ppermute | solution.py:376
  287.3 3.4 %collective-permute-start.14 = (f32[160,128]{1,0:T(8,128)S(1)}, f32[160,128]{1,0:T(8,128)S(1)}, u32[]{:S(2)}, u32[]{:S(2)}) collective-permute-start(f32[160,128]{1,0:T(8,128)S(1)} %get-tuple-element.44), channel_id=1, source_target_pairs={{0,6},{2,0},{4,2},{6,4},{1,7},{3,1},{5,3},{7,5},{8,14},{10,8},{12,... | collective-permute-start | bytes 245768 | tf_op jit(solution)/shard_map/ppermute | solution.py:38
  290.9 3.1 collective-permute-done.12
  294.0 4.2 %collective-permute-done.13 = f32[160,128]{1,0:T(8,128)S(1)} collective-permute-done((f32[160,128]{1,0:T(8,128)S(1)}, f32[160,128]{1,0:T(8,128)S(1)}, u32[]{:S(2)}, u32[]{:S(2)}) %collective-permute-start.13) | collective-permute-done | bytes 81952 | tf_op jit(solution)/shard_map/ppermute | solution.py:38
  299.8 2.9 collective-permute-done.15
  305.1 3.9 %collective-permute-done.18 = f32[160,128]{1,0:T(8,128)S(1)} collective-permute-done((f32[160,128]{1,0:T(8,128)S(1)}, f32[160,128]{1,0:T(8,128)S(1)}, u32[]{:S(2)}, u32[]{:S(2)}) %collective-permute-start.18) | collective-permute-done | bytes 81952 | tf_op jit(solution)/shard_map/ppermute | solution.py:38
  (73 shorter events, 39.9 us)
Async XLA Ops:
  7.2 139.7 %all-gather.5.cloned.1.call-start = ((), (), s32[]{:S(2)}) async-start(), calls=%async_computation.2 | async-start | bytes 16515072 | tf_op jit(solution)/shard_map/all_gather | solution.py:403
  10.1 166.3 %all-gather.7.cloned.1.call-start = ((), (), s32[]{:S(2)}) async-start(), calls=%async_computation.3 | async-start | bytes 2359296 | tf_op jit(solution)/shard_map/all_gather | solution.py:407
  10.2 48.8 %collective-permute-start = (f32[256,2048]{1,0:T(8,128)}, f32[256,2048]{1,0:T(8,128)S(1)}, u32[]{:S(2)}, u32[]{:S(2)}) collective-permute-start(f32[256,2048]{1,0:T(8,128)} %refs_3_.1), channel_id=1, source_target_pairs={{0,8},{8,0},{1,9},{9,1},{2,10},{10,2},{3,11},{11,3},{4,12},{12,4},... | collective-permute-start | bytes 6291464 | tf_op jit(solution)/shard_map/ppermute | solution.py:33
  13.2 47.4 %collective-permute-start.1 = (f32[256,2048]{1,0:T(8,128)}, f32[256,2048]{1,0:T(8,128)}, u32[]{:S(2)}, u32[]{:S(2)}) collective-permute-start(f32[256,2048]{1,0:T(8,128)} %refs_3_.1), channel_id=1, source_target_pairs={{0,16},{16,0},{1,17},{17,1},{2,18},{18,2},{3,19},{19,3},{4,20},{20... | collective-permute-start | bytes 6291464 | tf_op jit(solution)/shard_map/ppermute | solution.py:38
  51.3 14.1 %copy-start.5 = (s32[1024]{0:T(1024)S(1)}, s32[1024]{0:T(1024)}, u32[]{:S(2)}) copy-start(s32[1024]{0:T(1024)} %param.9) | copy-start | bytes 12292
  62.0 24.3 %collective-permute-start.3 = (f32[128,2048]{1,0:T(8,128)S(1)}, f32[128,2048]{1,0:T(8,128)S(1)}, u32[]{:S(2)}, u32[]{:S(2)}) collective-permute-start(f32[128,2048]{1,0:T(8,128)S(1)} %slice.15), channel_id=1, source_target_pairs={{0,8},{8,0},{1,9},{9,1},{2,10},{10,2},{3,11},{11,3},{4,12},{12,4},... | collective-permute-start | bytes 3145736 | tf_op jit(solution)/shard_map/ppermute | solution.py:33
  63.6 24.0 %collective-permute-start.2 = (f32[128,2048]{1,0:T(8,128)S(1)}, f32[128,2048]{1,0:T(8,128)}, u32[]{:S(2)}, u32[]{:S(2)}) collective-permute-start(f32[128,2048]{1,0:T(8,128)S(1)} %slice.14), channel_id=1, source_target_pairs={{0,16},{16,0},{1,17},{17,1},{2,18},{18,2},{3,19},{19,3},{4,20},{20... | collective-permute-start | bytes 3145736 | tf_op jit(solution)/shard_map/ppermute | solution.py:38
  65.1 213.6 %reduce-scatter.2.cloned.1.call-start = ((), (), s32[]{:S(2)}) async-start(), calls=%async_computation.1 | async-start | bytes 9437184 | tf_op jit(solution)/shard_map/reduce_scatter | solution.py:426
  189.6 10.0 %collective-permute-start.4 = (f32[2,256,128]{2,1,0:T(8,128)S(1)}, f32[2,256,128]{2,1,0:T(8,128)S(1)}, u32[]{:S(2)}, u32[]{:S(2)}) collective-permute-start(f32[2,256,128]{2,1,0:T(8,128)S(1)} %get-tuple-element.40), channel_id=1, source_target_pairs={{0,8},{1,9},{10,18},{11,19},{20,28},{21,29},{30,6},{31,7}} | collective-permute-start | bytes 786440 | tf_op jit(solution)/shard_map/ppermute | solution.py:345
  193.0 11.8 %collective-permute-start.6 = (f32[2,256,128]{2,1,0:T(8,128)S(1)}, f32[2,256,128]{2,1,0:T(8,128)S(1)}, u32[]{:S(2)}, u32[]{:S(2)}) collective-permute-start(f32[2,256,128]{2,1,0:T(8,128)S(1)} %get-tuple-element.41), channel_id=1, source_target_pairs={{0,24},{1,25},{10,2},{11,3},{20,12},{21,13},{30,22},{31,23}} | collective-permute-start | bytes 786440 | tf_op jit(solution)/shard_map/ppermute | solution.py:345
  194.6 10.2 %collective-permute-start.5 = (f32[2,256,128]{2,1,0:T(8,128)S(1)}, f32[2,256,128]{2,1,0:T(8,128)S(1)}, u32[]{:S(2)}, u32[]{:S(2)}) collective-permute-start(f32[2,256,128]{2,1,0:T(8,128)S(1)} %get-tuple-element.42), channel_id=1, source_target_pairs={{0,16},{1,17},{10,26},{11,27},{20,4},{21,5},{30,14},{31,15}} | collective-permute-start | bytes 786440 | tf_op jit(solution)/shard_map/ppermute | solution.py:345
  205.9 65.7 %collective-permute-start.8 = (f32[256,128]{1,0:T(8,128)S(1)}, f32[256,128]{1,0:T(8,128)S(1)}, u32[]{:S(2)}, u32[]{:S(2)}) collective-permute-start(f32[256,128]{1,0:T(8,128)S(1)} %get-tuple-element.50), channel_id=1, source_target_pairs={{0,2},{1,6},{2,0},{3,4},{4,3},{5,7},{6,1},{7,5},{8,10},{9,14},{10,... | collective-permute-start | bytes 393224 | tf_op jit(solution)/shard_map/ppermute | solution.py:358
  209.3 62.2 %collective-permute-start.7 = (f32[256,128]{1,0:T(8,128)S(1)}, f32[256,128]{1,0:T(8,128)S(1)}, u32[]{:S(2)}, u32[]{:S(2)}) collective-permute-start(f32[256,128]{1,0:T(8,128)S(1)} %get-tuple-element.51), channel_id=1, source_target_pairs={{0,0},{1,4},{2,2},{3,6},{4,1},{5,5},{6,3},{7,7},{8,8},{9,12},{10,1... | collective-permute-start | bytes 393224 | tf_op jit(solution)/shard_map/ppermute | solution.py:358
  271.6 6.1 %collective-permute-start.10 = (f32[256,128]{1,0:T(8,128)S(1)}, f32[256,128]{1,0:T(8,128)S(1)}, u32[]{:S(2)}, u32[]{:S(2)}) collective-permute-start(f32[256,128]{1,0:T(8,128)S(1)} %get-tuple-element.48), channel_id=1, source_target_pairs={{0,8},{1,24},{2,10},{3,26},{4,12},{5,28},{6,14},{7,30},{8,0},{9,16... | collective-permute-start | bytes 393224 | tf_op jit(solution)/shard_map/ppermute | solution.py:376
  271.7 6.0 %collective-permute-start.9 = (f32[256,128]{1,0:T(8,128)S(1)}, f32[256,128]{1,0:T(8,128)S(1)}, u32[]{:S(2)}, u32[]{:S(2)}) collective-permute-start(f32[256,128]{1,0:T(8,128)S(1)} %get-tuple-element.49), channel_id=1, source_target_pairs={{0,0},{1,16},{2,2},{3,18},{4,4},{5,20},{6,6},{7,22},{8,8},{9,24},{... | collective-permute-start | bytes 393224 | tf_op jit(solution)/shard_map/ppermute | solution.py:376
  281.7 4.1 %collective-permute-start.11 = (f32[640,128]{1,0:T(8,128)}, f32[640,128]{1,0:T(8,128)S(1)}, u32[]{:S(2)}, u32[]{:S(2)}) collective-permute-start(f32[640,128]{1,0:T(8,128)} %get-tuple-element.39), channel_id=1, source_target_pairs={{0,1},{1,0},{2,3},{3,2},{4,5},{5,4},{6,7},{7,6},{8,9},{9,8},{10,11... | collective-permute-start | bytes 983048 | tf_op jit(solution)/shard_map/ppermute | solution.py:33
  286.8 7.2 %collective-permute-start.12 = (f32[160,128]{1,0:T(8,128)S(1)}, f32[160,128]{1,0:T(8,128)S(1)}, u32[]{:S(2)}, u32[]{:S(2)}) collective-permute-start(f32[160,128]{1,0:T(8,128)S(1)} %get-tuple-element.43), channel_id=1, source_target_pairs={{0,2},{2,4},{4,6},{6,0},{1,3},{3,5},{5,7},{7,1},{8,10},{10,12},{12... | collective-permute-start | bytes 245768 | tf_op jit(solution)/shard_map/ppermute | solution.py:38
  287.3 6.7 %collective-permute-start.14 = (f32[160,128]{1,0:T(8,128)S(1)}, f32[160,128]{1,0:T(8,128)S(1)}, u32[]{:S(2)}, u32[]{:S(2)}) collective-permute-start(f32[160,128]{1,0:T(8,128)S(1)} %get-tuple-element.44), channel_id=1, source_target_pairs={{0,6},{2,0},{4,2},{6,4},{1,7},{3,1},{5,3},{7,5},{8,14},{10,8},{12,... | collective-permute-start | bytes 245768 | tf_op jit(solution)/shard_map/ppermute | solution.py:38
  290.7 7.5 %collective-permute-start.13 = (f32[160,128]{1,0:T(8,128)S(1)}, f32[160,128]{1,0:T(8,128)S(1)}, u32[]{:S(2)}, u32[]{:S(2)}) collective-permute-start(f32[160,128]{1,0:T(8,128)S(1)} %get-tuple-element.45), channel_id=1, source_target_pairs={{0,4},{2,6},{4,0},{6,2},{1,5},{3,7},{5,1},{7,3},{8,12},{10,14},{12... | collective-permute-start | bytes 245768 | tf_op jit(solution)/shard_map/ppermute | solution.py:38
  298.2 4.5 %collective-permute-start.15 = (f32[160,128]{1,0:T(8,128)S(1)}, f32[160,128]{1,0:T(8,128)S(1)}, u32[]{:S(2)}, u32[]{:S(2)}) collective-permute-start(f32[160,128]{1,0:T(8,128)S(1)} %fusion.29), channel_id=1, source_target_pairs={{0,8},{8,0},{1,9},{9,1},{2,10},{10,2},{3,11},{11,3},{4,12},{12,4},... | collective-permute-start | bytes 245768 | tf_op jit(solution)/shard_map/ppermute | solution.py:33
  302.8 6.2 %collective-permute-start.18 = (f32[160,128]{1,0:T(8,128)S(1)}, f32[160,128]{1,0:T(8,128)S(1)}, u32[]{:S(2)}, u32[]{:S(2)}) collective-permute-start(f32[160,128]{1,0:T(8,128)S(1)} %add.257), channel_id=1, source_target_pairs={{0,6},{2,0},{4,2},{6,4},{1,7},{3,1},{5,3},{7,5},{8,14},{10,8},{12,... | collective-permute-start | bytes 245768 | tf_op jit(solution)/shard_map/ppermute | solution.py:38
  304.5 7.0 %collective-permute-start.17 = (f32[160,128]{1,0:T(8,128)S(1)}, f32[160,128]{1,0:T(8,128)S(1)}, u32[]{:S(2)}, u32[]{:S(2)}) collective-permute-start(f32[160,128]{1,0:T(8,128)S(1)} %add.257), channel_id=1, source_target_pairs={{0,4},{2,6},{4,0},{6,2},{1,5},{3,7},{5,1},{7,3},{8,12},{10,14},{12... | collective-permute-start | bytes 245768 | tf_op jit(solution)/shard_map/ppermute | solution.py:38
  304.5 7.0 %collective-permute-start.16 = (f32[160,128]{1,0:T(8,128)S(1)}, f32[160,128]{1,0:T(8,128)S(1)}, u32[]{:S(2)}, u32[]{:S(2)}) collective-permute-start(f32[160,128]{1,0:T(8,128)S(1)} %add.257), channel_id=1, source_target_pairs={{0,2},{2,4},{4,6},{6,0},{1,3},{3,5},{5,7},{7,1},{8,10},{10,12},{12... | collective-permute-start | bytes 245768 | tf_op jit(solution)/shard_map/ppermute | solution.py:38
  312.2 1.7 collective-permute-start.19
  (5 other events, 11.4 us)
Sparse Core Ops, SparseCore 0:
  10.3 136.6 all-gather.4
  149.1 27.3 all-gather.6
  183.7 94.9 reduce-scatter.1

commit v8 on v7

--- a/solution.py
+++ b/solution.py
@@ -422,7 +422,9 @@
 
     weight = (high, low)
     partial, blocks = terms(place, first, partial, None, weight, product, test_matrix, 0, tile)
-    partial, blocks = terms(place, second, partial, blocks, weight, product, test_matrix, cut, tile)
+    small = tile // 2
+    fine = place.at[2].set(row * (height // small) - col * (width // small)).at[3].set(width // small)
+    partial, blocks = terms(fine, second, partial, blocks, weight, product, test_matrix, cut, small)
     off_samples = lax.psum_scatter(partial, ("z", "core"), scatter_dimension=0, tiled=True)
 
     leaves = leaf_blocks_here(place, front_trailing, blocks, tile)

time: 324 us -> 323 us (level)
  transfers between devices with their start and end apart: 23 -> 23, of which waited for: 17 -> 17; matrix products, arithmetic and copies ran while one was open for 5% -> 6% of each run, Pallas kernels for 48% -> 48%
where the time goes in v8:
time: 323 us
  Pallas kernels  165 us (51%)
  waiting for transfers between devices  88.6 us (27%)
  starting transfers between devices  29.9 us (9%)
  between operations  14.1 us (4%)
  matrix products  12 us (4%)
  local copies, waits for them, and re-layouts  9.35 us (3%)
  other arithmetic  3.24 us (1%)
    pallas_call x1, Pallas kernels, update(): pl.pallas_call(functools.partial(update_kernel, tiles), out_shape=jax.Sha...  61.5 us
    pallas_call x1, Pallas kernels, front_samples(): pl.pallas_call(samples_kernel, out_shape=jax.ShapeDtypeStruct((height, sa...  34.1 us
    pallas_call x2, Pallas kernels, terms(): pl.pallas_call(functools.partial(terms_kernel, base), out_shape=[jax.Shap...  32.2 us
    all_gather x1, waiting for transfers between devices, body(): lax.all_gather(panel_columns[:cut], ('z', 'core'), axis=0, tiled=False)  31.7 us
    pallas_call x1, Pallas kernels, weights(): pl.pallas_call(functools.partial(weights_kernel, len(blocks)), out_shape=...  27.6 us
    ppermute x5, waiting for transfers between devices, swap(): return lax.ppermute(value, axis, [(0, 1), (1, 0)])  22.6 us
    ppermute x8, waiting for transfers between devices, shift(): lax.ppermute(value, axis, [(at, (at + step) % count) for at in range(coun...  16.1 us
    dot_general x2, matrix products, body(): jnp.dot(part, chosen, preferred_element_type=F32).astype(BF16)  12 us
  transfers between devices with their start and end apart: 23, of which 17 were waited for; matrix products, arithmetic and copies ran while one was open for 6% of the time, Pallas kernels for 48%

profile of v8, /device:TPU:0, one launch (start us, length us, event | category | flops | bytes accessed | tf_op | source)
XLA Modules:
  0.0 322.5 jit_solution(4824998674324190944)
XLA Ops:
  7.2 2.9 slice.32
  10.2 3.0 collective-permute-start
  17.2 34.1 %samples.1.partial = f32[4096,512]{1,0:T(8,128)} custom-call(s32[5]{0:T(128)} %stack.67.place, f32[4096,2048]{1,0:T(8,128)} %front.5, f32[2048,512]{1,0:T(8,128)} %test.5), custom_call_target="tpu_custom_call" | custom-call | flops 25769803776 | bytes 33554432 | tf_op jit(solution)/shard_map/samples/pallas_call | solution.py:63
  51.3 7.7 %collective-permute-done.refs_4_ = f32[256,2048]{1,0:T(8,128)S(1)} collective-permute-done((f32[256,2048]{1,0:T(8,128)}, f32[256,2048]{1,0:T(8,128)S(1)}, u32[]{:S(2)}, u32[]{:S(2)}) %collective-permute-start) | collective-permute-done | bytes 2097184 | tf_op jit(solution)/shard_map/ppermute | solution.py:33
  65.2 6.0 %fusion.10.refs_0_ = bf16[1024,1024]{1,0:T(8,128)(2,1)} fusion(s32[1024]{0:T(1024)S(1)} %bitcast.81, s32[1024]{0:T(1024)S(1)} %copy-done.5, f32[1024,1024]{1,0:T(8,128)} %param.14), kind=kOutput, calls=%fused_computation.12 | convolution fusion | flops 2151677952 | bytes 6299648 | tf_op jit(solution)/shard_map/dot_general | solution.py:418
  71.2 6.0 %fusion.13.refs_1_ = bf16[1024,1024]{1,0:T(8,128)(2,1)} fusion(s32[1024]{0:T(1024)S(1)} %bitcast.82, s32[1024]{0:T(1024)S(1)} %copy-done.5, f32[1024,1024]{1,0:T(8,128)} %param.14), kind=kOutput, calls=%fused_computation.13 | convolution fusion | flops 2152726528 | bytes 6299648 | tf_op jit(solution)/shard_map/dot_general | solution.py:418
  77.2 9.2 %collective-permute-done.3.refs_7_ = f32[128,2048]{1,0:T(8,128)} collective-permute-done((f32[128,2048]{1,0:T(8,128)S(1)}, f32[128,2048]{1,0:T(8,128)}, u32[]{:S(2)}, u32[]{:S(2)}) %collective-permute-start.3) | collective-permute-done | bytes 1048608 | tf_op jit(solution)/shard_map/ppermute | solution.py:33
  87.6 27.6 %weights.1 = (bf16[1024,2048]{1,0:T(8,128)(2,1)}, bf16[1024,2048]{1,0:T(8,128)(2,1)}, bf16[1024,512]{1,0:T(8,128)(2,1)}, bf16[1024,512]{1,0:T(8,128)(2,1)}) custom-call(bf16[1024,1024]{1,0:T(8,128)(2,1)} %fusion.10.refs_0_, bf16[1024,1024]{1,0:T(8,128)(2,1)} %fusion.13.refs_1_, f32[2048,512]{1,0:T(8,128)} %test.5, f32[256,2048]{1,0:T(8,128)} %refs_3_.1, ...), custom_call_target="tpu_custom_call" | custom-call | flops 19327352832 | bytes 16777216 | tf_op jit(solution)/shard_map/weights/pallas_call | solution.py:113
  115.2 31.7 %all-gather.5.cloned.1.call-done = f32[28672,128]{1,0:T(8,128)} async-done(((f32[3584,128]{1,0:T(8,128)}), f32[28672,128]{1,0:T(8,128)}) %all-gather.5.cloned.1.call-update) | async-done | bytes 14680080 | tf_op jit(solution)/shard_map/all_gather | solution.py:403
  146.9 26.1 %terms.2 = (f32[4096,512]{1,0:T(8,128)}, f32[4096,128]{1,0:T(8,128)}) custom-call(s32[5]{0:T(128)} %stack.67.place, f32[8,3584,128]{2,1,0:T(8,128)} %bitcast.83, f32[4096,512]{1,0:T(8,128)} %samples.1.partial, bf16[1024,512]{1,0:T(8,128)(2,1)} %get-tuple-element.51.product_high, ...), custom_call_target="tpu_custom_call", output_to_operand_aliasing={{0}: (2, {})} | custom-call | flops 11274289152 | bytes 29360128 | tf_op jit(solution)/shard_map/terms/pallas_call | solution.py:172
  173.0 3.4 %all-gather.7.cloned.1.call-done = f32[4096,128]{1,0:T(8,128)} async-done(((f32[512,128]{1,0:T(8,128)}), f32[4096,128]{1,0:T(8,128)}) %all-gather.7.cloned.1.call-update) | async-done | bytes 2097168 | tf_op jit(solution)/shard_map/all_gather | solution.py:407
  176.4 6.1 %terms.3 = (f32[4096,512]{1,0:T(8,128)}, f32[4096,128]{1,0:T(8,128)}) custom-call(s32[5]{0:T(128)} %copy-done.4, f32[8,512,128]{2,1,0:T(8,128)} %bitcast.68, f32[4096,512]{1,0:T(8,128)} %get-tuple-element.54.partial, bf16[1024,512]{1,0:T(8,128)(2,1)} %get-tuple-element.51.product_high, ...), custom_call_target="tpu_custom_call", output_to_operand_aliasing={{0}: (2, {}), {1}: (8, {})} | custom-call | flops 1610612736 | bytes 4194304 | tf_op jit(solution)/shard_map/terms/pallas_call | solution.py:172
  182.6 4.8 %leaves.1 = f32[2048,128]{1,0:T(8,128)} custom-call(s32[5]{0:T(128)} %stack.67.place, f32[4096,2048]{1,0:T(8,128)} %front.5, f32[4096,128]{1,0:T(8,128)} %get-tuple-element.57.blocks), custom_call_target="tpu_custom_call" | custom-call | flops 262144 | bytes 4194304 | tf_op jit(solution)/shard_map/leaves/pallas_call | solution.py:204
  188.6 3.4 %collective-permute-start.4 = (f32[2,256,128]{2,1,0:T(8,128)S(1)}, f32[2,256,128]{2,1,0:T(8,128)S(1)}, u32[]{:S(2)}, u32[]{:S(2)}) collective-permute-start(f32[2,256,128]{2,1,0:T(8,128)S(1)} %get-tuple-element.64), channel_id=1, source_target_pairs={{0,8},{1,9},{10,18},{11,19},{20,28},{21,29},{30,6},{31,7}} | collective-permute-start | bytes 786440 | tf_op jit(solution)/shard_map/ppermute | solution.py:345
  195.0 3.7 %collective-permute-done.4 = f32[2,256,128]{2,1,0:T(8,128)S(1)} collective-permute-done((f32[2,256,128]{2,1,0:T(8,128)S(1)}, f32[2,256,128]{2,1,0:T(8,128)S(1)}, u32[]{:S(2)}, u32[]{:S(2)}) %collective-permute-start.4) | collective-permute-done | bytes 262176 | tf_op jit(solution)/shard_map/ppermute | solution.py:345
  198.6 5.3 %collective-permute-done.6 = f32[2,256,128]{2,1,0:T(8,128)S(1)} collective-permute-done((f32[2,256,128]{2,1,0:T(8,128)S(1)}, f32[2,256,128]{2,1,0:T(8,128)S(1)}, u32[]{:S(2)}, u32[]{:S(2)}) %collective-permute-start.6) | collective-permute-done | bytes 262176 | tf_op jit(solution)/shard_map/ppermute | solution.py:345
  205.0 3.4 %collective-permute-start.8 = (f32[256,128]{1,0:T(8,128)S(1)}, f32[256,128]{1,0:T(8,128)S(1)}, u32[]{:S(2)}, u32[]{:S(2)}) collective-permute-start(f32[256,128]{1,0:T(8,128)S(1)} %get-tuple-element.74), channel_id=1, source_target_pairs={{0,2},{1,6},{2,0},{3,4},{4,3},{5,7},{6,1},{7,5},{8,10},{9,14},{10,... | collective-permute-start | bytes 393224 | tf_op jit(solution)/shard_map/ppermute | solution.py:358
  209.0 61.5 %update.1 = f32[4096,2048]{1,0:T(8,128)} custom-call(f32[8,3584,128]{2,1,0:T(8,128)} %bitcast.84, f32[8,512,128]{2,1,0:T(8,128)} %bitcast.69, bf16[1024,2048]{1,0:T(8,128)(2,1)} %get-tuple-element.58.high, bf16[1024,2048]{1,0:T(8,128)(2,1)} %get-tuple-element.53.low, f32[4096,2048]{1,0:T(8,128)} %front.5), custom_call_target="tpu_custom_call" | custom-call | flops 51539607552 | bytes 75497472 | tf_op jit(solution)/shard_map/update/pallas_call | solution.py:237
  271.5 5.3 %collective-permute-done.10 = f32[256,128]{1,0:T(8,128)S(1)} collective-permute-done((f32[256,128]{1,0:T(8,128)S(1)}, f32[256,128]{1,0:T(8,128)S(1)}, u32[]{:S(2)}, u32[]{:S(2)}) %collective-permute-start.10) | collective-permute-done | bytes 131104 | tf_op jit(solution)/shard_map/ppermute | solution.py:376
  277.9 2.9 gram.1
  286.5 3.5 %collective-permute-start.14 = (f32[160,128]{1,0:T(8,128)S(1)}, f32[160,128]{1,0:T(8,128)S(1)}, u32[]{:S(2)}, u32[]{:S(2)}) collective-permute-start(f32[160,128]{1,0:T(8,128)S(1)} %get-tuple-element.68), channel_id=1, source_target_pairs={{0,6},{2,0},{4,2},{6,4},{1,7},{3,1},{5,3},{7,5},{8,14},{10,8},{12,... | collective-permute-start | bytes 245768 | tf_op jit(solution)/shard_map/ppermute | solution.py:38
  290.1 3.0 collective-permute-done.12
  293.2 3.9 %collective-permute-done.13 = f32[160,128]{1,0:T(8,128)S(1)} collective-permute-done((f32[160,128]{1,0:T(8,128)S(1)}, f32[160,128]{1,0:T(8,128)S(1)}, u32[]{:S(2)}, u32[]{:S(2)}) %collective-permute-start.13) | collective-permute-done | bytes 81952 | tf_op jit(solution)/shard_map/ppermute | solution.py:38
  306.7 3.9 %collective-permute-done.17 = f32[160,128]{1,0:T(8,128)S(1)} collective-permute-done((f32[160,128]{1,0:T(8,128)S(1)}, f32[160,128]{1,0:T(8,128)S(1)}, u32[]{:S(2)}, u32[]{:S(2)}) %collective-permute-start.17) | collective-permute-done | bytes 81952 | tf_op jit(solution)/shard_map/ppermute | solution.py:38
  (76 shorter events, 40.0 us)
Async XLA Ops:
  7.2 139.7 %all-gather.5.cloned.1.call-start = ((), (), s32[]{:S(2)}) async-start(), calls=%async_computation.2 | async-start | bytes 16515072 | tf_op jit(solution)/shard_map/all_gather | solution.py:403
  10.1 166.3 %all-gather.7.cloned.1.call-start = ((), (), s32[]{:S(2)}) async-start(), calls=%async_computation.3 | async-start | bytes 2359296 | tf_op jit(solution)/shard_map/all_gather | solution.py:407
  10.2 48.8 %collective-permute-start = (f32[256,2048]{1,0:T(8,128)}, f32[256,2048]{1,0:T(8,128)S(1)}, u32[]{:S(2)}, u32[]{:S(2)}) collective-permute-start(f32[256,2048]{1,0:T(8,128)} %refs_3_.1), channel_id=1, source_target_pairs={{0,8},{8,0},{1,9},{9,1},{2,10},{10,2},{3,11},{11,3},{4,12},{12,4},... | collective-permute-start | bytes 6291464 | tf_op jit(solution)/shard_map/ppermute | solution.py:33
  13.2 47.4 %collective-permute-start.1 = (f32[256,2048]{1,0:T(8,128)}, f32[256,2048]{1,0:T(8,128)}, u32[]{:S(2)}, u32[]{:S(2)}) collective-permute-start(f32[256,2048]{1,0:T(8,128)} %refs_3_.1), channel_id=1, source_target_pairs={{0,16},{16,0},{1,17},{17,1},{2,18},{18,2},{3,19},{19,3},{4,20},{20... | collective-permute-start | bytes 6291464 | tf_op jit(solution)/shard_map/ppermute | solution.py:38
  51.3 13.9 %copy-start.5 = (s32[1024]{0:T(1024)S(1)}, s32[1024]{0:T(1024)}, u32[]{:S(2)}) copy-start(s32[1024]{0:T(1024)} %param.13) | copy-start | bytes 12292
  62.0 24.4 %collective-permute-start.3 = (f32[128,2048]{1,0:T(8,128)S(1)}, f32[128,2048]{1,0:T(8,128)}, u32[]{:S(2)}, u32[]{:S(2)}) collective-permute-start(f32[128,2048]{1,0:T(8,128)S(1)} %slice.35), channel_id=1, source_target_pairs={{0,8},{8,0},{1,9},{9,1},{2,10},{10,2},{3,11},{11,3},{4,12},{12,4},... | collective-permute-start | bytes 3145736 | tf_op jit(solution)/shard_map/ppermute | solution.py:33
  63.6 24.0 %collective-permute-start.2 = (f32[128,2048]{1,0:T(8,128)S(1)}, f32[128,2048]{1,0:T(8,128)}, u32[]{:S(2)}, u32[]{:S(2)}) collective-permute-start(f32[128,2048]{1,0:T(8,128)S(1)} %slice.34), channel_id=1, source_target_pairs={{0,16},{16,0},{1,17},{17,1},{2,18},{18,2},{3,19},{19,3},{4,20},{20... | collective-permute-start | bytes 3145736 | tf_op jit(solution)/shard_map/ppermute | solution.py:38
  65.1 212.8 %reduce-scatter.2.cloned.1.call-start = ((), (), s32[]{:S(2)}) async-start(), calls=%async_computation.1 | async-start | bytes 9437184 | tf_op jit(solution)/shard_map/reduce_scatter | solution.py:428
  188.6 10.1 %collective-permute-start.4 = (f32[2,256,128]{2,1,0:T(8,128)S(1)}, f32[2,256,128]{2,1,0:T(8,128)S(1)}, u32[]{:S(2)}, u32[]{:S(2)}) collective-permute-start(f32[2,256,128]{2,1,0:T(8,128)S(1)} %get-tuple-element.64), channel_id=1, source_target_pairs={{0,8},{1,9},{10,18},{11,19},{20,28},{21,29},{30,6},{31,7}} | collective-permute-start | bytes 786440 | tf_op jit(solution)/shard_map/ppermute | solution.py:345
  192.0 12.0 %collective-permute-start.6 = (f32[2,256,128]{2,1,0:T(8,128)S(1)}, f32[2,256,128]{2,1,0:T(8,128)S(1)}, u32[]{:S(2)}, u32[]{:S(2)}) collective-permute-start(f32[2,256,128]{2,1,0:T(8,128)S(1)} %get-tuple-element.65), channel_id=1, source_target_pairs={{0,24},{1,25},{10,2},{11,3},{20,12},{21,13},{30,22},{31,23}} | collective-permute-start | bytes 786440 | tf_op jit(solution)/shard_map/ppermute | solution.py:345
  193.6 10.4 %collective-permute-start.5 = (f32[2,256,128]{2,1,0:T(8,128)S(1)}, f32[2,256,128]{2,1,0:T(8,128)S(1)}, u32[]{:S(2)}, u32[]{:S(2)}) collective-permute-start(f32[2,256,128]{2,1,0:T(8,128)S(1)} %get-tuple-element.66), channel_id=1, source_target_pairs={{0,16},{1,17},{10,26},{11,27},{20,4},{21,5},{30,14},{31,15}} | collective-permute-start | bytes 786440 | tf_op jit(solution)/shard_map/ppermute | solution.py:345
  205.0 65.6 %collective-permute-start.8 = (f32[256,128]{1,0:T(8,128)S(1)}, f32[256,128]{1,0:T(8,128)S(1)}, u32[]{:S(2)}, u32[]{:S(2)}) collective-permute-start(f32[256,128]{1,0:T(8,128)S(1)} %get-tuple-element.74), channel_id=1, source_target_pairs={{0,2},{1,6},{2,0},{3,4},{4,3},{5,7},{6,1},{7,5},{8,10},{9,14},{10,... | collective-permute-start | bytes 393224 | tf_op jit(solution)/shard_map/ppermute | solution.py:358
  208.4 62.2 %collective-permute-start.7 = (f32[256,128]{1,0:T(8,128)S(1)}, f32[256,128]{1,0:T(8,128)S(1)}, u32[]{:S(2)}, u32[]{:S(2)}) collective-permute-start(f32[256,128]{1,0:T(8,128)S(1)} %get-tuple-element.75), channel_id=1, source_target_pairs={{0,0},{1,4},{2,2},{3,6},{4,1},{5,5},{6,3},{7,7},{8,8},{9,12},{10,1... | collective-permute-start | bytes 393224 | tf_op jit(solution)/shard_map/ppermute | solution.py:358
  270.7 6.0 %collective-permute-start.10 = (f32[256,128]{1,0:T(8,128)S(1)}, f32[256,128]{1,0:T(8,128)S(1)}, u32[]{:S(2)}, u32[]{:S(2)}) collective-permute-start(f32[256,128]{1,0:T(8,128)S(1)} %get-tuple-element.72), channel_id=1, source_target_pairs={{0,8},{1,24},{2,10},{3,26},{4,12},{5,28},{6,14},{7,30},{8,0},{9,16... | collective-permute-start | bytes 393224 | tf_op jit(solution)/shard_map/ppermute | solution.py:376
  270.8 6.0 %collective-permute-start.9 = (f32[256,128]{1,0:T(8,128)S(1)}, f32[256,128]{1,0:T(8,128)S(1)}, u32[]{:S(2)}, u32[]{:S(2)}) collective-permute-start(f32[256,128]{1,0:T(8,128)S(1)} %get-tuple-element.73), channel_id=1, source_target_pairs={{0,0},{1,16},{2,2},{3,18},{4,4},{5,20},{6,6},{7,22},{8,8},{9,24},{... | collective-permute-start | bytes 393224 | tf_op jit(solution)/shard_map/ppermute | solution.py:376
  280.8 4.2 %collective-permute-start.11 = (f32[640,128]{1,0:T(8,128)}, f32[640,128]{1,0:T(8,128)S(1)}, u32[]{:S(2)}, u32[]{:S(2)}) collective-permute-start(f32[640,128]{1,0:T(8,128)} %get-tuple-element.63), channel_id=1, source_target_pairs={{0,1},{1,0},{2,3},{3,2},{4,5},{5,4},{6,7},{7,6},{8,9},{9,8},{10,11... | collective-permute-start | bytes 983048 | tf_op jit(solution)/shard_map/ppermute | solution.py:33
  286.1 7.1 %collective-permute-start.12 = (f32[160,128]{1,0:T(8,128)S(1)}, f32[160,128]{1,0:T(8,128)S(1)}, u32[]{:S(2)}, u32[]{:S(2)}) collective-permute-start(f32[160,128]{1,0:T(8,128)S(1)} %get-tuple-element.67), channel_id=1, source_target_pairs={{0,2},{2,4},{4,6},{6,0},{1,3},{3,5},{5,7},{7,1},{8,10},{10,12},{12... | collective-permute-start | bytes 245768 | tf_op jit(solution)/shard_map/ppermute | solution.py:38
  286.5 6.7 %collective-permute-start.14 = (f32[160,128]{1,0:T(8,128)S(1)}, f32[160,128]{1,0:T(8,128)S(1)}, u32[]{:S(2)}, u32[]{:S(2)}) collective-permute-start(f32[160,128]{1,0:T(8,128)S(1)} %get-tuple-element.68), channel_id=1, source_target_pairs={{0,6},{2,0},{4,2},{6,4},{1,7},{3,1},{5,3},{7,5},{8,14},{10,8},{12,... | collective-permute-start | bytes 245768 | tf_op jit(solution)/shard_map/ppermute | solution.py:38
  290.0 7.1 %collective-permute-start.13 = (f32[160,128]{1,0:T(8,128)S(1)}, f32[160,128]{1,0:T(8,128)S(1)}, u32[]{:S(2)}, u32[]{:S(2)}) collective-permute-start(f32[160,128]{1,0:T(8,128)S(1)} %get-tuple-element.69), channel_id=1, source_target_pairs={{0,4},{2,6},{4,0},{6,2},{1,5},{3,7},{5,1},{7,3},{8,12},{10,14},{12... | collective-permute-start | bytes 245768 | tf_op jit(solution)/shard_map/ppermute | solution.py:38
  297.1 4.6 %collective-permute-start.15 = (f32[160,128]{1,0:T(8,128)S(1)}, f32[160,128]{1,0:T(8,128)S(1)}, u32[]{:S(2)}, u32[]{:S(2)}) collective-permute-start(f32[160,128]{1,0:T(8,128)S(1)} %fusion.29), channel_id=1, source_target_pairs={{0,8},{8,0},{1,9},{9,1},{2,10},{10,2},{3,11},{11,3},{4,12},{12,4},... | collective-permute-start | bytes 245768 | tf_op jit(solution)/shard_map/ppermute | solution.py:33
  301.7 5.0 %collective-permute-start.18 = (f32[160,128]{1,0:T(8,128)S(1)}, f32[160,128]{1,0:T(8,128)S(1)}, u32[]{:S(2)}, u32[]{:S(2)}) collective-permute-start(f32[160,128]{1,0:T(8,128)S(1)} %add.261), channel_id=1, source_target_pairs={{0,6},{2,0},{4,2},{6,4},{1,7},{3,1},{5,3},{7,5},{8,14},{10,8},{12,... | collective-permute-start | bytes 245768 | tf_op jit(solution)/shard_map/ppermute | solution.py:38
  303.4 7.1 %collective-permute-start.17 = (f32[160,128]{1,0:T(8,128)S(1)}, f32[160,128]{1,0:T(8,128)S(1)}, u32[]{:S(2)}, u32[]{:S(2)}) collective-permute-start(f32[160,128]{1,0:T(8,128)S(1)} %add.261), channel_id=1, source_target_pairs={{0,4},{2,6},{4,0},{6,2},{1,5},{3,7},{5,1},{7,3},{8,12},{10,14},{12... | collective-permute-start | bytes 245768 | tf_op jit(solution)/shard_map/ppermute | solution.py:38
  303.4 7.1 %collective-permute-start.16 = (f32[160,128]{1,0:T(8,128)S(1)}, f32[160,128]{1,0:T(8,128)S(1)}, u32[]{:S(2)}, u32[]{:S(2)}) collective-permute-start(f32[160,128]{1,0:T(8,128)S(1)} %add.261), channel_id=1, source_target_pairs={{0,2},{2,4},{4,6},{6,0},{1,3},{3,5},{5,7},{7,1},{8,10},{10,12},{12... | collective-permute-start | bytes 245768 | tf_op jit(solution)/shard_map/ppermute | solution.py:38
  311.3 1.7 collective-permute-start.19
  (5 other events, 16.0 us)
Sparse Core Ops, SparseCore 0:
  10.3 136.6 all-gather.4
  149.1 27.3 all-gather.6
  182.7 95.1 reduce-scatter.1
